TPU v7x, 128 devices: a whole 4x4x4 slice. The times are simulated.
128 devices in a mesh: batch: 8 (over y_hi, x), blk: 16 (over y_lo, z, core).
Axes of the slice: x: 4, y: 4 (y_hi: 2, y_lo: 2; y = y_hi * 2 + y_lo), z: 4, core: 2. Of those that a mesh axis runs over, the one named last changes fastest.
Arguments:
- tokens: bfloat16 [8, 2048, 2048], P('batch', 'blk'), may hold values from -6 to 6
- cotangent: bfloat16 [8, 2048, 2048], P('batch', 'blk'), may hold values from -6 to 6
- block_places: int32 [8, 16], P('batch'), may hold values from 0 to 15, each once within a row
- valid_counts: int32 [8, 16], P('batch'), may hold values from 96 to 128, as said below
- attn_gain: bfloat16 [2048], replicated, may hold values from 0.5 to 1.5
- mlp_gain: bfloat16 [2048], replicated, may hold values from 0.5 to 1.5
- query_weight: bfloat16 [2048, 2048], P('blk'), may hold values from -0.1875 to 0.1875
- key_weight: bfloat16 [2048, 256], P('blk'), may hold values from -0.1875 to 0.1875
- value_weight: bfloat16 [2048, 256], P('blk'), may hold values from -0.125 to 0.125
- output_weight: bfloat16 [2048, 2048], P('blk'), may hold values from -0.1875 to 0.1875
- gate_weight: bfloat16 [2048, 5632], P('blk'), may hold values from -0.125 to 0.125
- up_weight: bfloat16 [2048, 5632], P('blk'), may hold values from -0.125 to 0.125
- down_weight: bfloat16 [5632, 2048], P(None, 'blk'), may hold values from -0.078125 to 0.078125
Outputs:
- layer_out: bfloat16 [8, 2048, 2048], P('batch', 'blk')
- tokens_grad: bfloat16 [8, 2048, 2048], P('batch', 'blk')
- attn_gain_grad: float32 [2048], replicated
- mlp_gain_grad: float32 [2048], replicated
- query_grad: float32 [2048, 2048], P('blk')
- key_grad: float32 [2048, 256], P('blk')
- value_grad: float32 [2048, 256], P('blk')
- output_grad: float32 [2048, 2048], P('blk')
- gate_grad: float32 [2048, 5632], P('blk')
- up_grad: float32 [2048, 5632], P('blk')
- down_grad: float32 [5632, 2048], P(None, 'blk')
Inputs may be any that keep to these rules, and one draw needn't show every extreme that they name: `valid_counts`: tokens in use come first in each block; the rest are padding. In every sequence one block is full and one holds 96 tokens. Each row is a permutation: the blocks of a sequence stand in the array in this order, block b holding positions block_places * 128 onward.
All inputs are finite; a program needn't handle non-finite values.
Results may differ from a plain program's by a relative error of at most 0.029.
Values may be sent and summed in bfloat16 or wider, within the bound.
No kernel may reach another device: no remote copies, remote signals or barrier semaphores. Data moves between devices by JAX's collectives and lax.ppermute only.
A program may use at most 320 MiB of HBM per device.

v0:
```python
import math

import jax
import jax.numpy as jnp
from jax import lax
from jax.sharding import PartitionSpec as P

HEADS = 32
KV_HEADS = 4
HEAD = 64


epsilon = 1e-05


def rms_scale(rows):
    return lax.rsqrt(jnp.mean(rows * rows, axis=-1, keepdims=True) + epsilon)


def norm_back(rows, scale, gain, upstream):
    weighted = gain * upstream
    return scale * weighted - rows * scale**3 * jnp.mean(weighted * rows, axis=-1, keepdims=True)


def lookup(entries, holder):
    matches = holder[:, None] == jnp.arange(entries.shape[0], dtype=jnp.int32)[None, :]
    return jnp.sum(jnp.where(matches, entries[None, :], 0), axis=1)


def key_mask(offset, length, places, counts, tok_dev, query_pos):
    key_rows = offset + jnp.arange(length, dtype=jnp.int32)
    holder = key_rows // tok_dev
    inside = key_rows - holder * tok_dev
    key_pos = lookup(places, holder) * tok_dev + inside
    usable = inside < lookup(counts, holder)
    return usable[None, :] & (key_pos[None, :] <= query_pos[:, None])


def contract_last(left_side, right_side):
    return lax.dot_general(
        left_side, right_side, (((1,), (1,)), ((), ())), preferred_element_type=jnp.float32
    )


def contract_first(left_side, right_side):
    return lax.dot_general(
        left_side, right_side, (((0,), (0,)), ((), ())), preferred_element_type=jnp.float32
    )


def over_blocks(advance, running, pieces):
    length = pieces[0].shape[0]
    block_rows = math.gcd(length, 512)
    stacked = tuple(
        (member.reshape((length // block_rows, block_rows) + member.shape[1:]) for member in pieces)
    )

    def scan_body(state, element):
        block_index, members = element
        return (advance(state, members, block_index * block_rows), None)

    running, unused = lax.scan(
        scan_body, running, (jnp.arange(length // block_rows, dtype=jnp.int32), stacked)
    )
    return running


def on_device(
    tokens,
    cotangent,
    block_places,
    valid_counts,
    attn_gain,
    mlp_gain,
    query_weight,
    key_weight,
    value_weight,
    output_weight,
    gate_weight,
    up_weight,
    down_weight,
):
    tok_dev = tokens.shape[1]
    blocks = lax.axis_size("blk")
    seq_len = tok_dev * blocks
    offset_bias = -math.log(seq_len)
    score_scale = HEAD ** (-0.5)
    groups = HEADS // KV_HEADS
    key_width = KV_HEADS * HEAD
    own_block = lax.axis_index("blk")
    places = block_places[0]
    counts = valid_counts[0]
    own_place = lax.dynamic_index_in_dim(places, own_block, keepdims=False)
    query_pos = own_place * tok_dev + jnp.arange(tok_dev, dtype=jnp.int32)
    gain_one = attn_gain.astype(jnp.float32)
    gain_two = mlp_gain.astype(jnp.float32)
    rows_in = tokens[0].astype(jnp.float32)
    scale_attn = rms_scale(rows_in)
    normed_attn = (rows_in * scale_attn * gain_one).astype(jnp.bfloat16)
    full_query, full_key, full_value, full_out = (
        lax.all_gather(query_weight, "blk", axis=0, tiled=True),
        lax.all_gather(key_weight, "blk", axis=0, tiled=True),
        lax.all_gather(value_weight, "blk", axis=0, tiled=True),
        lax.all_gather(output_weight, "blk", axis=0, tiled=True),
    )
    queries = jnp.dot(normed_attn, full_query, preferred_element_type=jnp.float32).astype(
        jnp.bfloat16
    )
    keys_local = jnp.dot(normed_attn, full_key, preferred_element_type=jnp.float32).astype(
        jnp.bfloat16
    )
    values_local = jnp.dot(normed_attn, full_value, preferred_element_type=jnp.float32).astype(
        jnp.bfloat16
    )
    grouped = queries.reshape(tok_dev, KV_HEADS, groups, HEAD)

    def block_scores(key_block):
        return (
            score_scale
            * jnp.einsum("qgjd,kgd->qgjk", grouped, key_block, preferred_element_type=jnp.float32)
            + offset_bias
        )

    def forward_block(running, members, offset):
        key_block = members[0].reshape(-1, KV_HEADS, HEAD)
        value_block = members[1].reshape(-1, KV_HEADS, HEAD)
        allowed = key_mask(offset, key_block.shape[0], places, counts, tok_dev, query_pos)
        weights = jnp.where(
            allowed[:, None, None, :], jax.nn.sigmoid(block_scores(key_block)), 0.0
        ).astype(jnp.bfloat16)
        return running + jnp.einsum(
            "qgjk,kgd->qgjd", weights, value_block, preferred_element_type=jnp.float32
        )

    attended = over_blocks(
        forward_block,
        jnp.zeros(grouped.shape, jnp.float32),
        (
            lax.all_gather(keys_local, "blk", axis=0, tiled=True),
            lax.all_gather(values_local, "blk", axis=0, tiled=True),
        ),
    )
    attn_rows = attended.reshape(tok_dev, HEADS * HEAD).astype(jnp.bfloat16)
    residual = rows_in + jnp.dot(attn_rows, full_out, preferred_element_type=jnp.float32)
    scale_mlp = rms_scale(residual)
    normed_mlp = (residual * scale_mlp * gain_two).astype(jnp.bfloat16)
    pieces = (
        lax.all_gather(gate_weight, "blk", axis=0, tiled=True),
        lax.all_gather(up_weight, "blk", axis=0, tiled=True),
    )
    columns = normed_mlp
    gate = jnp.dot(columns, pieces[0], preferred_element_type=jnp.float32)
    up_rows = jnp.dot(columns, pieces[1], preferred_element_type=jnp.float32)
    sig_gate = jax.nn.sigmoid(gate)
    silu_gate = gate * sig_gate
    hidden = (silu_gate * up_rows).astype(jnp.bfloat16)
    branch = jnp.dot(
        hidden,
        lax.all_gather(down_weight, "blk", axis=1, tiled=True),
        preferred_element_type=jnp.float32,
    )
    layer_out = (residual + branch).astype(jnp.bfloat16)[None]
    grad_rows = cotangent[0]
    columns = grad_rows
    hidden_grad = contract_last(columns, lax.all_gather(down_weight, "blk", axis=1, tiled=True))
    gate_grad_rows = (hidden_grad * up_rows * sig_gate * (1.0 + gate * (1.0 - sig_gate))).astype(
        jnp.bfloat16
    )
    up_grad_rows = (hidden_grad * silu_gate).astype(jnp.bfloat16)
    pieces = lax.all_gather((gate_weight, up_weight), "blk", axis=0, tiled=True)
    normed_grad = contract_last(gate_grad_rows, pieces[0]) + contract_last(up_grad_rows, pieces[1])
    residual_grad = grad_rows.astype(jnp.float32) + norm_back(
        residual, scale_mlp, gain_two, normed_grad
    )
    mlp_gain_part = jnp.sum(normed_grad * residual * scale_mlp, axis=0)
    branch_grad = residual_grad.astype(jnp.bfloat16)
    attn_grad = contract_last(branch_grad, full_out).astype(jnp.bfloat16)
    grouped_grad = attn_grad.reshape(tok_dev, KV_HEADS, groups, HEAD)

    def backward_block(running, members, offset):
        query_sum, key_terms, value_terms = running
        key_block = members[0].reshape(-1, KV_HEADS, HEAD)
        value_block = members[1].reshape(-1, KV_HEADS, HEAD)
        length = key_block.shape[0]
        allowed = key_mask(offset, length, places, counts, tok_dev, query_pos)[:, None, None, :]
        sig_scores = jax.nn.sigmoid(block_scores(key_block))
        weights = jnp.where(allowed, sig_scores, 0.0).astype(jnp.bfloat16)
        prob_grad = jnp.einsum(
            "qgjd,kgd->qgjk", grouped_grad, value_block, preferred_element_type=jnp.float32
        )
        score_grad = jnp.where(allowed, prob_grad * sig_scores * (1.0 - sig_scores), 0.0).astype(
            jnp.bfloat16
        )
        query_sum = query_sum + score_scale * jnp.einsum(
            "qgjk,kgd->qgjd", score_grad, key_block, preferred_element_type=jnp.float32
        )
        key_part = score_scale * jnp.einsum(
            "qgjk,qgjd->kgd", score_grad, grouped, preferred_element_type=jnp.float32
        )
        value_part = jnp.einsum(
            "qgjk,qgjd->kgd", weights, grouped_grad, preferred_element_type=jnp.float32
        )
        key_terms = lax.dynamic_update_slice_in_dim(
            key_terms, key_part.reshape(length, key_width), offset, 0
        )
        value_terms = lax.dynamic_update_slice_in_dim(
            value_terms, value_part.reshape(length, key_width), offset, 0
        )
        return (query_sum, key_terms, value_terms)

    zeros_keys = jnp.zeros((seq_len, key_width), jnp.float32)
    start_state = (jnp.zeros(grouped.shape, jnp.float32), zeros_keys, zeros_keys)
    query_sum, key_terms, value_terms = over_blocks(
        backward_block,
        start_state,
        (
            lax.all_gather(keys_local, "blk", axis=0, tiled=True),
            lax.all_gather(values_local, "blk", axis=0, tiled=True),
        ),
    )
    key_sums, value_sums = (
        lax.psum_scatter(
            key_terms.astype(jnp.bfloat16), "blk", scatter_dimension=0, tiled=True
        ).astype(jnp.float32),
        lax.psum_scatter(
            value_terms.astype(jnp.bfloat16), "blk", scatter_dimension=0, tiled=True
        ).astype(jnp.float32),
    )
    query_grad_rows = query_sum.reshape(tok_dev, HEADS * HEAD).astype(jnp.bfloat16)
    key_grad_rows = key_sums.astype(jnp.bfloat16)
    value_grad_rows = value_sums.astype(jnp.bfloat16)
    normed_attn_grad = (
        contract_last(query_grad_rows, full_query)
        + contract_last(key_grad_rows, full_key)
        + contract_last(value_grad_rows, full_value)
    )
    tokens_grad = (
        residual_grad + norm_back(rows_in, scale_attn, gain_one, normed_attn_grad)
    ).astype(jnp.bfloat16)[None]
    attn_gain_part = jnp.sum(normed_attn_grad * rows_in * scale_attn, axis=0)
    attn_gain_grad, mlp_gain_grad = lax.psum((attn_gain_part, mlp_gain_part), ("batch", "blk"))
    lefts = (normed_attn, normed_attn, normed_attn, attn_rows, normed_mlp, normed_mlp, grad_rows)
    rights = (
        query_grad_rows,
        key_grad_rows,
        value_grad_rows,
        branch_grad,
        gate_grad_rows,
        up_grad_rows,
        hidden,
    )
    blocks_out = []
    for factor, partner in zip(lefts, rights):
        columns = factor
        blocks_out.append(contract_first(columns, partner))
    summed = lax.psum_scatter(
        jnp.concatenate(blocks_out, axis=1).astype(jnp.bfloat16),
        "blk",
        scatter_dimension=0,
        tiled=True,
    ).astype(jnp.float32)
    summed = lax.psum(summed.astype(jnp.bfloat16), "batch").astype(jnp.float32)
    model_width = HEADS * HEAD
    wide = gate_weight.shape[1]
    edges = [
        0,
        model_width,
        model_width + key_width,
        model_width + 2 * key_width,
        2 * model_width + 2 * key_width,
    ]
    edges = edges + [edges[4] + wide, edges[4] + 2 * wide, edges[4] + 3 * wide]
    query_grad = summed[:, edges[0] : edges[1]]
    key_grad = summed[:, edges[1] : edges[2]]
    value_grad = summed[:, edges[2] : edges[3]]
    output_grad = summed[:, edges[3] : edges[4]]
    gate_grad = summed[:, edges[4] : edges[5]]
    up_grad = summed[:, edges[5] : edges[6]]
    down_grad = summed[:, edges[6] : edges[7]].T
    return (
        layer_out,
        tokens_grad,
        attn_gain_grad,
        mlp_gain_grad,
        query_grad,
        key_grad,
        value_grad,
        output_grad,
        gate_grad,
        up_grad,
        down_grad,
    )


def solution(mesh):
    in_specs = (
        P("batch", "blk", None),
        P("batch", "blk", None),
        P("batch", None),
        P("batch", None),
        P(),
        P(),
        P("blk", None),
        P("blk", None),
        P("blk", None),
        P("blk", None),
        P("blk", None),
        P("blk", None),
        P(None, "blk"),
    )
    out_specs = (
        P("batch", "blk", None),
        P("batch", "blk", None),
        P(),
        P(),
        P("blk", None),
        P("blk", None),
        P("blk", None),
        P("blk", None),
        P("blk", None),
        P("blk", None),
        P(None, "blk"),
    )
    return jax.shard_map(
        on_device, mesh=mesh, in_specs=in_specs, out_specs=out_specs, check_vma=False
    )
```

profile of v0, /device:TPU:24, one launch (start us, length us, event | category | flops | bytes accessed | tf_op | source)
XLA Modules:
  0.0 1595.8 jit_solution(15894172637702760403)
XLA Ops:
  11.3 33.0 %all-gather.10.cloned.1.call-done = bf16[2048,256]{1,0:T(8,128)(2,1)} async-done(((bf16[128,256]{1,0:T(8,128)(2,1)}), bf16[2048,256]{1,0:T(8,128)(2,1)}) %all-gather.10.cloned.1.call-update) | async-done | bytes 1048592 | tf_op jit(solution)/shard_map/all_gather | solution.py:103
  46.7 31.8 %all-gather.14.cloned.1.call-done = bf16[2048,256]{1,0:T(8,128)(2,1)} async-done(((bf16[128,256]{1,0:T(8,128)(2,1)}), bf16[2048,256]{1,0:T(8,128)(2,1)}) %all-gather.14.cloned.1.call-update) | async-done | bytes 1048592 | tf_op jit(solution)/shard_map/all_gather | solution.py:102
  85.1 28.3 %all-gather.12.cloned.1.call-done = bf16[2048,256]{1,0:T(8,128)(2,1)} async-done(((bf16[128,256]{1,0:T(8,128)(2,1)}), bf16[2048,256]{1,0:T(8,128)(2,1)}) %all-gather.12.cloned.1.call-update) | async-done | bytes 1048592 | tf_op jit(solution)/shard_map/all_gather | solution.py:140
  114.9 33.2 %all-gather.16.cloned.1.call-done = bf16[2048,256]{1,0:T(8,128)(2,1)} async-done(((bf16[128,256]{1,0:T(8,128)(2,1)}), bf16[2048,256]{1,0:T(8,128)(2,1)}) %all-gather.16.cloned.1.call-update) | async-done | bytes 1048592 | tf_op jit(solution)/shard_map/all_gather | solution.py:139
  150.3 51.5 %all-gather.18.cloned.1.call-done = bf16[2048,2048]{1,0:T(8,128)(2,1)} async-done(((bf16[128,2048]{1,0:T(8,128)(2,1)}), bf16[2048,2048]{1,0:T(8,128)(2,1)}) %all-gather.18.cloned.1.call-update) | async-done | bytes 8388624 | tf_op jit(solution)/shard_map/all_gather | solution.py:101
  201.8 5.5 convolution_convert_fusion.5
  208.7 37.4 %while.30 = (s32[]{:T(128)}, f32[128,4,8,64]{0,3,2,1:T(8,128)}, bf16[4,512,256]{1,2,0:T(8,128)(2,1)S(1)}, s32[4]{0:T(128)S(1)}, s32[1,16]{1,0:T(1,128)S(1)}, /*i...) while((s32[]{:T(128)}, f32[128,4,8,64]{0,3,2,1:T(8,128)}, ...), condition=%wide.region_4.5_spmd.clone, body=%wide.region_1.4_spmd.clone.sunk | while | flops 552274560 | bytes 4344115 | solution.py:62
  212.6 5.0 fusion.152
  221.5 5.4 fusion.152
  230.8 5.4 fusion.152
  240.1 5.4 fusion.152
  248.7 7.8 all-gather.20.cloned.1.call-done
  256.6 4.9 multiply_reduce_fusion.2
  261.7 118.7 %all-gather.22.cloned.1.call-done = bf16[2048,5632]{1,0:T(8,128)(2,1)} async-done(((bf16[128,5632]{1,0:T(8,128)(2,1)}), bf16[2048,5632]{1,0:T(8,128)(2,1)}) %all-gather.22.cloned.1.call-update) | async-done | bytes 23068688 | tf_op jit(solution)/shard_map/all_gather | solution.py:148
  380.4 12.3 fusion.78
  392.7 111.7 %all-gather.24.cloned.1.call-done = bf16[2048,5632]{1,0:T(8,128)(2,1)} async-done(((bf16[128,5632]{1,0:T(8,128)(2,1)}), bf16[2048,5632]{1,0:T(8,128)(2,1)}) %all-gather.24.cloned.1.call-update) | async-done | bytes 23068688 | tf_op jit(solution)/shard_map/all_gather | solution.py:149
  504.4 12.3 fusion.79
  516.7 119.9 %all-gather.26.cloned.1.call-done = bf16[5632,2048]{1,0:T(8,128)(2,1)} async-done(((bf16[5632,128]{1,0:T(8,128)(2,1)}), bf16[5632,2048]{1,0:T(8,128)(2,1)}) %all-gather.26.cloned.1.call-update) | async-done | bytes 23068688 | tf_op jit(solution)/shard_map/all_gather | solution.py:159
  636.6 14.8 multiply_convert_fusion
  651.4 13.2 fusion.80
  664.6 13.0 multiply_reduce_fusion
  680.0 6.3 convolution_convert_fusion.4
  688.8 95.1 %while.31 = (s32[]{:T(128)}, f32[128,4,8,64]{0,3,2,1:T(8,128)S(1)}, bf16[2048,256]{0,1:T(8,128)(2,1)}, bf16[2048,256]{0,1:T(8,128)(2,1)}, bf16[4,512,256]{1,2,0:...) while((s32[]{:T(128)}, f32[128,4,8,64]{0,3,2,1:T(8,128)S(1)}, ...), condition=%wide.region_10.11_spmd.clone, body=%wide.region_7.10_spmd.clone.sunk | while | flops 1366493824 | bytes 79120792 | solution.py:62
  696.3 4.0 fusion.164
  703.5 4.8 fusion.166
  720.1 4.0 fusion.164
  727.2 4.8 fusion.166
  743.8 4.0 fusion.164
  751.0 4.8 fusion.166
  767.6 4.0 fusion.164
  774.7 4.8 fusion.166
  789.6 5.8 convolution_convert_fusion
  795.4 12.4 copy.81
  807.9 5.6 convolution_convert_fusion.1
  813.5 12.4 copy.84
  825.9 8.4 constant_dynamic-update-slice_fusion.5
  834.3 13.1 reduce-scatter.10.cloned.1.call-done
  850.2 60.5 %reduce-scatter.12.cloned.1.call-done = bf16[128,256]{1,0:T(8,128)(2,1)} async-done(((bf16[2048,256]{1,0:T(8,128)(2,1)}), bf16[128,256]{1,0:T(8,128)(2,1)}) %reduce-scatter.12.cloned.1.call-update) | async-done | bytes 65552
  918.1 8.5 constant_dynamic-update-slice_fusion.2
  926.6 11.0 convert_dynamic-update-slice_fusion.1
  937.6 11.8 convert_dynamic-update-slice_fusion
  949.4 10.9 bitcast_dynamic-update-slice_fusion
  960.6 455.1 %reduce-scatter.8.cloned.1.call-done = bf16[128,21504]{1,0:T(8,128)(2,1)} async-done(((bf16[2048,21504]{1,0:T(8,128)(2,1)}), bf16[128,21504]{1,0:T(8,128)(2,1)}) %reduce-scatter.8.cloned.1.call-update) | async-done | bytes 5505040 | tf_op jit(solution)/shard_map/reduce_scatter | solution.py:256
  1415.8 6.4 fusion.81
  1422.3 12.3 fusion.41
  1436.6 134.5 %all-reduce = (f32[2048]{0:T(1024)}, f32[2048]{0:T(1024)}) all-reduce(f32[2048]{0:T(1024)S(1)} %get-tuple-element.490, f32[2048]{0:T(1024)S(1)} %copy-done.30), channel_id=1, replica_groups=mesh['batch'=8,'blk'=16] {'batch','blk'}, use_global_device_ids=true, to_apply=%region_15.16 | all-reduce | flops 4096 | bytes 32768 | tf_op jit(solution)/shard_map/psum | solution.py:241
  1573.6 3.7 convert_element_type.132
  1584.1 5.0 fusion.74
  (226 shorter events, 122.8 us)
Async XLA Ops:
  7.2 194.7 %copy-start.1 = (bf16[1,128,2048]{2,1,0:T(8,128)(2,1)S(1)}, bf16[1,128,2048]{2,1,0:T(8,128)(2,1)}, u32[]{:S(2)}) copy-start(bf16[1,128,2048]{2,1,0:T(8,128)(2,1)} %param.17) | copy-start | bytes 1572868
  7.2 77.2 %copy-start.33 = (bf16[2048]{0:T(1024)(128)(2,1)S(1)}, bf16[2048]{0:T(1024)(128)(2,1)}, u32[]{:S(2)}) copy-start(bf16[2048]{0:T(1024)(128)(2,1)} %param.22) | copy-start | bytes 12292
  7.2 77.2 %copy-start.29 = (s32[1,16]{1,0:T(1,128)S(1)}, s32[1,16]{1,0:T(1,128)}, u32[]{:S(2)}) copy-start(s32[1,16]{1,0:T(1,128)} %param.19) | copy-start | bytes 196
  7.2 37.1 %all-gather.10.cloned.1.call-start = ((), (), s32[]{:S(2)}) async-start(), calls=%async_computation.3 | async-start | bytes 1114112 | tf_op jit(solution)/shard_map/all_gather | solution.py:103
  7.9 70.6 %all-gather.14.cloned.1.call-start = ((), (), s32[]{:S(2)}) async-start(), calls=%async_computation.5 | async-start | bytes 1114112 | tf_op jit(solution)/shard_map/all_gather | solution.py:102
  8.7 104.7 %all-gather.12.cloned.1.call-start = ((), (), s32[]{:S(2)}) async-start(), calls=%async_computation.4 | async-start | bytes 1114112 | tf_op jit(solution)/shard_map/all_gather | solution.py:140
  9.4 192.4 %copy-start.24 = (f32[2048]{0:T(1024)}, f32[2048]{0:T(1024)S(1)}, u32[]{:S(2)}) copy-start(f32[2048]{0:T(1024)S(1)} %convert_element_type.108) | copy-start | bytes 24580
  11.3 196.1 %copy-start.31 = (f32[128]{0:T(128)}, f32[128]{0:T(128)S(1)}, u32[]{:S(2)}) copy-start(f32[128]{0:T(128)S(1)} %get-tuple-element.550) | copy-start | bytes 1540
  46.7 101.4 %all-gather.16.cloned.1.call-start = ((), (), s32[]{:S(2)}) async-start(), calls=%async_computation.6 | async-start | bytes 1114112 | tf_op jit(solution)/shard_map/all_gather | solution.py:139
  80.9 120.9 %all-gather.18.cloned.1.call-start = ((), (), s32[]{:S(2)}) async-start(), calls=%async_computation.7 | async-start | bytes 8912896 | tf_op jit(solution)/shard_map/all_gather | solution.py:101
  81.5 175.0 %all-gather.20.cloned.1.call-start = ((), (), s32[]{:S(2)}) async-start(), calls=%async_computation.8 | async-start | bytes 8912896 | tf_op jit(solution)/shard_map/all_gather | solution.py:104
  82.1 298.3 %all-gather.22.cloned.1.call-start = ((), (), s32[]{:S(2)}) async-start(), calls=%async_computation.9 | async-start | bytes 24510464 | tf_op jit(solution)/shard_map/all_gather | solution.py:148
  82.9 421.6 %all-gather.24.cloned.1.call-start = ((), (), s32[]{:S(2)}) async-start(), calls=%async_computation.10 | async-start | bytes 24510464 | tf_op jit(solution)/shard_map/all_gather | solution.py:149
  83.6 553.0 %all-gather.26.cloned.1.call-start = ((), (), s32[]{:S(2)}) async-start(), calls=%async_computation.11 | async-start | bytes 24510464 | tf_op jit(solution)/shard_map/all_gather | solution.py:159
  84.3 763.1 %reduce-scatter.10.cloned.1.call-start = ((), (), s32[]{:S(2)}) async-start(), calls=%async_computation.14 | async-start | bytes 1114112
  150.3 58.3 %copy-start.28 = (s32[1,16]{1,0:T(1,128)S(1)}, s32[1,16]{1,0:T(1,128)}, u32[]{:S(2)}) copy-start(s32[1,16]{1,0:T(1,128)} %param.20) | copy-start | bytes 196
  246.0 10.5 copy-start.11
  246.0 15.5 copy-start.5
  261.5 416.1 %copy-start.3 = (f32[128,2048]{1,0:T(8,128)}, f32[128,2048]{1,0:T(8,128)S(1)}, u32[]{:S(2)}) copy-start(f32[128,2048]{1,0:T(8,128)S(1)} %get-tuple-element.554) | copy-start | bytes 3145732
  261.7 242.7 %copy-start.9 = (bf16[128,2048]{1,0:T(8,128)(2,1)}, bf16[128,2048]{1,0:T(8,128)(2,1)S(1)}, u32[]{:S(2)}) copy-start(bf16[128,2048]{1,0:T(8,128)(2,1)S(1)} %multiply_convert_fusion.3) | copy-start | bytes 1572868
  392.7 243.9 %copy-start.20 = (bf16[1,128,2048]{2,1,0:T(8,128)(2,1)S(1)}, bf16[1,128,2048]{2,1,0:T(8,128)(2,1)}, u32[]{:S(2)}) copy-start(bf16[1,128,2048]{2,1,0:T(8,128)(2,1)} %param.18) | copy-start | bytes 1572868
  651.4 13.2 copy-start.13
  680.0 8.8 copy-start.6
  688.8 100.8 %copy-start.2 = (bf16[1,128,2048]{2,1,0:T(8,128)(2,1)S(1)}, bf16[1,128,2048]{2,1,0:T(8,128)(2,1)}, u32[]{:S(2)}) copy-start(bf16[1,128,2048]{2,1,0:T(8,128)(2,1)} %param.17) | copy-start | bytes 1572868
  688.8 100.8 %copy-start.25 = (f32[2048]{0:T(1024)S(1)}, f32[2048]{0:T(1024)}, u32[]{:S(2)}) copy-start(f32[2048]{0:T(1024)} %copy-done.24) | copy-start | bytes 24580
  688.8 100.8 %copy-start.32 = (f32[128]{0:T(128)S(1)}, f32[128]{0:T(128)}, u32[]{:S(2)}) copy-start(f32[128]{0:T(128)} %copy-done.31) | copy-start | bytes 1540
  692.5 3.8 copy-start
  716.3 3.8 copy-start
  740.0 3.8 copy-start
  786.4 124.3 %reduce-scatter.12.cloned.1.call-start = ((), (), s32[]{:S(2)}) async-start(), calls=%async_computation.15 | async-start | bytes 1114112
  788.7 627.0 %reduce-scatter.8.cloned.1.call-start = ((), (), s32[]{:S(2)}) async-start(), calls=%async_computation.12 | async-start | bytes 93585408 | tf_op jit(solution)/shard_map/reduce_scatter | solution.py:256
  795.4 12.5 copy-start.8
  795.4 12.5 copy-start.15
  918.1 8.5 copy-start.10
  918.1 8.5 copy-start.12
  926.6 11.0 copy-start.14
  937.6 11.8 copy-start.16
  937.6 11.8 copy-start.21
  960.3 455.4 %copy-start.19 = (bf16[128,4,8,64]{0,3,2,1:T(8,128)(2,1)S(1)}, bf16[128,4,8,64]{0,3,2,1:T(8,128)(2,1)}, u32[]{:S(2)}) copy-start(bf16[128,4,8,64]{0,3,2,1:T(8,128)(2,1)} %copy-done.18) | copy-start | bytes 1572868
  960.3 461.8 %copy-start.4 = (f32[128,2048]{1,0:T(8,128)S(1)}, f32[128,2048]{1,0:T(8,128)}, u32[]{:S(2)}) copy-start(f32[128,2048]{1,0:T(8,128)} %copy-done.3) | copy-start | bytes 3145732
  960.4 613.2 %all-reduce.3.cloned.1.call-start = ((), (), s32[]{:S(2)}) async-start(), calls=%async_computation.13 | async-start | bytes 11010048 | tf_op jit(solution)/shard_map/psum | solution.py:262
  1415.8 6.4 copy-start.17
  1422.2 12.4 copy-start.22
  1422.2 12.4 copy-start.27
  1422.2 12.8 copy-start.23
  1422.2 12.8 copy-start.26
  1422.2 14.4 copy-start.30
  1422.3 148.8 %copy-start.34 = (f32[128]{0:T(128)S(1)}, f32[128]{0:T(128)}, u32[]{:S(2)}) copy-start(f32[128]{0:T(128)} %get-tuple-element.549) | copy-start | bytes 1540
  (3 other events, 5.6 us)
Sparse Core Ops, SparseCore 0:
  9.8 34.4 all-gather.9
  46.0 32.4 all-gather.13
  80.8 32.5 all-gather.11
  115.5 32.5 all-gather.15
  149.6 52.1 all-gather.17
  203.4 53.1 all-gather.19
  258.3 122.0 all-gather.21
  382.1 122.2 all-gather.23
  506.0 130.5 all-gather.25
  786.5 60.9 reduce-scatter.9
  850.6 60.0 reduce-scatter.11
  960.5 455.2 reduce-scatter.7
  1418.4 130.0 all-reduce.2
where the time goes:
time: 1610 us; the launch traced here: 1600 us
  waiting for transfers between devices  1070 us (66%)
  matrix products  249 us (15%)
  blocking collectives  134 us (8%)
  local copies, waits for them, and re-layouts  100 us (6%)
  other arithmetic  21.2 us (1%)
    reduce_scatter x1, waiting for transfers between devices, on_device(): lax.psum_scatter(jnp.concatenate(blocks_out, axis=1).astype(jnp.bfloat16)...  455 us
    psum x1, blocking collectives, on_device(): lax.psum((attn_gain_part, mlp_gain_part), ('batch', 'blk'))  134 us
    all_gather x1, waiting for transfers between devices, on_device(): lax.all_gather(down_weight, 'blk', axis=1, tiled=True)  120 us
    all_gather x1, waiting for transfers between devices, on_device(): lax.all_gather(gate_weight, 'blk', axis=0, tiled=True)  119 us
    all_gather x1, waiting for transfers between devices, on_device(): lax.all_gather(up_weight, 'blk', axis=0, tiled=True)  112 us
    unnamed x15, waiting for transfers between devices  78.3 us
    dot_general x7, matrix products, contract_last(): lax.dot_general(left_side, right_side, (((1,), (1,)), ((), ())), preferre...  55.7 us
    all_gather x1, waiting for transfers between devices, on_device(): lax.all_gather(query_weight, 'blk', axis=0, tiled=True)  51.5 us
  transfers between devices with their start and end apart: 13, of which 12 were waited for; matrix products, arithmetic and copies ran while one was open for 10% of the time, Pallas kernels for 0%

commit v1 on v0

v1 whole, which is shorter than its diff:
```python
import itertools

import jax
import jax.numpy as jnp
from jax import lax
from jax.experimental import pallas as pl
from jax.experimental.pallas import tpu as pltpu
from jax.sharding import PartitionSpec as P

HEADS = 32
KV_HEADS = 4
HEAD = 64
D = 2048
FF = 5632
TOK = 128
RING = 4
WIDE = FF // 8
QUERY = HEADS * HEAD // 8
epsilon = 1e-05
BOTH = ("batch", "blk")
BF = jnp.bfloat16
F32 = jnp.float32


def device_index(yh, x, yl, z, c):
    return (((yh * 4 + x) * 2 + yl) * 4 + z) * 2 + c


def send(value, target):
    pairs = []
    for spot in itertools.product(range(2), range(4), range(2), range(4), range(2)):
        pairs.append((device_index(*spot), device_index(*target(*spot))))
    return lax.ppermute(value, BOTH, pairs)


def step(value, axis, way):
    def target(yh, x, yl, z, c):
        by = way * (1 - 2 * c)
        if axis == "x":
            x = (x + by) % 4
        elif axis == "z":
            z = (z + by) % 4
        else:
            y = (2 * yh + yl + by) % 4
            yh, yl = y // 2, y % 2
        return yh, x, yl, z, c

    return send(value, target)


def across(value, axis):
    def target(yh, x, yl, z, c):
        if axis == "x":
            x = (x + 2) % 4
        elif axis == "z":
            z = (z + 2) % 4
        else:
            yh = 1 - yh
        return yh, x, yl, z, c

    return send(value, target)


def swap(value):
    return send(value, lambda yh, x, yl, z, c: (yh, x, yl, z, 1 - c))


def to_half(value):
    return send(value, lambda yh, x, yl, z, c: (yh, x, 1 - yl, z, c))


def ring_gather(value, axis):
    first = step(value, axis, 1)
    second = step(value, axis, -1)
    third = step(first, axis, 1)
    return value, first, second, third


def add(*terms):
    total = terms[0].astype(F32)
    for term in terms[1:]:
        total = total + term.astype(F32)
    return total


def ring_scatter(own, before, after, far, axis):
    got_far = step(far.astype(BF), axis, 1)
    got_after = step(before.astype(BF), axis, -1)
    got_before = step(add(after, got_far).astype(BF), axis, 1)
    return add(own, got_after, got_before)


def take(value, index, axis=0):
    return lax.dynamic_index_in_dim(value, index, axis, keepdims=False)


def put_all(parts, spots, axis, count):
    shape = parts[0].shape[:axis] + (count,) + parts[0].shape[axis:]
    out = jnp.zeros(shape, parts[0].dtype)
    for part, spot in zip(parts, spots):
        out = lax.dynamic_update_index_in_dim(out, part, spot, axis)
    return out


def rms_scale(rows):
    return lax.rsqrt(jnp.mean(rows * rows, axis=-1, keepdims=True) + epsilon)


def norm_back(rows, scale, gain, upstream):
    weighted = gain * upstream
    return scale * weighted - rows * scale**3 * jnp.mean(weighted * rows, axis=-1, keepdims=True)


def lookup(entries, holder):
    matches = holder[:, None] == jnp.arange(entries.shape[0], dtype=jnp.int32)[None, :]
    return jnp.sum(jnp.where(matches, entries[None, :], 0), axis=1)


def dot(left, right):
    return jnp.dot(left, right, preferred_element_type=F32)


def dot_last(left, right):
    return lax.dot_general(left, right, (((1,), (1,)), ((), ())), preferred_element_type=F32)


def dot_first(left, right):
    return lax.dot_general(left, right, (((0,), (0,)), ((), ())), preferred_element_type=F32)


LOG2E = 1.4426950408889634
SCORE = HEAD**-0.5
SHIFT = 11.0


def head_rows(rows):
    return jnp.concatenate([rows[:, HEAD * h : HEAD * (h + 1)] for h in range(4)], axis=0)


def head_columns(rows):
    return jnp.concatenate([rows[TOK * h : TOK * (h + 1)] for h in range(4)], axis=1)


def attend_kernel(query_place, key_slot, q_ref, k_ref, v_ref, o_ref, total):
    place = query_place[pl.program_id(0)]
    queries = head_rows(q_ref[...])

    def block(j, diagonal):
        at = pl.ds(pl.multiple_of(j * TOK, TOK), TOK)
        scores = dot_last(queries, k_ref[at, :])
        weights = 1.0 / (1.0 + jnp.exp2(SHIFT - scores * (SCORE * LOG2E)))
        if diagonal:
            row = lax.broadcasted_iota(jnp.int32, weights.shape, 0) & (TOK - 1)
            column = lax.broadcasted_iota(jnp.int32, weights.shape, 1)
            weights = jnp.where(column <= row, weights, 0.0)
        return dot(weights.astype(BF), v_ref[at, :])

    total[...] = block(key_slot[place], True)

    @pl.loop(0, place)
    def _(p):
        total[...] += block(key_slot[p], False)

    o_ref[...] = head_columns(total[...]).astype(BF)


def attend(query_place, key_slot, q, k, v):
    rows = q.shape[0]
    whole = lambda i, *_: (0, 0)
    return pl.pallas_call(
        attend_kernel,
        grid_spec=pltpu.PrefetchScalarGridSpec(
            num_scalar_prefetch=2,
            grid=(rows // TOK,),
            in_specs=[
                pl.BlockSpec((TOK, QUERY), lambda i, *_: (i, 0)),
                pl.BlockSpec(k.shape, whole),
                pl.BlockSpec(v.shape, whole),
            ],
            out_specs=pl.BlockSpec((TOK, QUERY), lambda i, *_: (i, 0)),
            scratch_shapes=[pltpu.VMEM((4 * TOK, HEAD), F32)],
        ),
        out_shape=jax.ShapeDtypeStruct(q.shape, BF),
        compiler_params=pltpu.CompilerParams(vmem_limit_bytes=16 * 1024 * 1024),
        cost_estimate=pl.CostEstimate(flops=2 * 2 * 2048 * 2048 * 256, bytes_accessed=2 * 1024 * 1024, transcendentals=0),
    )(query_place, key_slot, q, k, v)


def attend_back_kernel(query_place, key_slot, q_ref, g_ref, k_ref, v_ref, kt_ref, dq_ref, dk_ref, dv_ref, total):
    step_at = pl.program_id(0)
    place = query_place[step_at]
    queries = head_rows(q_ref[...])
    grads = head_rows(g_ref[...])

    @pl.when(step_at == 0)
    def _():
        dk_ref[...] = jnp.zeros_like(dk_ref)
        dv_ref[...] = jnp.zeros_like(dv_ref)

    def block(j, diagonal):
        at = pl.ds(pl.multiple_of(j * TOK, TOK), TOK)
        scores = dot_last(k_ref[at, :], queries)
        sig = 1.0 / (1.0 + jnp.exp2(SHIFT - scores * (SCORE * LOG2E)))
        weights = sig
        if diagonal:
            row = lax.broadcasted_iota(jnp.int32, sig.shape, 1) & (TOK - 1)
            column = lax.broadcasted_iota(jnp.int32, sig.shape, 0)
            weights = jnp.where(column <= row, sig, 0.0)
        upstream = dot_last(v_ref[at, :], grads)
        score_grad = (upstream * weights * (1.0 - sig)).astype(BF)
        dk_ref[at, :] += dot(score_grad, queries)
        dv_ref[at, :] += dot(weights.astype(BF), grads)
        return dot(kt_ref[:, at], score_grad)

    total[...] = block(key_slot[place], True)

    @pl.loop(0, place)
    def _(p):
        total[...] += block(key_slot[p], False)

    dq_ref[...] = head_columns((total[...] * SCORE).T).astype(BF)


def attend_back(query_place, key_slot, q, g, k, v):
    rows = q.shape[0]
    whole = lambda i, *_: (0, 0)
    rows_spec = pl.BlockSpec((TOK, QUERY), lambda i, *_: (i, 0))
    return pl.pallas_call(
        attend_back_kernel,
        grid_spec=pltpu.PrefetchScalarGridSpec(
            num_scalar_prefetch=2,
            grid=(rows // TOK,),
            in_specs=[
                rows_spec,
                rows_spec,
                pl.BlockSpec(k.shape, whole),
                pl.BlockSpec(v.shape, whole),
                pl.BlockSpec((HEAD, k.shape[0]), whole),
            ],
            out_specs=[rows_spec, pl.BlockSpec(k.shape, whole), pl.BlockSpec(v.shape, whole)],
            scratch_shapes=[pltpu.VMEM((HEAD, 4 * TOK), F32)],
        ),
        out_shape=[
            jax.ShapeDtypeStruct(q.shape, BF),
            jax.ShapeDtypeStruct(k.shape, F32),
            jax.ShapeDtypeStruct(v.shape, F32),
        ],
        compiler_params=pltpu.CompilerParams(vmem_limit_bytes=16 * 1024 * 1024),
        cost_estimate=pl.CostEstimate(flops=5 * 2 * 2048 * 2048 * 256, bytes_accessed=4 * 1024 * 1024, transcendentals=0),
    )(query_place, key_slot, q, g, k, v, k.T)


def on_device(
    tokens,
    cotangent,
    block_places,
    valid_counts,
    attn_gain,
    mlp_gain,
    query_weight,
    key_weight,
    value_weight,
    output_weight,
    gate_weight,
    up_weight,
    down_weight,
):
    replica = lax.axis_index("batch")
    member = lax.axis_index("blk")
    yh, x = replica // 4, replica % 4
    yl, z, c = member // 8, (member // 2) % 4, member % 2
    y = 2 * yh + yl
    s = 1 - 2 * c
    first_core = c == 0

    def around(coordinate):
        return [coordinate, (coordinate - s) % 4, (coordinate + s) % 4, (coordinate + 2) % 4]


    def by_core(own, other):
        return jnp.where(first_core, jnp.stack([own, other]), jnp.stack([other, own]))

    def resplit(parts):
        mine = take(parts, c, 1)
        other = swap(take(parts, 1 - c, 1))
        owned = jnp.moveaxis(by_core(mine, other), 0, 1)
        spots = around(z)
        keep, before, after, far = [take(owned, spot) for spot in spots]
        got_before = step(after, "z", 1)
        got_after = step(before, "z", -1)
        got_far = across(far, "z")
        return put_all([keep, got_before, got_after, got_far], spots, 0, 4)

    def spread(part, lead):
        n = len(lead)
        columns = part.shape[-1]
        half = put_all(ring_gather(part, "x"), around(x), n + 1, 4).reshape(lead + (1024, columns))
        low = lax.slice_in_dim(half, 0, 512, axis=n)
        high = lax.slice_in_dim(half, 512, 1024, axis=n)
        other = jnp.concatenate([step(low, "y", 1), step(high, "y", -1)], axis=n)
        full = jnp.where(yl == 0, jnp.concatenate([half, other], axis=n), jnp.concatenate([other, half], axis=n))
        return full

    def rows_of(weight, count=32):
        return lax.dynamic_slice_in_dim(weight, x * count, count, axis=0)

    def chips_of(rows, width):
        return rows.reshape(rows.shape[0], 4, 2, width).transpose(1, 2, 0, 3)

    query_part = chips_of(rows_of(query_weight), QUERY)
    key_part = rows_of(key_weight).reshape(32, 4, HEAD).transpose(1, 0, 2)
    value_part = rows_of(value_weight).reshape(32, 4, HEAD).transpose(1, 0, 2)
    attn_part = resplit(jnp.concatenate([query_part, jnp.stack([key_part, value_part], axis=1)], axis=-1))
    out_part = send(
        rows_of(output_weight), lambda yh, x, yl, z, c: (yh, x, c, 2 * yl + z // 2, z % 2)
    )
    out_part = out_part.reshape(32, 8, QUERY).transpose(1, 0, 2)
    attn_part = jnp.concatenate([out_part, attn_part.reshape(8, 32, QUERY + HEAD)], axis=-1)
    attn_full = spread(attn_part, ())
    w_out = attn_full[:, :QUERY].reshape(2, 8, 128, QUERY).transpose(0, 2, 1, 3).reshape(QUERY, D)
    w_query = attn_full[:, QUERY : 2 * QUERY]
    w_kv = attn_full[:, 2 * QUERY :]

    down_rows = lax.dynamic_slice_in_dim(down_weight, x * 32, 32, axis=1).T
    mlp_rows = jnp.stack([rows_of(gate_weight), rows_of(up_weight), down_rows])
    mlp_part = resplit(mlp_rows.reshape(3, 32, 4, 2, WIDE).transpose(2, 3, 0, 1, 4))
    mlp_part = mlp_part.transpose(2, 0, 1, 3, 4).reshape(3, 8, 32, WIDE)
    w_gate_up = spread(mlp_part[:2], (2,))
    w_gate, w_up = w_gate_up[0], w_gate_up[1]
    w_down = spread(mlp_part[2:], (1,))[0]


    def gather_tokens(rows):
        parts = []
        for part in ring_gather(rows, "z"):
            parts += [part, swap(part)]
        return jnp.concatenate(parts, axis=0)

    def scatter_tokens(partial):
        groups = partial.reshape(4, 2, TOK, D)
        sums = [None] * 4
        for g in (3, 1, 2, 0):
            sums[g] = add(groups[g, 0], swap(groups[g, 1].astype(BF)))
        return ring_scatter(*sums, "z")

    def flip(rows):
        return jnp.flip(rows.reshape(-1, 2, TOK, rows.shape[-1]), axis=1).reshape(rows.shape)

    chips = around(z)
    chunk_chip = jnp.stack([chips[0], chips[0], chips[1], chips[2], chips[2], chips[1], chips[3], chips[3]])
    chunk_core = jnp.stack([c, 1 - c] * 4)
    chunk_block = chunk_chip * 2 + chunk_core
    places = block_places[0]
    counts = valid_counts[0]
    key_block = jnp.concatenate([yl * 8 + chunk_block, (1 - yl) * 8 + chunk_block])
    key_place = lookup(places, key_block)
    query_place = key_place[:8]
    key_count = lookup(counts, key_block)
    slots = jnp.arange(16, dtype=jnp.int32)
    key_slot = jnp.sum(jnp.where(key_place[None, :] == slots[:, None], slots[None, :], 0), axis=1)
    usable = (jnp.arange(TOK, dtype=jnp.int32)[None, :] < key_count[:, None]).reshape(16 * TOK, 1)

    gain_one = attn_gain.astype(F32)
    gain_two = mlp_gain.astype(F32)
    rows_in = tokens[0].astype(F32)
    scale_attn = rms_scale(rows_in)
    normed_attn = gather_tokens((rows_in * scale_attn * gain_one).astype(BF))
    grad_rows = gather_tokens(cotangent[0])

    queries = dot(normed_attn, w_query).astype(BF)
    kv_own = dot(normed_attn, w_kv).astype(BF)
    kv_mine = jnp.concatenate([kv_own, to_half(kv_own)], axis=0)
    kv_other = flip(swap(kv_mine))
    keys = jnp.where(first_core, kv_mine, kv_other)
    values = jnp.where(usable, jnp.where(first_core, kv_other, kv_mine), 0)
    attn_rows = attend(query_place, key_slot, queries, keys, values)
    residual = rows_in + scatter_tokens(dot(attn_rows, w_out))
    scale_mlp = rms_scale(residual)
    normed_mlp = gather_tokens((residual * scale_mlp * gain_two).astype(BF))

    gate = dot(normed_mlp, w_gate)
    up_rows = dot(normed_mlp, w_up)
    sig_gate = jax.nn.sigmoid(gate)
    silu_gate = gate * sig_gate
    hidden = (silu_gate * up_rows).astype(BF)
    hidden_grad = dot(grad_rows, w_down)
    gate_grad_rows = (hidden_grad * up_rows * sig_gate * (1.0 + gate * (1.0 - sig_gate))).astype(BF)
    up_grad_rows = (hidden_grad * silu_gate).astype(BF)
    normed_grad = scatter_tokens(dot_last(gate_grad_rows, w_gate) + dot_last(up_grad_rows, w_up))
    branch = scatter_tokens(dot_last(hidden, w_down))
    layer_out = (residual + branch).astype(BF)[None]

    residual_grad = cotangent[0].astype(F32) + norm_back(residual, scale_mlp, gain_two, normed_grad)
    mlp_gain_part = jnp.sum(normed_grad * residual * scale_mlp, axis=0)
    branch_grad = gather_tokens(residual_grad.astype(BF))
    attn_grad = dot_last(branch_grad, w_out).astype(BF)
    query_grad_rows, key_terms, value_terms = attend_back(
        query_place, key_slot, queries, attn_grad, keys, values
    )
    key_terms = (key_terms * SCORE).astype(BF)
    value_terms = jnp.where(usable, value_terms, 0.0).astype(BF)
    kv_keep = jnp.where(first_core, key_terms, value_terms)
    kv_give = flip(swap(jnp.where(first_core, value_terms, key_terms)))
    kv_terms = add(kv_keep, kv_give)
    half_rows = 8 * TOK
    kv_grad_rows = add(kv_terms[:half_rows], to_half(kv_terms[half_rows:].astype(BF))).astype(BF)
    normed_attn_grad = scatter_tokens(dot_last(query_grad_rows, w_query) + dot_last(kv_grad_rows, w_kv))
    tokens_grad = (
        residual_grad + norm_back(rows_in, scale_attn, gain_one, normed_attn_grad)
    ).astype(BF)[None]
    attn_gain_part = jnp.sum(normed_attn_grad * rows_in * scale_attn, axis=0)
    attn_gain_grad, mlp_gain_grad = lax.psum((attn_gain_part, mlp_gain_part), BOTH)


    def reduce_planes(grads, lead):
        n = len(lead)
        columns = grads.shape[-1]
        split = grads.reshape(lead + (2, 8, 2, 4, 16, columns))
        head = (slice(None),) * n

        def over_y(part):
            picks = []
            for spot in around(y):
                picks.append(take(take(part, spot // 2, n + 2), spot % 2, n))
            return ring_scatter(*picks, "y")

        low = over_y(split[head + (slice(None), slice(0, 4))])
        low = ring_scatter(*[take(low, spot, n + 1) for spot in around(x)], "x")
        high = split[head + (slice(None), slice(4, 8))]
        high = ring_scatter(*[take(high, spot, n + 3) for spot in around(x)], "x")
        high = over_y(high)
        return jnp.concatenate([low, high], axis=n).astype(BF)

    def resplit_back(part):
        spots = around(z)
        keep, before, after, far = [take(part, spot) for spot in spots]
        got_before = step(after, "z", 1)
        got_after = step(before, "z", -1)
        got_far = across(far, "z")
        got = put_all([keep, got_before, got_after, got_far], spots, 0, 4)
        mine = take(got, c, 1)
        other = swap(take(got, 1 - c, 1))
        return jnp.moveaxis(by_core(mine, other), 0, 1)

    def gather_batch(part, lead):
        n = len(lead)
        columns = part.shape[-1]
        head = (slice(None),) * n

        def over_yh(value, axis):
            other = across(value, "y")
            return jnp.where(yh == 0, jnp.stack([value, other], axis), jnp.stack([other, value], axis))

        low = put_all(ring_gather(part[head + (slice(0, 4),)], "x"), around(x), n + 1, 4)
        low = over_yh(low, n + 1)
        high = over_yh(part[head + (slice(4, 8),)], n + 1)
        high = put_all(ring_gather(high, "x"), around(x), n + 2, 4)
        return jnp.concatenate([low, high], axis=n).reshape(lead + (8, 128, columns))

    mlp_grads = jnp.stack(
        [
            dot_first(normed_mlp, gate_grad_rows).astype(BF),
            dot_first(normed_mlp, up_grad_rows).astype(BF),
            dot_first(grad_rows, hidden).astype(BF),
        ]
    )
    mlp_grads = reduce_planes(mlp_grads, (3,))
    mlp_grads = resplit_back(mlp_grads.reshape(3, 4, 2, 16, WIDE).transpose(1, 2, 0, 3, 4))
    mlp_grads = gather_batch(mlp_grads.transpose(2, 0, 1, 3, 4).reshape(3, 8, 16, WIDE), (3,))
    mlp_grads = mlp_grads.astype(F32).transpose(0, 2, 1, 3).reshape(3, 128, FF)
    gate_grad, up_grad, down_grad = mlp_grads[0], mlp_grads[1], mlp_grads[2].T

    out_grads = dot_first(attn_rows, branch_grad).astype(BF)
    out_grads = out_grads.reshape(2, 128, 8, QUERY).transpose(0, 2, 1, 3).reshape(D, QUERY)
    query_grads = dot_first(normed_attn, query_grad_rows).astype(BF)
    kv_grads = dot_first(normed_attn, kv_grad_rows).astype(BF)
    attn_grads = reduce_planes(jnp.concatenate([out_grads, query_grads, kv_grads], axis=-1), ())
    out_grads = send(
        attn_grads[..., :QUERY], lambda yh, x, yl, z, c: (yh, x, z // 2, 2 * (z % 2) + c, yl)
    )
    qkv_grads = resplit_back(attn_grads[..., QUERY:].reshape(4, 2, 16, QUERY + HEAD)).reshape(8, 16, QUERY + HEAD)
    attn_grads = gather_batch(jnp.concatenate([out_grads, qkv_grads], axis=-1), ()).astype(F32)
    output_grad = attn_grads[..., :QUERY].transpose(1, 0, 2).reshape(128, D)
    query_grad = attn_grads[..., QUERY : 2 * QUERY].transpose(1, 0, 2).reshape(128, D)
    kv_grad = attn_grads[..., 2 * QUERY :].reshape(4, 2, 128, HEAD).transpose(1, 2, 0, 3).reshape(2, 128, 4 * HEAD)
    return (
        layer_out,
        tokens_grad,
        attn_gain_grad,
        mlp_gain_grad,
        query_grad,
        kv_grad[0],
        kv_grad[1],
        output_grad,
        gate_grad,
        up_grad,
        down_grad,
    )


def solution(mesh):
    in_specs = (
        P("batch", "blk", None),
        P("batch", "blk", None),
        P("batch", None),
        P("batch", None),
        P(),
        P(),
        P("blk", None),
        P("blk", None),
        P("blk", None),
        P("blk", None),
        P("blk", None),
        P("blk", None),
        P(None, "blk"),
    )
    out_specs = (
        P("batch", "blk", None),
        P("batch", "blk", None),
        P(),
        P(),
        P("blk", None),
        P("blk", None),
        P("blk", None),
        P("blk", None),
        P("blk", None),
        P("blk", None),
        P(None, "blk"),
    )
    return jax.shard_map(
        on_device, mesh=mesh, in_specs=in_specs, out_specs=out_specs, check_vma=False
    )
```

time: 1610 us -> 871 us (0.54)
  waiting for transfers between devices: 1070 us -> 253 us
  matrix products: 249 us -> 98 us
  starting transfers between devices: 0.69 us -> 121 us
  local copies, waits for them, and re-layouts: 100 us -> 180 us
  blocking collectives: 134 us -> 64 us
  other arithmetic: 21.2 us -> 82.6 us
  Pallas kernels: 0 us -> 58.7 us
    all_gather x9 -> x0, waiting for transfers between devices: 536 us -> none  [the longest x1 120 us: on_device(): lax.all_gather(down_weight, 'blk', axis=1, tiled=True)]
    reduce_scatter x1 -> x0, waiting for transfers between devices: 455 us -> none  [on_device(): lax.psum_scatter(jnp.concatenate(blocks_out, axis=1).astype(jnp.bfloat16)...]
    ppermute x0 -> x133, waiting for transfers between devices: none -> 253 us  [send(): return lax.ppermute(value, BOTH, pairs)]
    dot_general x45 -> x18, matrix products: 249 us -> 98 us  [the longest x6 38.6 us: dot_last(): lax.dot_general(left, right, (((1,), (1,)), ((), ())), preferred_element_...]
    ppermute x0 -> x133, starting transfers between devices: none -> 121 us  [send(): return lax.ppermute(value, BOTH, pairs)]
    unnamed x15 -> x0, waiting for transfers between devices: 78.3 us -> none
    psum x1, blocking collectives: 134 us -> 64 us  [on_device(): lax.psum((attn_gain_part, mlp_gain_part), BOTH)]
    pallas_call x0 -> x2, Pallas kernels: none -> 58.7 us  [the longest x1 33.3 us: attend_back(): pl.pallas_call(attend_back_kernel, grid_spec=pltpu.PrefetchScalarGridSpec...]
  transfers between devices with their start and end apart: 13 -> 133, of which waited for: 12 -> 49; matrix products, arithmetic and copies ran while one was open for 10% -> 31% of each run, Pallas kernels for 0% -> 7%
where the time goes in v1:
time: 871 us; the launch traced here: 861 us
  waiting for transfers between devices  253 us (29%)
  local copies, waits for them, and re-layouts  180 us (21%)
  starting transfers between devices  121 us (14%)
  matrix products  98 us (11%)
  other arithmetic  82.6 us (9%)
  blocking collectives  64 us (7%)
  Pallas kernels  58.7 us (7%)
    ppermute x133, waiting for transfers between devices, send(): return lax.ppermute(value, BOTH, pairs)  253 us
    ppermute x133, starting transfers between devices, send(): return lax.ppermute(value, BOTH, pairs)  121 us
    psum x1, blocking collectives, on_device(): lax.psum((attn_gain_part, mlp_gain_part), BOTH)  64 us
    unnamed x164, local copies, waits for them, and re-layouts  43.3 us
    dot_general x6, matrix products, dot_last(): lax.dot_general(left, right, (((1,), (1,)), ((), ())), preferred_element_...  38.6 us
    pallas_call x1, Pallas kernels, attend_back(): pl.pallas_call(attend_back_kernel, grid_spec=pltpu.PrefetchScalarGridSpec...  33.3 us
    dot_general x6, matrix products, dot(): return jnp.dot(left, right, preferred_element_type=F32)  32 us
    dot_general x6, matrix products, dot_first(): lax.dot_general(left, right, (((0,), (0,)), ((), ())), preferred_element_...  27.3 us
  transfers between devices with their start and end apart: 133, of which 49 were waited for; matrix products, arithmetic and copies ran while one was open for 31% of the time, Pallas kernels for 7%

profile of v1, /device:TPU:24, one launch (start us, length us, event | category | flops | bytes accessed | tf_op | source)
XLA Modules:
  0.0 861.0 jit_solution(2769366542149593949)
XLA Ops:
  33.9 5.2 collective-permute-done.9
  53.4 6.4 collective-permute-done.12
  68.1 8.0 collective-permute-done.55
  91.8 6.2 collective-permute-done.36
  122.7 18.3 %collective-permute-done.42 = bf16[1,8,32,704]{3,2,1,0:T(8,128)(2,1)} collective-permute-done((bf16[1,8,32,704]{3,2,1,0:T(8,128)(2,1)}, bf16[1,8,32,704]{3,2,1,0:T(8,128)(2,1)}, u32[]{:S(2)}, u32[]{:S(2)}) %collective-permute-start.42) | collective-permute-done | bytes 360480 | tf_op jit(solution)/shard_map/ppermute | solution.py:33
  148.1 8.5 maximum_select_fusion.2
  179.1 25.4 %shard_map.212 = bf16[1024,256]{1,0:T(8,128)(2,1)S(1)} custom-call(s32[8]{0:T(128)S(1)} %bitcast.646, s32[16]{0:T(128)S(1)} %select_reduce_fusion.1.key_slot, bf16[1024,256]{1,0:T(8,128)(2,1)S(1)} %convolution_convert_fusion.7.q_ref, bf16[2048,64]{1,0:T(8,128)(2,1)S(1)} %copy.449.k_ref, bf16[2048,64]{1,0:T(8,128)(2,1)S(1)} %copy.450.v_ref), custom_call_target="tpu_custom_call" | custom-call | flops 4294967296 | bytes 2097152 | tf_op jit(solution)/shard_map/pallas_call | solution.py:170
  204.6 4.6 fusion.121
  222.9 5.8 collective-permute-start.46
  238.0 5.4 collective-permute-done.39
  262.1 7.1 fusion.108
  271.4 14.2 %collective-permute-done.40 = bf16[2,512,704]{1,2,0:T(8,128)(2,1)} collective-permute-done((bf16[2,512,704]{1,2,0:T(8,128)(2,1)}, bf16[2,512,704]{1,2,0:T(8,128)(2,1)}, u32[]{:S(2)}, u32[]{:S(2)}) %collective-permute-start.40) | collective-permute-done | bytes 1441824 | tf_op jit(solution)/shard_map/ppermute | solution.py:33
  291.9 6.5 maximum_select_fusion
  303.1 4.9 fusion.5
  308.0 8.2 multiply_convert_fusion.1
  321.7 4.7 dot_general.64
  326.4 7.5 convolution_convert_fusion.1
  333.9 7.8 fusion.4
  346.1 4.6 copy.500
  350.7 4.6 copy.501
  355.4 4.8 copy.502
  360.1 8.6 %pad_maximum_fusion = bf16[3,2,8,2,4,16,704]{6,5,4,3,2,1,0:T(8,128)(2,1)} fusion(bf16[1,2,8,2,4,16,704]{6,5,4,3,2,1,0:T(8,128)(2,1)} %bitcast.658, bf16[1,2,8,2,4,16,704]{6,5,4,3,2,1,0:T(8,128)(2,1)} %bitcast.657, bf16[1,2,8,2,4,16,704]{6,5,4,3,2,1,0:T(8,128)(2,1)} %bitcast.656), kind=kLoop, calls=%fused_computation | loop fusion | flops 8650752 | bytes 17301504 | tf_op jit(solution)/shard_map/stack | solution.py:460
  368.7 6.9 fusion.114
  375.6 6.0 constant_dynamic-slice_fusion.7
  385.3 11.9 %fusion.122 = (bf16[4,2,128,2048]{3,2,1,0:T(8,128)(2,1)S(1)}, f32[4,2,128,2048]{3,2,1,0:T(8,128)}) fusion(bf16[1024,704]{1,0:T(8,128)(2,1)S(1)} %bitcast.665, bf16[512,704]{1,0:T(8,128)(2,1)S(1)} %bitcast.698, bf16[512,704]{1,0:T(8,128)(2,1)S(1)} %bitcast.696, pred[]{:T(512)S(6)} %eq.136, bf16[4,2,128,704]{2,1,0,3:T(2,128)(2,1)S(1)} %copy-done.28), kind=kOutput, calls=%fused_computation.391 | convolution fusion | flops 2973630464 | bytes 16908288 | tf_op jit(solution)/shard_map/dot_general | solution.py:124
  398.9 7.0 convolution_add_fusion.1
  414.0 7.4 collective-permute-done.52
  435.7 10.6 %collective-permute-done.63 = bf16[128,2048]{1,0:T(8,128)(2,1)S(1)} collective-permute-done((bf16[128,2048]{1,0:T(8,128)(2,1)S(1)}, bf16[128,2048]{1,0:T(8,128)(2,1)S(1)}, u32[]{:S(2)}, u32[]{:S(2)}) %collective-permute-start.63) | collective-permute-done | bytes 524320 | tf_op jit(solution)/shard_map/ppermute | solution.py:33
  463.3 9.5 %collective-permute-done.69 = bf16[128,2048]{1,0:T(8,128)(2,1)S(1)} collective-permute-done((bf16[128,2048]{1,0:T(8,128)(2,1)}, bf16[128,2048]{1,0:T(8,128)(2,1)S(1)}, u32[]{:S(2)}, u32[]{:S(2)}) %collective-permute-start.69) | collective-permute-done | bytes 524320 | tf_op jit(solution)/shard_map/ppermute | solution.py:33
  475.8 7.8 collective-permute-done.115
  526.7 33.3 %shard_map.213 = (bf16[1024,256]{1,0:T(8,128)(2,1)S(1)}, f32[2048,64]{1,0:T(8,128)S(1)}, f32[2048,64]{1,0:T(8,128)S(1)}) custom-call(s32[8]{0:T(128)S(1)} %bitcast.647, s32[16]{0:T(128)S(1)} %select_reduce_fusion.1.key_slot, bf16[1024,256]{1,0:T(8,128)(2,1)S(1)} %copy-done.7, bf16[1024,256]{1,0:T(8,128)(2,1)S(1)} %convolution_convert_fusion.6.g_ref, ...), custom_call_target="tpu_custom_call" | custom-call | flops 10737418240 | bytes 4194304 | tf_op jit(solution)/shard_map/pallas_call | solution.py:228
  560.0 4.5 convolution_convert_fusion.3
  564.5 5.9 fusion.65
  578.4 4.7 collective-permute-start.131
  605.5 4.9 convolution_add_fusion
  614.1 6.9 collective-permute-done.91
  631.9 28.8 %collective-permute-done.86 = bf16[4,4,16,576]{3,2,0,1:T(8,128)(2,1)S(1)} collective-permute-done((bf16[4,4,16,576]{3,2,0,1:T(8,128)(2,1)S(1)}, bf16[4,4,16,576]{3,2,0,1:T(8,128)(2,1)S(1)}, u32[]{:S(2)}, u32[]{:S(2)}) %collective-permute-start.86) | collective-permute-done | bytes 294944 | tf_op jit(solution)/shard_map/ppermute | solution.py:33
  662.1 6.8 collective-permute-done.92
  687.1 5.0 collective-permute-done.97
  695.9 5.3 collective-permute-done.99
  704.6 6.6 collective-permute-done.96
  717.4 6.2 collective-permute-done.101
  723.7 4.5 collective-permute-done.102
  729.5 4.8 collective-permute-done.103
  734.3 6.5 collective-permute-done.106
  741.4 4.9 collective-permute-done.107
  753.1 5.5 collective-permute-done.108
  794.0 64.0 %all-reduce = (f32[2048]{0:T(1024)}, f32[2048]{0:T(1024)}) all-reduce(f32[2048]{0:T(1024)S(1)} %get-tuple-element.85, f32[2048]{0:T(1024)S(1)} %get-tuple-element.83), channel_id=1, replica_groups=mesh['batch'=8,'blk'=16] {'batch','blk'}, use_global_device_ids=true, to_apply=%region_8.9 | all-reduce | flops 4096 | bytes 32768 | tf_op jit(solution)/shard_map/psum | solution.py:412
  (626 shorter events, 404.5 us)
Async XLA Ops:
  6.1 54.2 %collective-permute-start = (bf16[128,2048]{1,0:T(8,128)(2,1)}, bf16[128,2048]{1,0:T(8,128)(2,1)}, u32[]{:S(2)}, u32[]{:S(2)}) collective-permute-start(bf16[128,2048]{1,0:T(8,128)(2,1)} %get-tuple-element.103), channel_id=1, source_target_pairs={{0,1},{1,0},{2,3},{3,2},{4,5},{5,4},{6,7},{7,6},{8,9},{9,8},{10,11... | collective-permute-start | bytes 1572872 | tf_op jit(solution)/shard_map/ppermute | solution.py:33
  6.1 59.3 %collective-permute-start.1 = (bf16[128,2048]{1,0:T(8,128)(2,1)}, bf16[128,2048]{1,0:T(8,128)(2,1)}, u32[]{:S(2)}, u32[]{:S(2)}) collective-permute-start(bf16[128,2048]{1,0:T(8,128)(2,1)} %get-tuple-element.103), channel_id=1, source_target_pairs={{0,2},{1,7},{2,4},{3,1},{4,6},{5,3},{6,0},{7,5},{8,10},{9,15},{10,... | collective-permute-start | bytes 1572872 | tf_op jit(solution)/shard_map/ppermute | solution.py:33
  8.0 94.9 %collective-permute-start.3 = (bf16[128,2048]{1,0:T(8,128)(2,1)}, bf16[128,2048]{1,0:T(8,128)(2,1)}, u32[]{:S(2)}, u32[]{:S(2)}) collective-permute-start(bf16[128,2048]{1,0:T(8,128)(2,1)} %get-tuple-element.103), channel_id=1, source_target_pairs={{0,6},{1,3},{2,0},{3,5},{4,2},{5,7},{6,4},{7,1},{8,14},{9,11},{10,... | collective-permute-start | bytes 1572872 | tf_op jit(solution)/shard_map/ppermute | solution.py:33
  15.4 33.4 %collective-permute-start.7 = (bf16[32,2048]{1,0:T(8,128)(2,1)}, bf16[32,2048]{1,0:T(8,128)(2,1)}, u32[]{:S(2)}, u32[]{:S(2)}) collective-permute-start(bf16[32,2048]{1,0:T(8,128)(2,1)} %constant_dynamic-slice_fusion.24), channel_id=1, source_target_pairs={{0,0},{1,8},{2,1},{3,9},{4,2},{5,10},{6,3},{7,11},{8,4},{9,12},{10... | collective-permute-start | bytes 393224 | tf_op jit(solution)/shard_map/ppermute | solution.py:33
  60.2 43.5 %collective-permute-start.57 = (bf16[128,2048]{1,0:T(8,128)(2,1)}, bf16[128,2048]{1,0:T(8,128)(2,1)}, u32[]{:S(2)}, u32[]{:S(2)}) collective-permute-start(bf16[128,2048]{1,0:T(8,128)(2,1)} %bitcast.99), channel_id=1, source_target_pairs={{0,6},{1,3},{2,0},{3,5},{4,2},{5,7},{6,4},{7,1},{8,14},{9,11},{10,... | collective-permute-start | bytes 1572872 | tf_op jit(solution)/shard_map/ppermute | solution.py:33
  76.1 29.4 %collective-permute-start.2 = (bf16[128,2048]{1,0:T(8,128)(2,1)}, bf16[128,2048]{1,0:T(8,128)(2,1)}, u32[]{:S(2)}, u32[]{:S(2)}) collective-permute-start(bf16[128,2048]{1,0:T(8,128)(2,1)} %collective-permute-done.1), channel_id=1, source_target_pairs={{0,1},{1,0},{2,3},{3,2},{4,5},{5,4},{6,7},{7,6},{8,9},{9,8},{10,11... | collective-permute-start | bytes 1572872 | tf_op jit(solution)/shard_map/ppermute | solution.py:33
  90.4 24.5 %collective-permute-start.5 = (bf16[128,2048]{1,0:T(8,128)(2,1)}, bf16[128,2048]{1,0:T(8,128)(2,1)}, u32[]{:S(2)}, u32[]{:S(2)}) collective-permute-start(bf16[128,2048]{1,0:T(8,128)(2,1)} %collective-permute-done.1), channel_id=1, source_target_pairs={{0,2},{1,7},{2,4},{3,1},{4,6},{5,3},{6,0},{7,5},{8,10},{9,15},{10,... | collective-permute-start | bytes 1572872 | tf_op jit(solution)/shard_map/ppermute | solution.py:33
  109.3 32.8 %collective-permute-start.15 = (bf16[512,576]{0,1:T(8,128)(2,1)S(1)}, bf16[512,576]{0,1:T(8,128)(2,1)S(1)}, u32[]{:S(2)}, u32[]{:S(2)}) collective-permute-start(bf16[512,576]{0,1:T(8,128)(2,1)S(1)} %copy-done.37), channel_id=1, source_target_pairs={{0,8},{1,73},{2,10},{3,75},{4,12},{5,77},{6,14},{7,79},{8,64},{9,1... | collective-permute-start | bytes 1769480 | tf_op jit(solution)/shard_map/ppermute | solution.py:33
  112.0 33.0 %collective-permute-start.16 = (bf16[512,576]{0,1:T(8,128)(2,1)}, bf16[512,576]{0,1:T(8,128)(2,1)}, u32[]{:S(2)}, u32[]{:S(2)}) collective-permute-start(bf16[512,576]{0,1:T(8,128)(2,1)} %copy.444), channel_id=1, source_target_pairs={{0,72},{1,9},{2,74},{3,11},{4,76},{5,13},{6,78},{7,15},{8,0},{9,65... | collective-permute-start | bytes 1769480 | tf_op jit(solution)/shard_map/ppermute | solution.py:33
  114.9 106.8 %collective-permute-start.37 = (bf16[2,8,32,704]{3,2,1,0:T(8,128)(2,1)}, bf16[2,8,32,704]{3,2,1,0:T(8,128)(2,1)}, u32[]{:S(2)}, u32[]{:S(2)}) collective-permute-start(bf16[2,8,32,704]{3,2,1,0:T(8,128)(2,1)} %bitcast.67), channel_id=1, source_target_pairs={{0,16},{1,49},{2,18},{3,51},{4,20},{5,53},{6,22},{7,55},{8,24},{9,... | collective-permute-start | bytes 2162696 | tf_op jit(solution)/shard_map/ppermute | solution.py:33
  116.7 24.3 %collective-permute-start.42 = (bf16[1,8,32,704]{3,2,1,0:T(8,128)(2,1)}, bf16[1,8,32,704]{3,2,1,0:T(8,128)(2,1)}, u32[]{:S(2)}, u32[]{:S(2)}) collective-permute-start(bf16[1,8,32,704]{3,2,1,0:T(8,128)(2,1)} %bitcast.78), channel_id=1, source_target_pairs={{0,16},{1,49},{2,18},{3,51},{4,20},{5,53},{6,22},{7,55},{8,24},{9,... | collective-permute-start | bytes 1081352 | tf_op jit(solution)/shard_map/ppermute | solution.py:33
  117.6 105.3 %collective-permute-start.38 = (bf16[2,8,32,704]{3,2,1,0:T(8,128)(2,1)}, bf16[2,8,32,704]{3,2,1,0:T(8,128)(2,1)}, u32[]{:S(2)}, u32[]{:S(2)}) collective-permute-start(bf16[2,8,32,704]{3,2,1,0:T(8,128)(2,1)} %bitcast.67), channel_id=1, source_target_pairs={{0,48},{1,17},{2,50},{3,19},{4,52},{5,21},{6,54},{7,23},{8,56},{9,... | collective-permute-start | bytes 2162696 | tf_op jit(solution)/shard_map/ppermute | solution.py:33
  145.0 84.9 %collective-permute-start.60 = (bf16[128,2048]{1,0:T(8,128)(2,1)}, bf16[128,2048]{1,0:T(8,128)(2,1)}, u32[]{:S(2)}, u32[]{:S(2)}) collective-permute-start(bf16[128,2048]{1,0:T(8,128)(2,1)} %collective-permute-done.59), channel_id=1, source_target_pairs={{0,1},{1,0},{2,3},{3,2},{4,5},{5,4},{6,7},{7,6},{8,9},{9,8},{10,11... | collective-permute-start | bytes 1572872 | tf_op jit(solution)/shard_map/ppermute | solution.py:33
  156.7 54.1 %collective-permute-start.44 = (bf16[1,8,32,704]{3,2,1,0:T(8,128)(2,1)}, bf16[1,8,32,704]{3,2,1,0:T(8,128)(2,1)}, u32[]{:S(2)}, u32[]{:S(2)}) collective-permute-start(bf16[1,8,32,704]{3,2,1,0:T(8,128)(2,1)} %collective-permute-done.42), channel_id=1, source_target_pairs={{0,16},{1,49},{2,18},{3,51},{4,20},{5,53},{6,22},{7,55},{8,24},{9,... | collective-permute-start | bytes 1081352 | tf_op jit(solution)/shard_map/ppermute | solution.py:33
  217.9 33.4 %collective-permute-start.45 = (bf16[1,512,704]{1,2,0:T(8,128)(2,1)}, bf16[1,512,704]{1,2,0:T(8,128)(2,1)}, u32[]{:S(2)}, u32[]{:S(2)}) collective-permute-start(bf16[1,512,704]{1,2,0:T(8,128)(2,1)} %copy.472), channel_id=1, source_target_pairs={{0,8},{1,73},{2,10},{3,75},{4,12},{5,77},{6,14},{7,79},{8,64},{9,1... | collective-permute-start | bytes 2162696 | tf_op jit(solution)/shard_map/ppermute | solution.py:33
  222.9 32.4 %collective-permute-start.46 = (bf16[1,512,704]{1,2,0:T(8,128)(2,1)}, bf16[1,512,704]{1,2,0:T(8,128)(2,1)}, u32[]{:S(2)}, u32[]{:S(2)}) collective-permute-start(bf16[1,512,704]{1,2,0:T(8,128)(2,1)} %copy.474), channel_id=1, source_target_pairs={{0,72},{1,9},{2,74},{3,11},{4,76},{5,13},{6,78},{7,15},{8,0},{9,65... | collective-permute-start | bytes 2162696 | tf_op jit(solution)/shard_map/ppermute | solution.py:33
  231.9 26.0 %collective-permute-start.19 = (bf16[128,2048]{1,0:T(8,128)(2,1)}, bf16[128,2048]{1,0:T(8,128)(2,1)S(1)}, u32[]{:S(2)}, u32[]{:S(2)}) collective-permute-start(bf16[128,2048]{1,0:T(8,128)(2,1)} %get-tuple-element.138), channel_id=1, source_target_pairs={{0,1},{1,0},{2,3},{3,2},{4,5},{5,4},{6,7},{7,6},{8,9},{9,8},{10,11... | collective-permute-start | bytes 1572872 | tf_op jit(solution)/shard_map/ppermute | solution.py:33
  234.8 23.1 %collective-permute-start.21 = (bf16[128,2048]{1,0:T(8,128)(2,1)}, bf16[128,2048]{1,0:T(8,128)(2,1)}, u32[]{:S(2)}, u32[]{:S(2)}) collective-permute-start(bf16[128,2048]{1,0:T(8,128)(2,1)} %get-tuple-element.115), channel_id=1, source_target_pairs={{0,6},{1,3},{2,0},{3,5},{4,2},{5,7},{6,4},{7,1},{8,14},{9,11},{10,... | collective-permute-start | bytes 1572872 | tf_op jit(solution)/shard_map/ppermute | solution.py:33
  251.3 34.3 %collective-permute-start.40 = (bf16[2,512,704]{1,2,0:T(8,128)(2,1)}, bf16[2,512,704]{1,2,0:T(8,128)(2,1)}, u32[]{:S(2)}, u32[]{:S(2)}) collective-permute-start(bf16[2,512,704]{1,2,0:T(8,128)(2,1)} %copy.462), channel_id=1, source_target_pairs={{0,8},{1,73},{2,10},{3,75},{4,12},{5,77},{6,14},{7,79},{8,64},{9,1... | collective-permute-start | bytes 4325384 | tf_op jit(solution)/shard_map/ppermute | solution.py:33
  255.3 32.9 %collective-permute-start.41 = (bf16[2,512,704]{1,2,0:T(8,128)(2,1)}, bf16[2,512,704]{1,2,0:T(8,128)(2,1)}, u32[]{:S(2)}, u32[]{:S(2)}) collective-permute-start(bf16[2,512,704]{1,2,0:T(8,128)(2,1)} %copy.463), channel_id=1, source_target_pairs={{0,72},{1,9},{2,74},{3,11},{4,76},{5,13},{6,78},{7,15},{8,0},{9,65... | collective-permute-start | bytes 4325384 | tf_op jit(solution)/shard_map/ppermute | solution.py:33
  261.1 29.6 %collective-permute-start.27 = (bf16[128,2048]{1,0:T(8,128)(2,1)S(1)}, bf16[128,2048]{1,0:T(8,128)(2,1)S(1)}, u32[]{:S(2)}, u32[]{:S(2)}) collective-permute-start(bf16[128,2048]{1,0:T(8,128)(2,1)S(1)} %get-tuple-element.99), channel_id=1, source_target_pairs={{0,2},{1,7},{2,4},{3,1},{4,6},{5,3},{6,0},{7,5},{8,10},{9,15},{10,... | collective-permute-start | bytes 1572872 | tf_op jit(solution)/shard_map/ppermute | solution.py:33
  269.2 29.7 %collective-permute-start.26 = (bf16[128,2048]{1,0:T(8,128)(2,1)S(1)}, bf16[128,2048]{1,0:T(8,128)(2,1)}, u32[]{:S(2)}, u32[]{:S(2)}) collective-permute-start(bf16[128,2048]{1,0:T(8,128)(2,1)S(1)} %get-tuple-element.99), channel_id=1, source_target_pairs={{0,1},{1,0},{2,3},{3,2},{4,5},{5,4},{6,7},{7,6},{8,9},{9,8},{10,11... | collective-permute-start | bytes 1572872 | tf_op jit(solution)/shard_map/ppermute | solution.py:33
  269.2 29.1 %collective-permute-start.29 = (bf16[128,2048]{1,0:T(8,128)(2,1)S(1)}, bf16[128,2048]{1,0:T(8,128)(2,1)}, u32[]{:S(2)}, u32[]{:S(2)}) collective-permute-start(bf16[128,2048]{1,0:T(8,128)(2,1)S(1)} %get-tuple-element.99), channel_id=1, source_target_pairs={{0,6},{1,3},{2,0},{3,5},{4,2},{5,7},{6,4},{7,1},{8,14},{9,11},{10,... | collective-permute-start | bytes 1572872 | tf_op jit(solution)/shard_map/ppermute | solution.py:33
  382.7 46.6 %collective-permute-start.110 = (bf16[3,4,4,16,704]{4,3,1,0,2:T(8,128)(2,1)}, bf16[3,4,4,16,704]{4,3,1,0,2:T(8,128)(2,1)}, u32[]{:S(2)}, u32[]{:S(2)}) collective-permute-start(bf16[3,4,4,16,704]{4,3,1,0,2:T(8,128)(2,1)} %bitcast.630), channel_id=1, source_target_pairs={{0,8},{1,73},{2,10},{3,75},{4,12},{5,77},{6,14},{7,79},{8,64},{9,1... | collective-permute-start | bytes 3244040 | tf_op jit(solution)/shard_map/ppermute | solution.py:33
  435.6 24.5 %collective-permute-start.109 = (bf16[3,4,4,16,704]{4,3,1,0,2:T(8,128)(2,1)}, bf16[3,4,4,16,704]{4,3,1,0,2:T(8,128)(2,1)}, u32[]{:S(2)}, u32[]{:S(2)}) collective-permute-start(bf16[3,4,4,16,704]{4,3,1,0,2:T(8,128)(2,1)} %bitcast.631), channel_id=1, source_target_pairs={{0,72},{1,9},{2,74},{3,11},{4,76},{5,13},{6,78},{7,15},{8,0},{9,65... | collective-permute-start | bytes 3244040 | tf_op jit(solution)/shard_map/ppermute | solution.py:33
  446.3 27.0 %collective-permute-start.111 = (bf16[3,4,4,16,704]{4,3,1,0,2:T(8,128)(2,1)}, bf16[3,4,4,16,704]{4,3,1,0,2:T(8,128)(2,1)}, u32[]{:S(2)}, u32[]{:S(2)}) collective-permute-start(bf16[3,4,4,16,704]{4,3,1,0,2:T(8,128)(2,1)} %fusion.8), channel_id=1, source_target_pairs={{0,8},{1,73},{2,10},{3,75},{4,12},{5,77},{6,14},{7,79},{8,64},{9,1... | collective-permute-start | bytes 3244040 | tf_op jit(solution)/shard_map/ppermute | solution.py:33
  455.4 28.2 %collective-permute-start.115 = (bf16[3,2,4,2,16,704]{5,4,3,2,1,0:T(8,128)(2,1)}, bf16[3,2,4,2,16,704]{5,4,3,2,1,0:T(8,128)(2,1)}, u32[]{:S(2)}, u32[]{:S(2)}) collective-permute-start(bf16[3,2,4,2,16,704]{5,4,3,2,1,0:T(8,128)(2,1)} %get-tuple-element.124), channel_id=1, source_target_pairs={{0,48},{1,17},{2,50},{3,19},{4,52},{5,21},{6,54},{7,23},{8,56},{9,... | collective-permute-start | bytes 3244040 | tf_op jit(solution)/shard_map/ppermute | solution.py:33
  458.5 26.9 %collective-permute-start.117 = (bf16[3,2,4,2,16,704]{5,4,3,2,1,0:T(8,128)(2,1)}, bf16[3,2,4,2,16,704]{5,4,3,2,1,0:T(8,128)(2,1)}, u32[]{:S(2)}, u32[]{:S(2)}) collective-permute-start(bf16[3,2,4,2,16,704]{5,4,3,2,1,0:T(8,128)(2,1)} %fusion.6), channel_id=1, source_target_pairs={{0,16},{1,49},{2,18},{3,51},{4,20},{5,53},{6,22},{7,55},{8,24},{9,... | collective-permute-start | bytes 3244040 | tf_op jit(solution)/shard_map/ppermute | solution.py:33
  460.1 34.9 %collective-permute-start.71 = (bf16[128,2048]{1,0:T(8,128)(2,1)}, bf16[128,2048]{1,0:T(8,128)(2,1)S(1)}, u32[]{:S(2)}, u32[]{:S(2)}) collective-permute-start(bf16[128,2048]{1,0:T(8,128)(2,1)} %get-tuple-element.95), channel_id=1, source_target_pairs={{0,6},{1,3},{2,0},{3,5},{4,2},{5,7},{6,4},{7,1},{8,14},{9,11},{10,... | collective-permute-start | bytes 1572872 | tf_op jit(solution)/shard_map/ppermute | solution.py:33
  473.2 26.3 %collective-permute-start.73 = (bf16[128,2048]{1,0:T(8,128)(2,1)S(1)}, bf16[128,2048]{1,0:T(8,128)(2,1)S(1)}, u32[]{:S(2)}, u32[]{:S(2)}) collective-permute-start(bf16[128,2048]{1,0:T(8,128)(2,1)S(1)} %collective-permute-done.69), channel_id=1, source_target_pairs={{0,2},{1,7},{2,4},{3,1},{4,6},{5,3},{6,0},{7,5},{8,10},{9,15},{10,... | collective-permute-start | bytes 1572872 | tf_op jit(solution)/shard_map/ppermute | solution.py:33
  499.5 24.1 %collective-permute-start.74 = (bf16[128,2048]{1,0:T(8,128)(2,1)S(1)}, bf16[128,2048]{1,0:T(8,128)(2,1)S(1)}, u32[]{:S(2)}, u32[]{:S(2)}) collective-permute-start(bf16[128,2048]{1,0:T(8,128)(2,1)S(1)} %collective-permute-done.73), channel_id=1, source_target_pairs={{0,1},{1,0},{2,3},{3,2},{4,5},{5,4},{6,7},{7,6},{8,9},{9,8},{10,11... | collective-permute-start | bytes 1572872 | tf_op jit(solution)/shard_map/ppermute | solution.py:33
  518.9 64.1 %collective-permute-start.125 = (bf16[3,4,16,704]{3,2,1,0:T(8,128)(2,1)}, bf16[3,4,16,704]{3,2,1,0:T(8,128)(2,1)}, u32[]{:S(2)}, u32[]{:S(2)}) collective-permute-start(bf16[3,4,16,704]{3,2,1,0:T(8,128)(2,1)} %get-tuple-element.173), channel_id=1, source_target_pairs={{0,16},{1,49},{2,18},{3,51},{4,20},{5,53},{6,22},{7,55},{8,24},{9,... | collective-permute-start | bytes 811016 | tf_op jit(solution)/shard_map/ppermute | solution.py:33
  519.4 69.1 %collective-permute-start.126 = (bf16[3,4,16,704]{3,2,1,0:T(8,128)(2,1)}, bf16[3,4,16,704]{3,2,1,0:T(8,128)(2,1)}, u32[]{:S(2)}, u32[]{:S(2)}) collective-permute-start(bf16[3,4,16,704]{3,2,1,0:T(8,128)(2,1)} %get-tuple-element.173), channel_id=1, source_target_pairs={{0,48},{1,17},{2,50},{3,19},{4,52},{5,21},{6,54},{7,23},{8,56},{9,... | collective-permute-start | bytes 811016 | tf_op jit(solution)/shard_map/ppermute | solution.py:33
  522.2 54.2 %collective-permute-start.129 = (bf16[3,4,16,704]{3,2,1,0:T(8,128)(2,1)}, bf16[3,4,16,704]{3,2,1,0:T(8,128)(2,1)}, u32[]{:S(2)}, u32[]{:S(2)}) collective-permute-start(bf16[3,4,16,704]{3,2,1,0:T(8,128)(2,1)} %get-tuple-element.176), channel_id=1, source_target_pairs={{0,64},{1,65},{2,66},{3,67},{4,68},{5,69},{6,70},{7,71},{8,72},{9,... | collective-permute-start | bytes 811016 | tf_op jit(solution)/shard_map/ppermute | solution.py:33
  578.4 42.7 %collective-permute-start.130 = (bf16[3,4,2,16,704]{4,3,1,0,2:T(8,128)(2,1)}, bf16[3,4,2,16,704]{4,3,1,0,2:T(8,128)(2,1)}, u32[]{:S(2)}, u32[]{:S(2)}) collective-permute-start(bf16[3,4,2,16,704]{4,3,1,0,2:T(8,128)(2,1)} %maximum_select_fusion.8), channel_id=1, source_target_pairs={{0,16},{1,49},{2,18},{3,51},{4,20},{5,53},{6,22},{7,55},{8,24},{9,... | collective-permute-start | bytes 1622024 | tf_op jit(solution)/shard_map/ppermute | solution.py:33
  578.4 46.8 %collective-permute-start.131 = (bf16[3,4,2,16,704]{4,3,1,0,2:T(8,128)(2,1)}, bf16[3,4,2,16,704]{4,3,1,0,2:T(8,128)(2,1)}, u32[]{:S(2)}, u32[]{:S(2)}) collective-permute-start(bf16[3,4,2,16,704]{4,3,1,0,2:T(8,128)(2,1)} %maximum_select_fusion.8), channel_id=1, source_target_pairs={{0,48},{1,17},{2,50},{3,19},{4,52},{5,21},{6,54},{7,23},{8,56},{9,... | collective-permute-start | bytes 1622024 | tf_op jit(solution)/shard_map/ppermute | solution.py:33
  583.1 29.5 %collective-permute-start.127 = (bf16[3,4,16,704]{3,2,1,0:T(8,128)(2,1)}, bf16[3,4,16,704]{3,2,1,0:T(8,128)(2,1)}, u32[]{:S(2)}, u32[]{:S(2)}) collective-permute-start(bf16[3,4,16,704]{3,2,1,0:T(8,128)(2,1)} %collective-permute-done.125), channel_id=1, source_target_pairs={{0,16},{1,49},{2,18},{3,51},{4,20},{5,53},{6,22},{7,55},{8,24},{9,... | collective-permute-start | bytes 811016 | tf_op jit(solution)/shard_map/ppermute | solution.py:33
  605.2 26.7 %collective-permute-start.84 = (bf16[4,4,16,576]{3,2,0,1:T(8,128)(2,1)S(1)}, bf16[4,4,16,576]{3,2,0,1:T(8,128)(2,1)S(1)}, u32[]{:S(2)}, u32[]{:S(2)}) collective-permute-start(bf16[4,4,16,576]{3,2,0,1:T(8,128)(2,1)S(1)} %bitcast.711), channel_id=1, source_target_pairs={{0,72},{1,9},{2,74},{3,11},{4,76},{5,13},{6,78},{7,15},{8,0},{9,65... | collective-permute-start | bytes 884744 | tf_op jit(solution)/shard_map/ppermute | solution.py:33
  621.1 39.7 %collective-permute-start.90 = (bf16[2,4,2,16,576]{4,3,2,1,0:T(8,128)(2,1)S(1)}, bf16[2,4,2,16,576]{4,3,2,1,0:T(8,128)(2,1)S(1)}, u32[]{:S(2)}, u32[]{:S(2)}) collective-permute-start(bf16[2,4,2,16,576]{4,3,2,1,0:T(8,128)(2,1)S(1)} %get-tuple-element.158), channel_id=1, source_target_pairs={{0,48},{1,17},{2,50},{3,19},{4,52},{5,21},{6,54},{7,23},{8,56},{9,... | collective-permute-start | bytes 884744 | tf_op jit(solution)/shard_map/ppermute | solution.py:33
  625.1 125.1 %collective-permute-start.80 = (bf16[128,2048]{1,0:T(8,128)(2,1)S(1)}, bf16[128,2048]{1,0:T(8,128)(2,1)S(1)}, u32[]{:S(2)}, u32[]{:S(2)}) collective-permute-start(bf16[128,2048]{1,0:T(8,128)(2,1)S(1)} %get-tuple-element.128), channel_id=1, source_target_pairs={{0,1},{1,0},{2,3},{3,2},{4,5},{5,4},{6,7},{7,6},{8,9},{9,8},{10,11... | collective-permute-start | bytes 1572872 | tf_op jit(solution)/shard_map/ppermute | solution.py:33
  627.1 164.6 %collective-permute-start.77 = (bf16[128,2048]{1,0:T(8,128)(2,1)}, bf16[128,2048]{1,0:T(8,128)(2,1)}, u32[]{:S(2)}, u32[]{:S(2)}) collective-permute-start(bf16[128,2048]{1,0:T(8,128)(2,1)} %get-tuple-element.126), channel_id=1, source_target_pairs={{0,1},{1,0},{2,3},{3,2},{4,5},{5,4},{6,7},{7,6},{8,9},{9,8},{10,11... | collective-permute-start | bytes 1572872 | tf_op jit(solution)/shard_map/ppermute | solution.py:33
  627.6 33.1 %collective-permute-start.86 = (bf16[4,4,16,576]{3,2,0,1:T(8,128)(2,1)S(1)}, bf16[4,4,16,576]{3,2,0,1:T(8,128)(2,1)S(1)}, u32[]{:S(2)}, u32[]{:S(2)}) collective-permute-start(bf16[4,4,16,576]{3,2,0,1:T(8,128)(2,1)S(1)} %fusion.70), channel_id=1, source_target_pairs={{0,8},{1,73},{2,10},{3,75},{4,12},{5,77},{6,14},{7,79},{8,64},{9,1... | collective-permute-start | bytes 884744 | tf_op jit(solution)/shard_map/ppermute | solution.py:33
  631.9 126.7 %collective-permute-start.128 = (bf16[3,4,4,16,704]{4,3,2,1,0:T(8,128)(2,1)S(1)}, bf16[3,4,4,16,704]{4,3,2,1,0:T(8,128)(2,1)S(1)}, u32[]{:S(2)}, u32[]{:S(2)}) collective-permute-start(bf16[3,4,4,16,704]{4,3,2,1,0:T(8,128)(2,1)S(1)} %bitcast_dynamic-update-slice_fusion.10), channel_id=1, source_target_pairs={{0,64},{1,65},{2,66},{3,67},{4,68},{5,69},{6,70},{7,71},{8,72},{9,... | collective-permute-start | bytes 3244040 | tf_op jit(solution)/shard_map/ppermute | solution.py:33
  684.9 43.4 %collective-permute-start.132 = (bf16[3,4,2,16,704]{4,3,1,0,2:T(8,128)(2,1)}, bf16[3,4,2,16,704]{4,3,1,0,2:T(8,128)(2,1)S(1)}, u32[]{:S(2)}, u32[]{:S(2)}) collective-permute-start(bf16[3,4,2,16,704]{4,3,1,0,2:T(8,128)(2,1)} %collective-permute-done.130), channel_id=1, source_target_pairs={{0,16},{1,49},{2,18},{3,51},{4,20},{5,53},{6,22},{7,55},{8,24},{9,... | collective-permute-start | bytes 1622024 | tf_op jit(solution)/shard_map/ppermute | solution.py:33
  728.2 23.8 %collective-permute-start.82 = (bf16[128,2048]{1,0:T(8,128)(2,1)S(1)}, bf16[128,2048]{1,0:T(8,128)(2,1)S(1)}, u32[]{:S(2)}, u32[]{:S(2)}) collective-permute-start(bf16[128,2048]{1,0:T(8,128)(2,1)S(1)} %get-tuple-element.110), channel_id=1, source_target_pairs={{0,2},{1,7},{2,4},{3,1},{4,6},{5,3},{6,0},{7,5},{8,10},{9,15},{10,... | collective-permute-start | bytes 1572872 | tf_op jit(solution)/shard_map/ppermute | solution.py:33
  746.3 45.4 %collective-permute-start.79 = (bf16[128,2048]{1,0:T(8,128)(2,1)}, bf16[128,2048]{1,0:T(8,128)(2,1)}, u32[]{:S(2)}, u32[]{:S(2)}) collective-permute-start(bf16[128,2048]{1,0:T(8,128)(2,1)} %get-tuple-element.109), channel_id=1, source_target_pairs={{0,6},{1,3},{2,0},{3,5},{4,2},{5,7},{6,4},{7,1},{8,14},{9,11},{10,... | collective-permute-start | bytes 1572872 | tf_op jit(solution)/shard_map/ppermute | solution.py:33
  750.2 33.3 %collective-permute-start.104 = (bf16[4,4,16,576]{3,2,1,0:T(8,128)(2,1)S(1)}, bf16[4,4,16,576]{3,2,1,0:T(8,128)(2,1)S(1)}, u32[]{:S(2)}, u32[]{:S(2)}) collective-permute-start(bf16[4,4,16,576]{3,2,1,0:T(8,128)(2,1)S(1)} %bitcast_dynamic-update-slice_fusion.17), channel_id=1, source_target_pairs={{0,64},{1,65},{2,66},{3,67},{4,68},{5,69},{6,70},{7,71},{8,72},{9,... | collective-permute-start | bytes 884744 | tf_op jit(solution)/shard_map/ppermute | solution.py:33
  758.6 33.1 %collective-permute-start.83 = (bf16[128,2048]{1,0:T(8,128)(2,1)}, bf16[128,2048]{1,0:T(8,128)(2,1)}, u32[]{:S(2)}, u32[]{:S(2)}) collective-permute-start(bf16[128,2048]{1,0:T(8,128)(2,1)} %fusion.25), channel_id=1, source_target_pairs={{0,2},{1,7},{2,4},{3,1},{4,6},{5,3},{6,0},{7,5},{8,10},{9,15},{10,... | collective-permute-start | bytes 1572872 | tf_op jit(solution)/shard_map/ppermute | solution.py:33
  (147 other events, 1763.4 us)

commit v2 on v1

v2 whole, which is shorter than its diff:
```python
import itertools

import jax
import jax.numpy as jnp
from jax import lax
from jax.experimental import pallas as pl
from jax.experimental.pallas import tpu as pltpu
from jax.sharding import PartitionSpec as P

HEADS = 32
KV_HEADS = 4
HEAD = 64
D = 2048
FF = 5632
TOK = 128
WIDE = FF // 8
QUERY = HEADS * HEAD // 8
QKV = QUERY + HEAD
PACK = QUERY + QKV
epsilon = 1e-05
BOTH = ("batch", "blk")
BF = jnp.bfloat16
F32 = jnp.float32
MIB = 1024 * 1024
LOG2E = 1.4426950408889634
SCORE = HEAD**-0.5
SHIFT = 11.0


def device_index(yh, x, yl, z, c):
    return (((yh * 4 + x) * 2 + yl) * 4 + z) * 2 + c


def send(value, target):
    pairs = []
    for spot in itertools.product(range(2), range(4), range(2), range(4), range(2)):
        pairs.append((device_index(*spot), device_index(*target(*spot))))
    return lax.ppermute(value, BOTH, pairs)


def step(value, axis, way):
    def target(yh, x, yl, z, c):
        by = way * (1 - 2 * c)
        if axis == "x":
            x = (x + by) % 4
        elif axis == "z":
            z = (z + by) % 4
        else:
            y = (2 * yh + yl + by) % 4
            yh, yl = y // 2, y % 2
        return yh, x, yl, z, c

    return send(value, target)


def across(value, axis):
    def target(yh, x, yl, z, c):
        if axis == "z":
            z = (z + 2) % 4
        else:
            yh = 1 - yh
        return yh, x, yl, z, c

    return send(value, target)


def swap(value):
    return send(value, lambda yh, x, yl, z, c: (yh, x, yl, z, 1 - c))


def to_half(value):
    return send(value, lambda yh, x, yl, z, c: (yh, x, 1 - yl, z, c))


def ring_gather(value, axis):
    first = step(value, axis, 1)
    second = step(value, axis, -1)
    third = step(first, axis, 1)
    return value, first, second, third


def add(*terms):
    total = terms[0].astype(F32)
    for term in terms[1:]:
        total = total + term.astype(F32)
    return total


def ring_scatter(own, before, after, far, axis):
    got_far = step(far, axis, 1)
    got_after = step(before, axis, -1)
    got_before = step(add(after, got_far).astype(BF), axis, 1)
    return add(own, got_after, got_before)


def exchange_z(own, before, after, far):
    return own, step(after, "z", 1), step(before, "z", -1), across(far, "z")


def after(value, *others):
    return lax.optimization_barrier((value,) + others)[0]


def rms_scale(rows):
    return lax.rsqrt(jnp.mean(rows * rows, axis=-1, keepdims=True) + epsilon)


def norm_back(rows, scale, gain, upstream):
    weighted = gain * upstream
    return scale * weighted - rows * scale**3 * jnp.mean(weighted * rows, axis=-1, keepdims=True)


def lookup(entries, holder):
    matches = holder[:, None] == jnp.arange(entries.shape[0], dtype=jnp.int32)[None, :]
    return jnp.sum(jnp.where(matches, entries[None, :], 0), axis=1)


def dot(left, right):
    return jnp.dot(left, right, preferred_element_type=F32)


def dot_last(left, right):
    return lax.dot_general(left, right, (((1,), (1,)), ((), ())), preferred_element_type=F32)


def params(mib):
    return pltpu.CompilerParams(vmem_limit_bytes=mib * MIB)


def cost(flops, moved):
    return pl.CostEstimate(flops=flops, bytes_accessed=moved, transcendentals=0)


def call(body, tables, grid, in_specs, out_specs, out_shape, scratch, mib, flops, moved, args, aliases=None):
    return pl.pallas_call(
        body,
        grid_spec=pltpu.PrefetchScalarGridSpec(
            num_scalar_prefetch=len(tables), grid=grid, in_specs=in_specs, out_specs=out_specs, scratch_shapes=scratch
        ),
        out_shape=out_shape,
        compiler_params=params(mib),
        cost_estimate=cost(flops, moved),
        input_output_aliases=aliases or {},
    )(*tables, *args)


def sds(shape, dtype=BF):
    return jax.ShapeDtypeStruct(shape, dtype)


def at_rows(start, count):
    return pl.ds(pl.multiple_of(start, 16), count)


def pack_attn_kernel(spots, core, q_ref, k_ref, v_ref, mine_ref, other_ref):
    first = core[0] == 0
    keys = [k_ref[:, HEAD * h : HEAD * (h + 1)].astype(F32) for h in range(KV_HEADS)]
    vals = [v_ref[:, HEAD * h : HEAD * (h + 1)].astype(F32) for h in range(KV_HEADS)]
    for r in range(4):
        chip = spots[1 + r]
        both = q_ref[:, pl.ds(pl.multiple_of(chip * 2 * QUERY, 128), 2 * QUERY)].astype(F32)
        key, val = keys[0], vals[0]
        for h in range(1, KV_HEADS):
            key = jnp.where(chip == h, keys[h], key)
            val = jnp.where(chip == h, vals[h], val)
        low = jnp.concatenate([both[:, :QUERY], key], axis=1)
        high = jnp.concatenate([both[:, QUERY:], val], axis=1)
        mine_ref[r] = jnp.where(first, low, high).astype(BF)
        other_ref[r] = jnp.where(first, high, low).astype(BF)


def pack_attn(spots, core, q, k, v):
    rows = lambda i, spots, core: (spots[0], 0)
    whole = lambda i, *_: (0, 0, 0)
    shape = (4, 32, QKV)
    return call(
        pack_attn_kernel, (spots, core), (1,),
        [pl.BlockSpec((32, w.shape[1]), rows) for w in (q, k, v)],
        [pl.BlockSpec(shape, whole)] * 2, [sds(shape)] * 2, [], 16, 1000, 400000, (q, k, v),
    )


def pack_mlp_kernel(spots, core, gate_ref, up_ref, down_ref, mine_ref, other_ref, turned):
    first = core[0] == 0
    turned[...] = down_ref[...].astype(F32).T
    for r in range(4):
        at = pl.ds(pl.multiple_of(spots[1 + r] * 2 * WIDE, 128), 2 * WIDE)
        parts = (
            gate_ref[:, at].astype(F32),
            up_ref[:, at].astype(F32),
            turned[at_rows(spots[0] * 32, 32), at],
        )
        for m, both in enumerate(parts):
            low, high = both[:, :WIDE], both[:, WIDE:]
            mine_ref[r, m] = jnp.where(first, low, high).astype(BF)
            other_ref[r, m] = jnp.where(first, high, low).astype(BF)


def pack_mlp(spots, core, gate, up, down):
    rows = lambda i, spots, core: (spots[0], 0)
    whole = lambda i, *_: (0, 0, 0, 0)
    shape = (4, 3, 32, WIDE)
    return call(
        pack_mlp_kernel, (spots, core), (1,),
        [pl.BlockSpec((32, FF), rows), pl.BlockSpec((32, FF), rows), pl.BlockSpec((FF, 128), lambda i, *_: (0, 0))],
        [pl.BlockSpec(shape, whole)] * 2, [sds(shape)] * 2, [pltpu.VMEM((128, FF), F32)],
        24, 1000, 4000000, (gate, up, down),
    )


def place_attn_kernel(slot, xs, halves, *refs):
    pieces, (qkv_ref, out_ref) = refs[:8], refs[8:]
    for e in range(2):
        for r in range(4):
            piece = pieces[4 * e + r][0]
            rows = at_rows(xs[r] * 32, 32)
            out_ref[halves[e], rows, :] = piece[:, :QUERY]
            qkv_ref[halves[e], 0, rows, :] = piece[:, QUERY:]


def place_attn(slot, xs, halves, pieces):
    qkv, out = call(
        place_attn_kernel, (slot, xs, halves), (8,),
        [pl.BlockSpec((1, 32, PACK), lambda i, *_: (i, 0, 0))] * 8,
        [
            pl.BlockSpec((2, 1, 128, QKV), lambda i, slot, *_: (0, slot[i], 0, 0)),
            pl.BlockSpec((2, 128, QUERY), lambda i, *_: (0, 0, i)),
        ],
        [sds((2, 8, 128, QKV)), sds((2, 128, D))], [], 16, 1000, 5000000, tuple(pieces),
    )
    return qkv.reshape(D, QKV), out.reshape(QUERY, D)


def place_mlp_kernel(slot, xs, halves, *refs):
    pieces, out_ref = refs[:8], refs[8]
    for e in range(2):
        for r in range(4):
            rows = at_rows(xs[r] * 32, 32)
            for m in range(3):
                out_ref[m, halves[e], 0, rows, :] = pieces[4 * e + r][0, m]


def place_mlp(slot, xs, halves, pieces):
    out = call(
        place_mlp_kernel, (slot, xs, halves), (8,),
        [pl.BlockSpec((1, 3, 32, WIDE), lambda i, *_: (i, 0, 0, 0))] * 8,
        pl.BlockSpec((3, 2, 1, 128, WIDE), lambda i, slot, *_: (0, 0, slot[i], 0, 0)),
        sds((3, 2, 8, 128, WIDE)), [], 16, 1000, 18000000, tuple(pieces),
    )
    return out.reshape(3, D, WIDE)


def head_rows(rows):
    return jnp.concatenate([rows[:, HEAD * h : HEAD * (h + 1)] for h in range(4)], axis=0)


def head_columns(rows):
    return jnp.concatenate([rows[TOK * h : TOK * (h + 1)] for h in range(4)], axis=1)


def attend_kernel(query_place, key_slot, q_ref, k_ref, v_ref, w_ref, o_ref, part_ref, total):
    place = query_place[pl.program_id(0)]
    queries = head_rows(q_ref[...])

    def block(j, diagonal):
        at = pl.ds(pl.multiple_of(j * TOK, TOK), TOK)
        scores = dot_last(queries, k_ref[at, :])
        weights = 1.0 / (1.0 + jnp.exp2(SHIFT - scores * (SCORE * LOG2E)))
        if diagonal:
            row = lax.broadcasted_iota(jnp.int32, weights.shape, 0) & (TOK - 1)
            column = lax.broadcasted_iota(jnp.int32, weights.shape, 1)
            weights = jnp.where(column <= row, weights, 0.0)
        return dot(weights.astype(BF), v_ref[at, :])

    total[...] = block(key_slot[place], True)

    @pl.loop(0, place // 2)
    def _(p):
        total[...] += block(key_slot[2 * p], False) + block(key_slot[2 * p + 1], False)

    @pl.when(place % 2 == 1)
    def _():
        total[...] += block(key_slot[place - 1], False)

    out = head_columns(total[...]).astype(BF)
    o_ref[...] = out
    part_ref[...] = dot(out, w_ref[...]).astype(BF)


def attend(query_place, key_slot, q, k, v, w):
    rows = q.shape[0]
    whole = lambda i, *_: (0, 0)
    q_spec = pl.BlockSpec((TOK, QUERY), lambda i, *_: (i, 0))
    return call(
        attend_kernel, (query_place, key_slot), (rows // TOK,),
        [q_spec, pl.BlockSpec(k.shape, whole), pl.BlockSpec(v.shape, whole), pl.BlockSpec(w.shape, whole)],
        [q_spec, pl.BlockSpec((TOK, D), lambda i, *_: (i, 0))],
        [sds(q.shape), sds((rows, D))], [pltpu.VMEM((4 * TOK, HEAD), F32)],
        16, 6 * rows * 2048 * 256, 3 * MIB, (q, k, v, w),
    )


def attend_back_kernel(query_place, key_slot, q_ref, g_ref, k_ref, v_ref, kt_ref, dq_ref, dk_ref, dv_ref, total):
    step_at = pl.program_id(0)
    place = query_place[step_at]
    queries = head_rows(q_ref[...])
    grads = head_rows(g_ref[...])

    @pl.when(step_at == 0)
    def _():
        dk_ref[...] = jnp.zeros_like(dk_ref)
        dv_ref[...] = jnp.zeros_like(dv_ref)

    def block(j, diagonal):
        at = pl.ds(pl.multiple_of(j * TOK, TOK), TOK)
        scores = dot_last(k_ref[at, :], queries)
        sig = 1.0 / (1.0 + jnp.exp2(SHIFT - scores * (SCORE * LOG2E)))
        weights = sig
        if diagonal:
            row = lax.broadcasted_iota(jnp.int32, sig.shape, 1) & (TOK - 1)
            column = lax.broadcasted_iota(jnp.int32, sig.shape, 0)
            weights = jnp.where(column <= row, sig, 0.0)
        upstream = dot_last(v_ref[at, :], grads)
        score_grad = (upstream * weights * (1.0 - sig)).astype(BF)
        dk_ref[at, :] += dot(score_grad, queries)
        dv_ref[at, :] += dot(weights.astype(BF), grads)
        return dot(kt_ref[:, at], score_grad)

    total[...] = block(key_slot[place], True)

    @pl.loop(0, place // 2)
    def _(p):
        total[...] += block(key_slot[2 * p], False) + block(key_slot[2 * p + 1], False)

    @pl.when(place % 2 == 1)
    def _():
        total[...] += block(key_slot[place - 1], False)

    dq_ref[...] = head_columns((total[...] * SCORE).T).astype(BF)


def attend_back(query_place, key_slot, q, g, k, v):
    rows = q.shape[0]
    whole = lambda i, *_: (0, 0)
    rows_spec = pl.BlockSpec((TOK, QUERY), lambda i, *_: (i, 0))
    return call(
        attend_back_kernel, (query_place, key_slot), (rows // TOK,),
        [rows_spec, rows_spec, pl.BlockSpec(k.shape, whole), pl.BlockSpec(v.shape, whole), pl.BlockSpec((HEAD, k.shape[0]), whole)],
        [rows_spec, pl.BlockSpec(k.shape, whole), pl.BlockSpec(v.shape, whole)],
        [sds(q.shape), sds(k.shape, F32), sds(v.shape, F32)], [pltpu.VMEM((HEAD, 4 * TOK), F32)],
        16, 10 * 2048 * 2048 * 256, 4 * MIB, (q, g, k, v, k.T),
    )


SPLIT = 4
DEEP = D // SPLIT


def mlp_kernel(chunk, a_ref, b_ref, ga_ref, gb_ref, w_ref, *refs):
    refs = refs[-14:]
    z_ref, da_ref, dc_ref, grad_mine, grad_peer, out_mine, out_peer = refs[:7]
    weights, gate, up, back, gate_grad, up_grad, hidden = refs[7:]
    k = pl.program_id(0)

    @pl.when(k < SPLIT)
    def _():
        rows = jnp.concatenate([a_ref[...], b_ref[...]], axis=0)
        grads = jnp.concatenate([ga_ref[...], gb_ref[...]], axis=0)
        terms = (dot(rows, w_ref[0]), dot(rows, w_ref[1]), dot(grads, w_ref[2]))
        weights[k] = w_ref[...]

        @pl.when(k == 0)
        def _():
            for total, term in zip((gate, up, back), terms):
                total[...] = term

        @pl.when(k > 0)
        def _():
            for total, term in zip((gate, up, back), terms):
                total[...] += term

    @pl.when(k == SPLIT - 1)
    def _():
        a, c, dz = gate[...], up[...], back[...]
        sig = 1.0 / (1.0 + jnp.exp(-a))
        silu = a * sig
        hidden[...] = (silu * c).astype(BF)
        gate_grad[...] = (dz * c * sig * (1.0 + a * (1.0 - sig))).astype(BF)
        up_grad[...] = (dz * silu).astype(BF)
        z_ref[...] = hidden[...]
        da_ref[...] = gate_grad[...]
        dc_ref[...] = up_grad[...]

    @pl.when(k >= SPLIT)
    def _():
        j = k - SPLIT
        grad = dot_last(gate_grad[...], weights[j, 0]) + dot_last(up_grad[...], weights[j, 1])
        out = dot_last(hidden[...], weights[j, 2])
        grad_mine[...] = grad[:TOK].astype(BF)
        grad_peer[...] = grad[TOK:].astype(BF)
        out_mine[...] = out[:TOK].astype(BF)
        out_peer[...] = out[TOK:].astype(BF)


def mlp_group(group, chunk, own, peer, grads, weights, kept):
    deep = lambda k: jnp.minimum(k, SPLIT - 1)
    token_spec = pl.BlockSpec((TOK, DEEP), lambda k, chunk: (0, deep(k)))
    out_spec = pl.BlockSpec((TOK, DEEP), lambda k, chunk: (0, jnp.maximum(k - SPLIT, 0)))
    kept_spec = pl.BlockSpec((2 * TOK, WIDE), lambda k, chunk: (group, 0))
    args = (own, peer, grads, grads, weights)
    specs = [
        token_spec,
        token_spec,
        pl.BlockSpec((TOK, DEEP), lambda k, chunk: (chunk[2 * group], deep(k))),
        pl.BlockSpec((TOK, DEEP), lambda k, chunk: (chunk[2 * group + 1], deep(k))),
        pl.BlockSpec((3, DEEP, WIDE), lambda k, chunk: (0, deep(k), 0)),
    ]
    aliases = {}
    if kept is not None:
        args = args + tuple(kept)
        specs = specs + [pl.BlockSpec(memory_space=pl.ANY)] * 3
        aliases = {6: 0, 7: 1, 8: 2}
    wide = pltpu.VMEM((2 * TOK, WIDE), F32)
    narrow = pltpu.VMEM((2 * TOK, WIDE), BF)
    out = call(
        mlp_kernel, (chunk,), (2 * SPLIT,), specs, [kept_spec] * 3 + [out_spec] * 4,
        [sds((8 * TOK, WIDE))] * 3 + [sds((TOK, D))] * 4,
        [pltpu.VMEM((SPLIT, 3, DEEP, WIDE), BF), wide, wide, wide, narrow, narrow, narrow],
        40, 12 * 2 * TOK * D * WIDE, 14 * MIB, args, aliases,
    )
    return out[:3], out[3:]


def mlp_grads_kernel(column, xs, yhs, core, nat, *refs):
    tokens, (g_ref, da_ref, dc_ref, z_ref), outs, (turned, grads) = refs[:8], refs[8:12], refs[12:16], refs[16:]
    half = pl.program_id(0)
    rows = jnp.concatenate([ref[...] for ref in tokens], axis=0).T
    grads[0] = dot(rows, da_ref[...])
    grads[1] = dot(rows, dc_ref[...])
    for r in range(8):
        turned[:, TOK * r : TOK * (r + 1)] = g_ref[pl.ds(pl.multiple_of(nat[r] * TOK, TOK), TOK), :].T
    grads[2] = dot(turned[...], z_ref[...])
    for r in range(4):
        for pos in range(2):
            for rc in range(2):
                start = jnp.abs(core[0] - rc) * 128 + yhs[2 * half + pos] * 64 + xs[r] * 16
                for m in range(3):
                    outs[r][pos, 0, rc, m] = grads[m, at_rows(start, 16), :].astype(BF)


def mlp_grads(column, xs, yhs, core, nat, tokens, g, da, dc, z):
    col = lambda h, p, column, *_: (0, column[4 * h + p])
    whole = lambda h, p, *_: (0, 0)
    hidden = pl.BlockSpec((8 * TOK, WIDE), whole)
    out = pl.BlockSpec((2, 1, 2, 3, 16, WIDE), lambda h, p, *_: (h, p, 0, 0, 0, 0))
    return call(
        mlp_grads_kernel, (column, xs, yhs, core, nat), (2, 4),
        [pl.BlockSpec((TOK, 256), col)] * 8 + [pl.BlockSpec((8 * TOK, 256), col), hidden, hidden, hidden],
        [out] * 4, [sds((4, 4, 2, 3, 16, WIDE))] * 4,
        [pltpu.VMEM((256, 8 * TOK), BF), pltpu.VMEM((3, 256, WIDE), F32)],
        32, 6 * 8 * TOK * D * WIDE, 22 * MIB, tuple(tokens) + (g, da, dc, z),
    )


def attn_grads_kernel(column, xs, yhs, core, halves, h_ref, g_ref, o_ref, dqkv_ref, w_ref, *refs):
    outs, gain_ref, (first, second) = refs[:4], refs[4], refs[5:]
    half = pl.program_id(0)
    first[...] = dot(h_ref[...].T, dqkv_ref[...])
    second[...] = dot(o_ref[...].T, g_ref[...])
    gain = jnp.sum(first[...] * w_ref[...].astype(F32), axis=1, keepdims=True)
    gain_ref[0] = jnp.broadcast_to(gain, (256, 128)).T[:8]
    for r in range(4):
        for pos in range(2):
            inside = yhs[2 * half + pos] * 64 + xs[r] * 16
            for rc in range(2):
                start = jnp.abs(core[0] - rc) * 128 + inside
                outs[r][pos, 0, rc, :, :QUERY] = second[at_rows(inside, 16), QUERY * rc : QUERY * (rc + 1)].astype(BF)
                outs[r][pos, 0, rc, :, QUERY:] = first[at_rows(start, 16), :].astype(BF)


def attn_grads(column, xs, yhs, core, halves, h, g, o, dqkv, w):
    col = lambda i, p, column, *_: (0, column[4 * i + p])
    out = pl.BlockSpec((2, 1, 2, 16, PACK), lambda i, p, *_: (i, p, 0, 0, 0))
    *outs, gain = call(
        attn_grads_kernel, (column, xs, yhs, core, halves), (2, 4),
        [
            pl.BlockSpec((8 * TOK, 256), col),
            pl.BlockSpec((8 * TOK, 2 * QUERY), lambda i, p, *_: (0, p)),
            pl.BlockSpec((8 * TOK, 128), lambda i, p, column, xs, yhs, core, halves: (0, halves[i])),
            pl.BlockSpec((8 * TOK, QKV), lambda i, p, *_: (0, 0)),
            pl.BlockSpec((256, QKV), lambda i, p, column, *_: (column[4 * i + p], 0)),
        ],
        [out] * 4 + [pl.BlockSpec((1, 8, 256), lambda i, p, column, *_: (column[4 * i + p], 0, 0))],
        [sds((4, 4, 2, 16, PACK))] * 4 + [sds((8, 8, 256), F32)],
        [pltpu.VMEM((256, QKV), F32), pltpu.VMEM((128, 2 * QUERY), F32)],
        24, 2 * 8 * TOK * D * PACK, 12 * MIB, (h, g, o, dqkv, w),
    )
    return outs, gain[:, 0, :].reshape(D)


def finish_mlp_kernel(spots, xs, yhs, core, *refs):
    parts, (gate_ref, up_ref, down_ref), (rows,) = refs[:4], refs[4:7], refs[7:]
    first = core[0] == 0
    for m, out_ref in enumerate((gate_ref, up_ref, rows)):
        for r in range(4):
            for h in range(2):
                at = at_rows(yhs[h] * 64 + xs[r] * 16, 16)
                own = parts[r][h, 0, 0, m].astype(F32)
                other = parts[r][h, 1, 0, m].astype(F32)
                low, high = jnp.where(first, own, other), jnp.where(first, other, own)
                out_ref[at, :] = jnp.concatenate([low, high], axis=1)
    down_ref[...] = rows[...].T


def finish_mlp(spots, xs, yhs, core, parts):
    side = pl.BlockSpec((128, 2 * WIDE), lambda p, spots, *_: (0, spots[1 + p]))
    return call(
        finish_mlp_kernel, (spots, xs, yhs, core), (4,),
        [pl.BlockSpec((2, 2, 1, 3, 16, WIDE), lambda p, *_: (0, 0, p, 0, 0, 0))] * 4,
        [side, side, pl.BlockSpec((2 * WIDE, 128), lambda p, spots, *_: (spots[1 + p], 0))],
        [sds((128, FF), F32), sds((128, FF), F32), sds((FF, 128), F32)], [pltpu.VMEM((128, 2 * WIDE), F32)],
        24, 1000, 14 * MIB, tuple(parts),
    )


def finish_attn_kernel(spots, xs, yhs, core, *refs):
    parts, (q_ref, k_ref, v_ref, o_ref) = refs[:4], refs[4:]
    first = core[0] == 0
    for r in range(4):
        for h in range(2):
            at = at_rows(yhs[h] * 64 + xs[r] * 16, 16)
            keys, vals = [None] * KV_HEADS, [None] * KV_HEADS
            for p in range(4):
                chip = spots[1 + p]
                own = parts[r][h, 0, p].astype(F32)
                other = parts[r][h, 1, p].astype(F32)
                o_ref[at, QUERY * p : QUERY * (p + 1)] = own[:, :QUERY]
                o_ref[at, QUERY * (p + 4) : QUERY * (p + 5)] = other[:, :QUERY]
                low = jnp.where(first, own[:, QUERY:], other[:, QUERY:])
                high = jnp.where(first, other[:, QUERY:], own[:, QUERY:])
                q_ref[at, pl.ds(pl.multiple_of(chip * 2 * QUERY, 128), QUERY)] = low[:, :QUERY]
                q_ref[at, pl.ds(pl.multiple_of(chip * 2 * QUERY + QUERY, 128), QUERY)] = high[:, :QUERY]
                for j in range(KV_HEADS):
                    key, val = low[:, QUERY:], high[:, QUERY:]
                    keys[j] = key if p == 0 else jnp.where(chip == j, key, keys[j])
                    vals[j] = val if p == 0 else jnp.where(chip == j, val, vals[j])
            k_ref[at, :] = jnp.concatenate(keys, axis=1)
            v_ref[at, :] = jnp.concatenate(vals, axis=1)


def finish_attn(spots, xs, yhs, core, parts):
    whole = lambda i, *_: (0, 0)
    shapes = [(128, D), (128, KV_HEADS * HEAD), (128, KV_HEADS * HEAD), (128, D)]
    return call(
        finish_attn_kernel, (spots, xs, yhs, core), (1,),
        [pl.BlockSpec((2, 2, 4, 16, PACK), lambda i, *_: (0, 0, 0, 0, 0))] * 4,
        [pl.BlockSpec(shape, whole) for shape in shapes], [sds(shape, F32) for shape in shapes], [],
        16, 1000, 4 * MIB, tuple(parts),
    )


def on_device(
    tokens,
    cotangent,
    block_places,
    valid_counts,
    attn_gain,
    mlp_gain,
    query_weight,
    key_weight,
    value_weight,
    output_weight,
    gate_weight,
    up_weight,
    down_weight,
):
    replica = lax.axis_index("batch")
    member = lax.axis_index("blk")
    yh, x = replica // 4, replica % 4
    yl, z, c = member // 8, (member // 2) % 4, member % 2
    y = 2 * yh + yl
    s = 1 - 2 * c
    first_core = c == 0

    def table(*entries):
        return jnp.stack([jnp.asarray(entry, jnp.int32) for entry in entries])

    def around(coordinate):
        return [coordinate, (coordinate - s) % 4, (coordinate + s) % 4, (coordinate + 2) % 4]

    chips = around(z)
    core = table(c)
    xs = table(*around(x))
    spots = table(x, *chips)
    halves = table(yl, 1 - yl)
    slot = table(*[2 * chip + each for chip in chips for each in (c, 1 - c)])
    column = table(*[4 * half + chip for half in (yl, 1 - yl) for chip in chips])
    y_around = around(y)
    yhs = table(yh, 1 - yh, y_around[1] // 2, y_around[2] // 2)
    chunk = table(*[
        2 * chip + each
        for pair in ((0, 0), (1, 2), (2, 1), (3, 3))
        for chip, each in zip((chips[pair[0]], chips[pair[1]]), (c, 1 - c))
    ])


    def gather_tokens(rows):
        parts = []
        for part in ring_gather(rows, "z"):
            parts += [part, swap(part)]
        return parts

    def scatter_tokens(mine, peer):
        own, before, forward, far = [add(a, swap(b)) for a, b in zip(mine, peer)]
        got = [
            across(far.astype(BF), "z"),
            step(before.astype(BF), "z", -1),
            step(forward.astype(BF), "z", 1),
        ]
        return add(own, *got)

    def flip(rows):
        return jnp.flip(rows.reshape(-1, 2, TOK, rows.shape[-1]), axis=1).reshape(rows.shape)

    gain_one = attn_gain.astype(F32)
    gain_two = mlp_gain.astype(F32)
    rows_in = tokens[0].astype(F32)
    scale_attn = rms_scale(rows_in)


    def exchange(mine, other):
        got = swap(other)
        own = jnp.stack([mine[0], got[0]])
        before = jnp.stack([mine[1], got[2]])
        forward = jnp.stack([mine[2], got[1]])
        far = jnp.stack([mine[3], got[3]])
        parts = jnp.concatenate(exchange_z(own, before, forward, far))
        return parts

    def spread(part):
        pieces = ring_gather(part, "x")
        return list(pieces) + [step(piece, "y", 1) for piece in pieces]

    out_rows = lax.dynamic_slice_in_dim(output_weight, x * 32, 32, axis=0)
    out_part = send(
        out_rows.reshape(32, 8, QUERY).transpose(1, 0, 2),
        lambda yh, x, yl, z, c: (yh, x, c, 2 * yl + z // 2, z % 2),
    )
    attn_part = exchange(*pack_attn(spots, core, query_weight, key_weight, value_weight))
    attn_part = jnp.concatenate([out_part, attn_part], axis=-1)
    attn_pieces = spread(attn_part)
    w_qkv, w_out = place_attn(slot, xs, halves, attn_pieces)

    normed_parts = gather_tokens((rows_in * scale_attn * gain_one).astype(BF))
    normed_attn = jnp.concatenate(normed_parts)

    mlp_mine, mlp_other = pack_mlp(spots, core, gate_weight, up_weight, down_weight)
    mlp_part = exchange(mlp_mine, after(mlp_other, attn_part))
    w_mlp = place_mlp(slot, xs, halves, spread(after(mlp_part, attn_pieces[3])))

    grad_rows = lax.all_gather(
        after(cotangent[0], normed_parts[6]), "blk", axis=0, tiled=True,
        axis_index_groups=[list(range(8)), list(range(8, 16))],
    )


    places = block_places[0]
    counts = valid_counts[0]
    key_block = jnp.concatenate([yl * 8 + chunk, (1 - yl) * 8 + chunk])
    key_place = lookup(places, key_block)
    query_place = key_place[:8]
    key_count = lookup(counts, key_block)
    slots = jnp.arange(16, dtype=jnp.int32)
    key_slot = jnp.sum(jnp.where(key_place[None, :] == slots[:, None], slots[None, :], 0), axis=1)
    usable = (jnp.arange(TOK, dtype=jnp.int32)[None, :] < key_count[:, None]).reshape(16 * TOK, 1)

    projected = dot(normed_attn, w_qkv).astype(BF)
    queries, kv_own = projected[:, :QUERY], projected[:, QUERY:]
    kv_mine = jnp.concatenate([kv_own, to_half(kv_own)], axis=0)
    kv_other = flip(swap(kv_mine))
    keys = jnp.where(first_core, kv_mine, kv_other)
    values = jnp.where(usable, jnp.where(first_core, kv_other, kv_mine), 0)
    attended, mine, peer = [None] * 4, [None] * 4, [None] * 4
    for g in (3, 1, 2, 0):
        rows = slice(2 * TOK * g, 2 * TOK * (g + 1))
        attended[g], part = attend(query_place[2 * g : 2 * g + 2], key_slot, queries[rows], keys, values, w_out)
        mine[g], peer[g] = part[:TOK], part[TOK:]
    attn_rows = jnp.concatenate(attended)
    residual = rows_in + scatter_tokens(mine, peer)
    scale_mlp = rms_scale(residual)
    mlp_parts = gather_tokens((residual * scale_mlp * gain_two).astype(BF))


    kept, results = None, []
    for g in range(4):
        kept, result = mlp_group(g, chunk, mlp_parts[2 * g], mlp_parts[2 * g + 1], grad_rows, w_mlp, kept)
        results.append(result)
    hidden, gate_grad_rows, up_grad_rows = kept
    grad_mine, grad_peer, out_mine, out_peer = zip(*results)
    normed_grad = scatter_tokens(grad_mine, grad_peer)
    residual_grad = cotangent[0].astype(F32) + norm_back(residual, scale_mlp, gain_two, normed_grad)
    mlp_gain_part = jnp.sum(normed_grad * residual * scale_mlp, axis=0)
    branch_parts = gather_tokens(residual_grad.astype(BF))
    branch_grad = jnp.concatenate(branch_parts)
    layer_out = (residual + scatter_tokens(out_mine, out_peer)).astype(BF)[None]


    def reduce_planes(outs):
        got = ring_scatter(*outs, "x").astype(BF)
        return ring_scatter(got[0], got[2], got[3], got[1], "y").astype(BF)

    def resplit_back(part):
        got = exchange_z(part[0], part[1], part[2], part[3])
        mine = jnp.stack([each[0] for each in got])
        other = swap(jnp.stack([got[p][1] for p in (0, 2, 1, 3)]))
        return jnp.stack([mine, other])

    def gather_batch(part):
        return ring_gather(jnp.stack([part, across(part, "y")]), "x")

    mlp_sums = mlp_grads(
        column, xs, yhs, core, chunk, mlp_parts, grad_rows, gate_grad_rows, up_grad_rows, hidden
    )
    mlp_sums = gather_batch(resplit_back(reduce_planes(mlp_sums)))
    gate_grad, up_grad, down_grad = finish_mlp(spots, xs, yhs, core, mlp_sums)


    attn_grad = dot_last(branch_grad, w_out).astype(BF)
    query_grad_rows, key_terms, value_terms = attend_back(
        query_place, key_slot, queries, attn_grad, keys, values
    )
    key_terms = (key_terms * SCORE).astype(BF)
    value_terms = jnp.where(usable, value_terms, 0.0).astype(BF)
    kv_keep = jnp.where(first_core, key_terms, value_terms)
    kv_give = flip(swap(jnp.where(first_core, value_terms, key_terms)))
    kv_terms = add(kv_keep, kv_give)
    half_rows = 8 * TOK
    kv_grad_rows = add(kv_terms[:half_rows], to_half(kv_terms[half_rows:].astype(BF))).astype(BF)
    qkv_grad_rows = jnp.concatenate([query_grad_rows, kv_grad_rows], axis=1)

    attn_sums, attn_gain_part = attn_grads(
        column, xs, yhs, core, halves, normed_attn, branch_grad, attn_rows, qkv_grad_rows, w_qkv
    )
    gain_grads = jnp.stack([attn_gain_part / gain_one, mlp_gain_part])
    for axis in ("blk", "batch"):
        gain_grads = jnp.sum(lax.all_gather(gain_grads, axis), axis=0)
    attn_sums = reduce_planes(attn_sums)
    out_sums = send(
        attn_sums[..., :QUERY], lambda yh, x, yl, z, c: (yh, x, z // 2, 2 * (z % 2) + c, yl)
    )
    qkv_sums = resplit_back(attn_sums[..., QUERY:])
    attn_sums = jnp.concatenate([out_sums.reshape(2, 4, 16, QUERY), qkv_sums], axis=-1)
    query_grad, key_grad, value_grad, output_grad = finish_attn(spots, xs, yhs, core, gather_batch(attn_sums))

    attn_partial = dot_last(qkv_grad_rows, w_qkv).astype(BF).reshape(4, 2, TOK, D)
    normed_attn_grad = scatter_tokens(attn_partial[:, 0], attn_partial[:, 1])
    tokens_grad = (
        residual_grad + norm_back(rows_in, scale_attn, gain_one, normed_attn_grad)
    ).astype(BF)[None]
    return (
        layer_out,
        tokens_grad,
        gain_grads[0],
        gain_grads[1],
        query_grad,
        key_grad,
        value_grad,
        output_grad,
        gate_grad,
        up_grad,
        down_grad,
    )


def solution(mesh):
    in_specs = (
        P("batch", "blk", None),
        P("batch", "blk", None),
        P("batch", None),
        P("batch", None),
        P(),
        P(),
        P("blk", None),
        P("blk", None),
        P("blk", None),
        P("blk", None),
        P("blk", None),
        P("blk", None),
        P(None, "blk"),
    )
    out_specs = (
        P("batch", "blk", None),
        P("batch", "blk", None),
        P(),
        P(),
        P("blk", None),
        P("blk", None),
        P("blk", None),
        P("blk", None),
        P("blk", None),
        P("blk", None),
        P(None, "blk"),
    )
    return jax.shard_map(
        on_device, mesh=mesh, in_specs=in_specs, out_specs=out_specs, check_vma=False
    )
```

time: 871 us -> 673 us (0.77)
  local copies, waits for them, and re-layouts: 180 us -> 62.6 us
  matrix products: 98 us -> 10.2 us
  Pallas kernels: 58.7 us -> 134 us
  waiting for transfers between devices: 253 us -> 197 us
  other arithmetic: 82.6 us -> 41 us
  starting transfers between devices: 121 us -> 147 us
  between operations: 3.47 us -> 16.2 us
  blocking collectives: 64 us -> 54.4 us
    pallas_call x2 -> x17, Pallas kernels: 58.7 us -> 134 us  [call(): pl.pallas_call(body, grid_spec=pltpu.PrefetchScalarGridSpec(num_scalar_pr...]
    psum x1 -> x0, blocking collectives: 64 us -> none  [on_device(): lax.psum((attn_gain_part, mlp_gain_part), BOTH)]
    ppermute x133 -> x105, waiting for transfers between devices: 253 us -> 197 us  [send(): return lax.ppermute(value, BOTH, pairs)]
    all_gather x0 -> x2, blocking collectives: none -> 54.4 us  [on_device(): gain_grads = jnp.sum(lax.all_gather(gain_grads, axis), axis=0)]
    slice x22 -> x23, local copies, waits for them, and re-layouts: 40.1 us -> 5.58 us  [the longest x4 2.14 us: exchange(): far = jnp.stack([mine[3], got[3]])]
    dot_general x6 -> x2, matrix products: 38.6 us -> 5.68 us  [dot_last(): lax.dot_general(left, right, (((1,), (1,)), ((), ())), preferred_element_...]
    dot_general x6 -> x1, matrix products: 32 us -> 4.5 us  [dot(): return jnp.dot(left, right, preferred_element_type=F32)]
    dot_general x6 -> x0, matrix products: 27.3 us -> none  [dot_first(): lax.dot_general(left, right, (((0,), (0,)), ((), ())), preferred_element_...]
  transfers between devices with their start and end apart: 133 -> 106, of which waited for: 49 -> 40; matrix products, arithmetic and copies ran while one was open for 31% -> 12% of each run, Pallas kernels for 7% -> 20%
where the time goes in v2:
time: 673 us; the launch traced here: 662 us
  waiting for transfers between devices  197 us (29%)
  starting transfers between devices  147 us (22%)
  Pallas kernels  134 us (20%)
  local copies, waits for them, and re-layouts  62.6 us (9%)
  blocking collectives  54.4 us (8%)
  other arithmetic  41 us (6%)
  between operations  16.2 us (2%)
  matrix products  10.2 us (2%)
    ppermute x105, waiting for transfers between devices, send(): return lax.ppermute(value, BOTH, pairs)  197 us
    ppermute x105, starting transfers between devices, send(): return lax.ppermute(value, BOTH, pairs)  147 us
    pallas_call x17, Pallas kernels, call(): pl.pallas_call(body, grid_spec=pltpu.PrefetchScalarGridSpec(num_scalar_pr...  134 us
    all_gather x2, blocking collectives, on_device(): gain_grads = jnp.sum(lax.all_gather(gain_grads, axis), axis=0)  54.4 us
    unnamed x182, local copies, waits for them, and re-layouts  43.7 us
  transfers between devices with their start and end apart: 106, of which 40 were waited for; matrix products, arithmetic and copies ran while one was open for 12% of the time, Pallas kernels for 20%

profile of v2, /device:TPU:24, one launch (start us, length us, event | category | flops | bytes accessed | tf_op | source)
XLA Modules:
  0.0 661.9 jit_solution(17649602878857151584)
XLA Ops:
  16.9 4.0 collective-permute-start.7
  41.5 4.3 collective-permute-done.11
  50.5 4.5 collective-permute-done.13.refs_2_
  92.3 4.5 convolution_convert_fusion.1
  100.9 4.7 collective-permute-done.19
  106.8 3.9 collective-permute-start.33
  117.2 5.2 shard_map.217
  123.4 7.8 %shard_map.216 = (bf16[256,256]{1,0:T(8,128)(2,1)S(1)}, bf16[256,2048]{1,0:T(8,128)(2,1)S(1)}) custom-call(s32[2]{0:T(128)S(1)} %copy-done.51, s32[16]{0:T(128)S(1)} %copy-done.59, bf16[256,256]{1,0:T(8,128)(2,1)S(1)} %get-tuple-element.165.q_ref, bf16[2048,64]{1,0:T(8,128)(2,1)S(1)} %get-tuple-element.162.k_ref, ...), custom_call_target="tpu_custom_call" | custom-call | flops 805306368 | bytes 3145728 | tf_op jit(solution)/shard_map/pallas_call | solution.py:135
  135.6 4.2 shard_map.214
  140.1 9.3 %collective-permute-start.35 = (bf16[8,3,32,704]{3,2,1,0:T(8,128)(2,1)S(1)}, bf16[8,3,32,704]{3,2,1,0:T(8,128)(2,1)S(1)}, u32[]{:S(2)}, u32[]{:S(2)}) collective-permute-start(bf16[8,3,32,704]{3,2,1,0:T(8,128)(2,1)S(1)} %collective-permute-done.33.refs_1_), channel_id=1, source_target_pairs={{0,16},{1,49},{2,18},{3,51},{4,20},{5,53},{6,22},{7,55},{8,24},{9,... | collective-permute-start | bytes 3244040 | tf_op jit(solution)/shard_map/ppermute | solution.py:38
  155.8 8.5 %collective-permute-done.27 = bf16[128,2048]{1,0:T(8,128)(2,1)S(1)} collective-permute-done((bf16[128,2048]{1,0:T(8,128)(2,1)S(1)}, bf16[128,2048]{1,0:T(8,128)(2,1)S(1)}, u32[]{:S(2)}, u32[]{:S(2)}) %collective-permute-start.27) | collective-permute-done | bytes 524320 | tf_op jit(solution)/shard_map/ppermute | solution.py:38
  164.4 6.6 collective-permute-done.25
  171.0 4.8 collective-permute-start.38
  180.6 10.4 %collective-permute-done.41.a_ref.refs_2_ = bf16[128,2048]{1,0:T(8,128)(2,1)} collective-permute-done((bf16[128,2048]{1,0:T(8,128)(2,1)S(1)}, bf16[128,2048]{1,0:T(8,128)(2,1)}, u32[]{:S(2)}, u32[]{:S(2)}) %collective-permute-start.41) | collective-permute-done | bytes 524320 | tf_op jit(solution)/shard_map/ppermute | solution.py:38
  191.1 4.9 collective-permute-done.38.refs_6_
  196.6 5.2 collective-permute-done.42.a_ref.refs_6_
  201.7 6.9 %collective-permute-done.39.refs_7_ = bf16[8,3,32,704]{3,2,1,0:T(8,128)(2,1)S(1)} collective-permute-done((bf16[8,3,32,704]{3,2,1,0:T(8,128)(2,1)S(1)}, bf16[8,3,32,704]{3,2,1,0:T(8,128)(2,1)S(1)}, u32[]{:S(2)}, u32[]{:S(2)}) %collective-permute-start.39) | collective-permute-done | bytes 1081376 | tf_op jit(solution)/shard_map/ppermute | solution.py:38
  210.6 3.6 copy-done.5
  219.2 12.4 %shard_map.220 = (bf16[1024,704]{1,0:T(8,128)(2,1)S(1)}, bf16[1024,704]{1,0:T(8,128)(2,1)S(1)}, bf16[1024,704]{1,0:T(8,128)(2,1)S(1)}, bf16[128,2048]{1,0:T(8,12...) custom-call(s32[8]{0:T(128)S(1)} %stack.206.chunk.nat, ...), custom_call_target="tpu_custom_call" | custom-call | flops 4429185024 | bytes 14680064 | tf_op jit(solution)/shard_map/pallas_call | solution.py:135
  232.3 12.4 %shard_map.221 = (bf16[1024,704]{1,0:T(8,128)(2,1)S(1)}, bf16[1024,704]{1,0:T(8,128)(2,1)S(1)}, bf16[1024,704]{1,0:T(8,128)(2,1)S(1)}, bf16[128,2048]{1,0:T(8,12...) custom-call(s32[8]{0:T(128)S(1)} %stack.206.chunk.nat, ...), custom_call_target="tpu_custom_call", output_to_operand_aliasing={{0}: (6, {}), {1}: (7, {}), {2}: (8, {})} | custom-call | flops 4429185024 | bytes 14680064 | tf_op jit(solution)/shard_map/pallas_call | solution.py:135
  245.6 12.4 %shard_map.222 = (bf16[1024,704]{1,0:T(8,128)(2,1)S(1)}, bf16[1024,704]{1,0:T(8,128)(2,1)S(1)}, bf16[1024,704]{1,0:T(8,128)(2,1)S(1)}, bf16[128,2048]{1,0:T(8,12...) custom-call(s32[8]{0:T(128)S(1)} %stack.206.chunk.nat, ...), custom_call_target="tpu_custom_call", output_to_operand_aliasing={{0}: (6, {}), {1}: (7, {}), {2}: (8, {})} | custom-call | flops 4429185024 | bytes 14680064 | tf_op jit(solution)/shard_map/pallas_call | solution.py:135
  258.0 12.4 %shard_map.223 = (bf16[1024,704]{1,0:T(8,128)(2,1)S(1)}, bf16[1024,704]{1,0:T(8,128)(2,1)S(1)}, bf16[1024,704]{1,0:T(8,128)(2,1)S(1)}, bf16[128,2048]{1,0:T(8,12...) custom-call(s32[8]{0:T(128)S(1)} %stack.206.chunk.nat, ...), custom_call_target="tpu_custom_call", output_to_operand_aliasing={{0}: (6, {}), {1}: (7, {}), {2}: (8, {})} | custom-call | flops 4429185024 | bytes 14680064 | tf_op jit(solution)/shard_map/pallas_call | solution.py:135
  273.9 9.4 %collective-permute-start.57 = (bf16[128,2048]{1,0:T(8,128)(2,1)S(1)}, bf16[128,2048]{1,0:T(8,128)(2,1)S(1)}, u32[]{:S(2)}, u32[]{:S(2)}) collective-permute-start(bf16[128,2048]{1,0:T(8,128)(2,1)S(1)} %add_convert_fusion.5), channel_id=1, source_target_pairs={{0,6},{1,3},{2,0},{3,5},{4,2},{5,7},{6,4},{7,1},{8,14},{9,11},{10,... | collective-permute-start | bytes 1572872 | tf_op jit(solution)/shard_map/ppermute | solution.py:38
  289.6 4.8 collective-permute-start.59
  294.4 16.0 %collective-permute-done.57 = bf16[128,2048]{1,0:T(8,128)(2,1)S(1)} collective-permute-done((bf16[128,2048]{1,0:T(8,128)(2,1)S(1)}, bf16[128,2048]{1,0:T(8,128)(2,1)S(1)}, u32[]{:S(2)}, u32[]{:S(2)}) %collective-permute-start.57) | collective-permute-done | bytes 524320 | tf_op jit(solution)/shard_map/ppermute | solution.py:38
  311.2 7.7 %collective-permute-done.52 = bf16[128,2048]{1,0:T(8,128)(2,1)S(1)} collective-permute-done((bf16[128,2048]{1,0:T(8,128)(2,1)S(1)}, bf16[128,2048]{1,0:T(8,128)(2,1)S(1)}, u32[]{:S(2)}, u32[]{:S(2)}) %collective-permute-start.52) | collective-permute-done | bytes 524320 | tf_op jit(solution)/shard_map/ppermute | solution.py:38
  318.9 6.3 collective-permute-done.59
  350.3 17.3 %shard_map.227 = (bf16[4,4,2,3,16,704]{5,4,3,2,1,0:T(8,128)(2,1)S(1)}, bf16[4,4,2,3,16,704]{5,4,3,2,1,0:T(8,128)(2,1)}, bf16[4,4,2,3,16,704]{5,4,3,2,1,0:T(8,128)(2,1)S(1)}, bf16[4,4,2,3,16,704]{5,4,3,2,1,0:T(8,128)(2,1)}) custom-call(s32[8]{0:T(128)S(1)} %copy-done.47, s32[4]{0:T(128)S(1)} %pad_add_fusion.1.xs, s32[4]{0:T(128)S(1)} %copy-done.41, ...), custom_call_target="tpu_custom_call" | custom-call | flops 8858370048 | bytes 23068672 | tf_op jit(solution)/shard_map/pallas_call | solution.py:135
  367.7 4.6 collective-permute-start.92
  378.8 24.9 %shard_map.224 = (bf16[1024,256]{1,0:T(8,128)(2,1)S(1)}, f32[2048,64]{1,0:T(8,128)S(1)}, f32[2048,64]{1,0:T(8,128)S(1)}) custom-call(s32[8]{0:T(128)S(1)} %bitcast.188, s32[16]{0:T(128)S(1)} %copy-done.60, bf16[1024,256]{1,0:T(8,128)(2,1)S(1)} %copy-done.30, bf16[1024,256]{1,0:T(8,128)(2,1)S(1)} %convolution_convert_fusion.2.g_ref, ...), custom_call_target="tpu_custom_call" | custom-call | flops 10737418240 | bytes 4194304 | tf_op jit(solution)/shard_map/pallas_call | solution.py:135
  404.7 4.1 collective-permute-start.91
  413.1 5.9 collective-permute-start.68
  419.0 4.0 add_convert_fusion.1
  425.5 8.6 %shard_map.225 = (bf16[4,4,2,16,576]{4,3,2,1,0:T(8,128)(2,1)S(1)}, bf16[4,4,2,16,576]{4,3,2,1,0:T(8,128)(2,1)S(1)}, bf16[4,4,2,16,576]{4,3,2,1,0:T(8,128)(2,1)S(...) custom-call(s32[8]{0:T(128)S(1)} %copy-done.48, s32[4]{0:T(128)S(1)} %pad_add_fusion.1.xs, s32[4]{0:T(128)S(1)} %copy-done.42, ...), custom_call_target="tpu_custom_call" | custom-call | flops 2415919104 | bytes 12582912 | tf_op jit(solution)/shard_map/pallas_call | solution.py:135
  437.9 4.4 convolution_convert_fusion
  442.3 20.1 %all-gather.2 = f32[16,2,2048]{2,1,0:T(2,128)S(1)} all-gather(f32[1,2,2048]{2,1,0:T(2,128)S(1)} %maximum_bitcast_fusion.2), channel_id=2, replica_groups=mesh['batch'=8,'blk'=16] {'blk'}, dimensions={0}, use_global_device_ids=true | all-gather | bytes 278528 | tf_op jit(solution)/shard_map/all_gather | solution.py:746
  465.5 14.4 %collective-permute-done.77 = bf16[4,4,2,16,576]{4,3,2,1,0:T(8,128)(2,1)S(1)} collective-permute-done((bf16[4,4,2,16,576]{4,3,2,1,0:T(8,128)(2,1)}, bf16[4,4,2,16,576]{4,3,2,1,0:T(8,128)(2,1)S(1)}, u32[]{:S(2)}, u32[]{:S(2)}) %collective-permute-start.77) | collective-permute-done | bytes 589856 | tf_op jit(solution)/shard_map/ppermute | solution.py:38
  491.4 34.3 %all-gather.3 = f32[8,2,2048]{2,1,0:T(2,128)S(1)} all-gather(f32[1,2,2048]{2,1,0:T(2,128)S(1)} %bitcast.205), channel_id=3, replica_groups=mesh['batch'=8,'blk'=16] {'batch'}, dimensions={0}, use_global_device_ids=true | all-gather | bytes 147456 | tf_op jit(solution)/shard_map/all_gather | solution.py:746
  536.7 8.6 %collective-permute-done.94 = bf16[4,2,3,16,704]{4,3,2,1,0:T(8,128)(2,1)S(1)} collective-permute-done((bf16[4,2,3,16,704]{4,3,2,1,0:T(8,128)(2,1)S(1)}, bf16[4,2,3,16,704]{4,3,2,1,0:T(8,128)(2,1)S(1)}, u32[]{:S(2)}, u32[]{:S(2)}) %collective-permute-start.94) | collective-permute-done | bytes 540704 | tf_op jit(solution)/shard_map/ppermute | solution.py:38
  556.2 5.9 collective-permute-done.99
  562.1 6.3 collective-permute-done.97
  576.4 10.9 %collective-permute-done.101 = bf16[2,4,3,16,704]{4,3,2,1,0:T(8,128)(2,1)S(1)} collective-permute-done((bf16[2,4,3,16,704]{4,3,2,1,0:T(8,128)(2,1)S(1)}, bf16[2,4,3,16,704]{4,3,2,1,0:T(8,128)(2,1)S(1)}, u32[]{:S(2)}, u32[]{:S(2)}) %collective-permute-start.101) | collective-permute-done | bytes 540704 | tf_op jit(solution)/shard_map/ppermute | solution.py:38
  596.3 3.6 collective-permute-start.87
  600.5 3.5 collective-permute-done.87
  607.1 4.7 collective-permute-start.88
  614.6 24.8 %collective-permute-done.88.refs_1_ = bf16[2,2,4,16,576]{4,3,2,1,0:T(8,128)(2,1)S(1)} collective-permute-done((bf16[2,2,4,16,576]{4,3,2,1,0:T(8,128)(2,1)S(1)}, bf16[2,2,4,16,576]{4,3,2,1,0:T(8,128)(2,1)S(1)}, u32[]{:S(2)}, u32[]{:S(2)}) %collective-permute-start.88) | collective-permute-done | bytes 294944 | tf_op jit(solution)/shard_map/ppermute | solution.py:38
  642.0 5.7 collective-permute-done.90.refs_3_
  649.8 4.8 shard_map.228
  (477 shorter events, 227.2 us)
Async XLA Ops:
  7.2 207.8 %all-gather.6.cloned.1.call-start = ((), (), s32[]{:S(2)}) async-start(), calls=%async_computation | async-start | bytes 4718592 | tf_op jit(solution)/shard_map/all_gather | solution.py:661
  12.6 47.4 %collective-permute-start.1 = (bf16[128,2048]{1,0:T(8,128)(2,1)}, bf16[128,2048]{1,0:T(8,128)(2,1)}, u32[]{:S(2)}, u32[]{:S(2)}) collective-permute-start(bf16[128,2048]{1,0:T(8,128)(2,1)} %get-tuple-element.150), channel_id=1, source_target_pairs={{0,2},{1,7},{2,4},{3,1},{4,6},{5,3},{6,0},{7,5},{8,10},{9,15},{10,... | collective-permute-start | bytes 1572872 | tf_op jit(solution)/shard_map/ppermute | solution.py:38
  14.5 42.1 %collective-permute-start = (bf16[128,2048]{1,0:T(8,128)(2,1)}, bf16[128,2048]{1,0:T(8,128)(2,1)}, u32[]{:S(2)}, u32[]{:S(2)}) collective-permute-start(bf16[128,2048]{1,0:T(8,128)(2,1)} %get-tuple-element.150), channel_id=1, source_target_pairs={{0,1},{1,0},{2,3},{3,2},{4,5},{5,4},{6,7},{7,6},{8,9},{9,8},{10,11... | collective-permute-start | bytes 1572872 | tf_op jit(solution)/shard_map/ppermute | solution.py:38
  16.9 29.5 %collective-permute-start.7 = (bf16[8,32,256]{2,1,0:T(8,128)(2,1)}, bf16[8,32,256]{2,1,0:T(8,128)(2,1)}, u32[]{:S(2)}, u32[]{:S(2)}) collective-permute-start(bf16[8,32,256]{2,1,0:T(8,128)(2,1)} %bitcast.178), channel_id=1, source_target_pairs={{0,0},{1,8},{2,1},{3,9},{4,2},{5,10},{6,3},{7,11},{8,4},{9,12},{10... | collective-permute-start | bytes 393224 | tf_op jit(solution)/shard_map/ppermute | solution.py:38
  63.7 19.5 %collective-permute-start.5 = (bf16[128,2048]{1,0:T(8,128)(2,1)}, bf16[128,2048]{1,0:T(8,128)(2,1)}, u32[]{:S(2)}, u32[]{:S(2)}) collective-permute-start(bf16[128,2048]{1,0:T(8,128)(2,1)} %collective-permute-done.1), channel_id=1, source_target_pairs={{0,2},{1,7},{2,4},{3,1},{4,6},{5,3},{6,0},{7,5},{8,10},{9,15},{10,... | collective-permute-start | bytes 1572872 | tf_op jit(solution)/shard_map/ppermute | solution.py:38
  74.5 24.4 %collective-permute-start.30 = (bf16[2,3,32,704]{3,2,1,0:T(8,128)(2,1)}, bf16[2,3,32,704]{3,2,1,0:T(8,128)(2,1)}, u32[]{:S(2)}, u32[]{:S(2)}) collective-permute-start(bf16[2,3,32,704]{3,2,1,0:T(8,128)(2,1)} %pad_maximum_fusion.7), channel_id=1, source_target_pairs={{0,2},{1,7},{2,4},{3,1},{4,6},{5,3},{6,0},{7,5},{8,10},{9,15},{10,... | collective-permute-start | bytes 811016 | tf_op jit(solution)/shard_map/ppermute | solution.py:38
  78.0 21.9 %collective-permute-start.31 = (bf16[2,3,32,704]{3,2,1,0:T(8,128)(2,1)}, bf16[2,3,32,704]{3,2,1,0:T(8,128)(2,1)}, u32[]{:S(2)}, u32[]{:S(2)}) collective-permute-start(bf16[2,3,32,704]{3,2,1,0:T(8,128)(2,1)} %pad_maximum_fusion.8), channel_id=1, source_target_pairs={{0,6},{1,3},{2,0},{3,5},{4,2},{5,7},{6,4},{7,1},{8,14},{9,11},{10,... | collective-permute-start | bytes 811016 | tf_op jit(solution)/shard_map/ppermute | solution.py:38
  83.3 22.6 %collective-permute-start.32 = (bf16[2,3,32,704]{3,2,1,0:T(8,128)(2,1)}, bf16[2,3,32,704]{3,2,1,0:T(8,128)(2,1)}, u32[]{:S(2)}, u32[]{:S(2)}) collective-permute-start(bf16[2,3,32,704]{3,2,1,0:T(8,128)(2,1)} %pad_maximum_fusion.9), channel_id=1, source_target_pairs={{0,4},{1,5},{2,6},{3,7},{4,0},{5,1},{6,2},{7,3},{8,12},{9,13},{10,... | collective-permute-start | bytes 811016 | tf_op jit(solution)/shard_map/ppermute | solution.py:38
  106.8 33.0 %collective-permute-start.33 = (bf16[8,3,32,704]{3,2,1,0:T(8,128)(2,1)S(1)}, bf16[8,3,32,704]{3,2,1,0:T(8,128)(2,1)S(1)}, u32[]{:S(2)}, u32[]{:S(2)}) collective-permute-start(bf16[8,3,32,704]{3,2,1,0:T(8,128)(2,1)S(1)} %constant_dynamic-update-slice_fusion.13.refs_0_), channel_id=1, source_target_pairs={{0,16},{1,49},{2,18},{3,51},{4,20},{5,53},{6,22},{7,55},{8,24},{9,... | collective-permute-start | bytes 3244040 | tf_op jit(solution)/shard_map/ppermute | solution.py:38
  123.4 29.8 %collective-permute-start.34 = (bf16[8,3,32,704]{3,2,1,0:T(8,128)(2,1)S(1)}, bf16[8,3,32,704]{3,2,1,0:T(8,128)(2,1)S(1)}, u32[]{:S(2)}, u32[]{:S(2)}) collective-permute-start(bf16[8,3,32,704]{3,2,1,0:T(8,128)(2,1)S(1)} %constant_dynamic-update-slice_fusion.13.refs_0_), channel_id=1, source_target_pairs={{0,48},{1,17},{2,50},{3,19},{4,52},{5,21},{6,54},{7,23},{8,56},{9,... | collective-permute-start | bytes 3244040 | tf_op jit(solution)/shard_map/ppermute | solution.py:38
  140.1 36.4 %collective-permute-start.35 = (bf16[8,3,32,704]{3,2,1,0:T(8,128)(2,1)S(1)}, bf16[8,3,32,704]{3,2,1,0:T(8,128)(2,1)S(1)}, u32[]{:S(2)}, u32[]{:S(2)}) collective-permute-start(bf16[8,3,32,704]{3,2,1,0:T(8,128)(2,1)S(1)} %collective-permute-done.33.refs_1_), channel_id=1, source_target_pairs={{0,16},{1,49},{2,18},{3,51},{4,20},{5,53},{6,22},{7,55},{8,24},{9,... | collective-permute-start | bytes 3244040 | tf_op jit(solution)/shard_map/ppermute | solution.py:38
  149.7 21.3 %collective-permute-start.25 = (bf16[128,2048]{1,0:T(8,128)(2,1)S(1)}, bf16[128,2048]{1,0:T(8,128)(2,1)S(1)}, u32[]{:S(2)}, u32[]{:S(2)}) collective-permute-start(bf16[128,2048]{1,0:T(8,128)(2,1)S(1)} %add_convert_fusion.12), channel_id=1, source_target_pairs={{0,6},{1,3},{2,0},{3,5},{4,2},{5,7},{6,4},{7,1},{8,14},{9,11},{10,... | collective-permute-start | bytes 1572872 | tf_op jit(solution)/shard_map/ppermute | solution.py:38
  153.2 22.6 %collective-permute-start.23 = (bf16[128,2048]{1,0:T(8,128)(2,1)S(1)}, bf16[128,2048]{1,0:T(8,128)(2,1)S(1)}, u32[]{:S(2)}, u32[]{:S(2)}) collective-permute-start(bf16[128,2048]{1,0:T(8,128)(2,1)S(1)} %add_convert_fusion.13), channel_id=1, source_target_pairs={{0,4},{1,5},{2,6},{3,7},{4,0},{5,1},{6,2},{7,3},{8,12},{9,13},{10,... | collective-permute-start | bytes 1572872 | tf_op jit(solution)/shard_map/ppermute | solution.py:38
  154.4 24.7 %collective-permute-start.36 = (bf16[8,3,32,704]{3,2,1,0:T(8,128)(2,1)S(1)}, bf16[8,3,32,704]{3,2,1,0:T(8,128)(2,1)S(1)}, u32[]{:S(2)}, u32[]{:S(2)}) collective-permute-start(bf16[8,3,32,704]{3,2,1,0:T(8,128)(2,1)S(1)} %constant_dynamic-update-slice_fusion.13.refs_0_), channel_id=1, source_target_pairs={{0,8},{1,73},{2,10},{3,75},{4,12},{5,77},{6,14},{7,79},{8,64},{9,1... | collective-permute-start | bytes 3244040 | tf_op jit(solution)/shard_map/ppermute | solution.py:38
  164.4 31.6 %collective-permute-start.37 = (bf16[8,3,32,704]{3,2,1,0:T(8,128)(2,1)S(1)}, bf16[8,3,32,704]{3,2,1,0:T(8,128)(2,1)S(1)}, u32[]{:S(2)}, u32[]{:S(2)}) collective-permute-start(bf16[8,3,32,704]{3,2,1,0:T(8,128)(2,1)S(1)} %collective-permute-done.33.refs_1_), channel_id=1, source_target_pairs={{0,8},{1,73},{2,10},{3,75},{4,12},{5,77},{6,14},{7,79},{8,64},{9,1... | collective-permute-start | bytes 3244040 | tf_op jit(solution)/shard_map/ppermute | solution.py:38
  171.0 25.0 %collective-permute-start.38 = (bf16[8,3,32,704]{3,2,1,0:T(8,128)(2,1)S(1)}, bf16[8,3,32,704]{3,2,1,0:T(8,128)(2,1)S(1)}, u32[]{:S(2)}, u32[]{:S(2)}) collective-permute-start(bf16[8,3,32,704]{3,2,1,0:T(8,128)(2,1)S(1)} %collective-permute-done.34.refs_2_), channel_id=1, source_target_pairs={{0,8},{1,73},{2,10},{3,75},{4,12},{5,77},{6,14},{7,79},{8,64},{9,1... | collective-permute-start | bytes 3244040 | tf_op jit(solution)/shard_map/ppermute | solution.py:38
  176.5 32.1 %collective-permute-start.39 = (bf16[8,3,32,704]{3,2,1,0:T(8,128)(2,1)S(1)}, bf16[8,3,32,704]{3,2,1,0:T(8,128)(2,1)S(1)}, u32[]{:S(2)}, u32[]{:S(2)}) collective-permute-start(bf16[8,3,32,704]{3,2,1,0:T(8,128)(2,1)S(1)} %collective-permute-done.35.refs_3_), channel_id=1, source_target_pairs={{0,8},{1,73},{2,10},{3,75},{4,12},{5,77},{6,14},{7,79},{8,64},{9,1... | collective-permute-start | bytes 3244040 | tf_op jit(solution)/shard_map/ppermute | solution.py:38
  196.0 36.3 %collective-permute-start.46 = (bf16[128,2048]{1,0:T(8,128)(2,1)}, bf16[128,2048]{1,0:T(8,128)(2,1)}, u32[]{:S(2)}, u32[]{:S(2)}) collective-permute-start(bf16[128,2048]{1,0:T(8,128)(2,1)} %collective-permute-done.41.a_ref.refs_2_), channel_id=1, source_target_pairs={{0,1},{1,0},{2,3},{3,2},{4,5},{5,4},{6,7},{7,6},{8,9},{9,8},{10,11... | collective-permute-start | bytes 1572872 | tf_op jit(solution)/shard_map/ppermute | solution.py:38
  196.5 48.3 %collective-permute-start.45 = (bf16[128,2048]{1,0:T(8,128)(2,1)}, bf16[128,2048]{1,0:T(8,128)(2,1)}, u32[]{:S(2)}, u32[]{:S(2)}) collective-permute-start(bf16[128,2048]{1,0:T(8,128)(2,1)} %collective-permute-done.44.a_ref.refs_4_), channel_id=1, source_target_pairs={{0,1},{1,0},{2,3},{3,2},{4,5},{5,4},{6,7},{7,6},{8,9},{9,8},{10,11... | collective-permute-start | bytes 1572872 | tf_op jit(solution)/shard_map/ppermute | solution.py:38
  201.7 56.2 %collective-permute-start.43 = (bf16[128,2048]{1,0:T(8,128)(2,1)}, bf16[128,2048]{1,0:T(8,128)(2,1)}, u32[]{:S(2)}, u32[]{:S(2)}) collective-permute-start(bf16[128,2048]{1,0:T(8,128)(2,1)} %collective-permute-done.42.a_ref.refs_6_), channel_id=1, source_target_pairs={{0,1},{1,0},{2,3},{3,2},{4,5},{5,4},{6,7},{7,6},{8,9},{9,8},{10,11... | collective-permute-start | bytes 1572872 | tf_op jit(solution)/shard_map/ppermute | solution.py:38
  231.7 52.5 %collective-permute-start.40 = (bf16[128,2048]{1,0:T(8,128)(2,1)S(1)}, bf16[128,2048]{1,0:T(8,128)(2,1)S(1)}, u32[]{:S(2)}, u32[]{:S(2)}) collective-permute-start(bf16[128,2048]{1,0:T(8,128)(2,1)S(1)} %get-tuple-element.89), channel_id=1, source_target_pairs={{0,1},{1,0},{2,3},{3,2},{4,5},{5,4},{6,7},{7,6},{8,9},{9,8},{10,11... | collective-permute-start | bytes 1572872 | tf_op jit(solution)/shard_map/ppermute | solution.py:38
  231.8 55.5 %collective-permute-start.53 = (bf16[128,2048]{1,0:T(8,128)(2,1)S(1)}, bf16[128,2048]{1,0:T(8,128)(2,1)S(1)}, u32[]{:S(2)}, u32[]{:S(2)}) collective-permute-start(bf16[128,2048]{1,0:T(8,128)(2,1)S(1)} %get-tuple-element.106), channel_id=1, source_target_pairs={{0,1},{1,0},{2,3},{3,2},{4,5},{5,4},{6,7},{7,6},{8,9},{9,8},{10,11... | collective-permute-start | bytes 1572872 | tf_op jit(solution)/shard_map/ppermute | solution.py:38
  244.6 26.0 %collective-permute-start.49 = (bf16[128,2048]{1,0:T(8,128)(2,1)S(1)}, bf16[128,2048]{1,0:T(8,128)(2,1)S(1)}, u32[]{:S(2)}, u32[]{:S(2)}) collective-permute-start(bf16[128,2048]{1,0:T(8,128)(2,1)S(1)} %get-tuple-element.102), channel_id=1, source_target_pairs={{0,1},{1,0},{2,3},{3,2},{4,5},{5,4},{6,7},{7,6},{8,9},{9,8},{10,11... | collective-permute-start | bytes 1572872 | tf_op jit(solution)/shard_map/ppermute | solution.py:38
  244.8 26.3 %collective-permute-start.56 = (bf16[128,2048]{1,0:T(8,128)(2,1)S(1)}, bf16[128,2048]{1,0:T(8,128)(2,1)S(1)}, u32[]{:S(2)}, u32[]{:S(2)}) collective-permute-start(bf16[128,2048]{1,0:T(8,128)(2,1)S(1)} %get-tuple-element.110), channel_id=1, source_target_pairs={{0,1},{1,0},{2,3},{3,2},{4,5},{5,4},{6,7},{7,6},{8,9},{9,8},{10,11... | collective-permute-start | bytes 1572872 | tf_op jit(solution)/shard_map/ppermute | solution.py:38
  273.9 36.5 %collective-permute-start.57 = (bf16[128,2048]{1,0:T(8,128)(2,1)S(1)}, bf16[128,2048]{1,0:T(8,128)(2,1)S(1)}, u32[]{:S(2)}, u32[]{:S(2)}) collective-permute-start(bf16[128,2048]{1,0:T(8,128)(2,1)S(1)} %add_convert_fusion.5), channel_id=1, source_target_pairs={{0,6},{1,3},{2,0},{3,5},{4,2},{5,7},{6,4},{7,1},{8,14},{9,11},{10,... | collective-permute-start | bytes 1572872 | tf_op jit(solution)/shard_map/ppermute | solution.py:38
  283.4 27.0 %collective-permute-start.48 = (bf16[128,2048]{1,0:T(8,128)(2,1)S(1)}, bf16[128,2048]{1,0:T(8,128)(2,1)S(1)}, u32[]{:S(2)}, u32[]{:S(2)}) collective-permute-start(bf16[128,2048]{1,0:T(8,128)(2,1)S(1)} %add_convert_fusion.10), channel_id=1, source_target_pairs={{0,4},{1,5},{2,6},{3,7},{4,0},{5,1},{6,2},{7,3},{8,12},{9,13},{10,... | collective-permute-start | bytes 1572872 | tf_op jit(solution)/shard_map/ppermute | solution.py:38
  284.2 27.1 %collective-permute-start.55 = (bf16[128,2048]{1,0:T(8,128)(2,1)S(1)}, bf16[128,2048]{1,0:T(8,128)(2,1)S(1)}, u32[]{:S(2)}, u32[]{:S(2)}) collective-permute-start(bf16[128,2048]{1,0:T(8,128)(2,1)S(1)} %add_convert_fusion.6), channel_id=1, source_target_pairs={{0,4},{1,5},{2,6},{3,7},{4,0},{5,1},{6,2},{7,3},{8,12},{9,13},{10,... | collective-permute-start | bytes 1572872 | tf_op jit(solution)/shard_map/ppermute | solution.py:38
  287.3 31.6 %collective-permute-start.52 = (bf16[128,2048]{1,0:T(8,128)(2,1)S(1)}, bf16[128,2048]{1,0:T(8,128)(2,1)S(1)}, u32[]{:S(2)}, u32[]{:S(2)}) collective-permute-start(bf16[128,2048]{1,0:T(8,128)(2,1)S(1)} %add_convert_fusion.8), channel_id=1, source_target_pairs={{0,2},{1,7},{2,4},{3,1},{4,6},{5,3},{6,0},{7,5},{8,10},{9,15},{10,... | collective-permute-start | bytes 1572872 | tf_op jit(solution)/shard_map/ppermute | solution.py:38
  289.6 35.7 %collective-permute-start.59 = (bf16[128,2048]{1,0:T(8,128)(2,1)S(1)}, bf16[128,2048]{1,0:T(8,128)(2,1)S(1)}, u32[]{:S(2)}, u32[]{:S(2)}) collective-permute-start(bf16[128,2048]{1,0:T(8,128)(2,1)S(1)} %add_convert_fusion.4), channel_id=1, source_target_pairs={{0,2},{1,7},{2,4},{3,1},{4,6},{5,3},{6,0},{7,5},{8,10},{9,15},{10,... | collective-permute-start | bytes 1572872 | tf_op jit(solution)/shard_map/ppermute | solution.py:38
  336.8 35.5 %collective-permute-start.63 = (bf16[128,2048]{1,0:T(8,128)(2,1)}, bf16[128,2048]{1,0:T(8,128)(2,1)S(1)}, u32[]{:S(2)}, u32[]{:S(2)}) collective-permute-start(bf16[128,2048]{1,0:T(8,128)(2,1)} %get-tuple-element.144), channel_id=1, source_target_pairs={{0,6},{1,3},{2,0},{3,5},{4,2},{5,7},{6,4},{7,1},{8,14},{9,11},{10,... | collective-permute-start | bytes 1572872 | tf_op jit(solution)/shard_map/ppermute | solution.py:38
  337.5 35.6 %collective-permute-start.60 = (bf16[128,2048]{1,0:T(8,128)(2,1)}, bf16[128,2048]{1,0:T(8,128)(2,1)S(1)}, u32[]{:S(2)}, u32[]{:S(2)}) collective-permute-start(bf16[128,2048]{1,0:T(8,128)(2,1)} %get-tuple-element.144), channel_id=1, source_target_pairs={{0,1},{1,0},{2,3},{3,2},{4,5},{5,4},{6,7},{7,6},{8,9},{9,8},{10,11... | collective-permute-start | bytes 1572872 | tf_op jit(solution)/shard_map/ppermute | solution.py:38
  341.0 33.2 %collective-permute-start.65 = (bf16[128,2048]{1,0:T(8,128)(2,1)}, bf16[128,2048]{1,0:T(8,128)(2,1)S(1)}, u32[]{:S(2)}, u32[]{:S(2)}) collective-permute-start(bf16[128,2048]{1,0:T(8,128)(2,1)} %collective-permute-done.61), channel_id=1, source_target_pairs={{0,2},{1,7},{2,4},{3,1},{4,6},{5,3},{6,0},{7,5},{8,10},{9,15},{10,... | collective-permute-start | bytes 1572872 | tf_op jit(solution)/shard_map/ppermute | solution.py:38
  343.5 30.8 %collective-permute-start.62 = (bf16[128,2048]{1,0:T(8,128)(2,1)}, bf16[128,2048]{1,0:T(8,128)(2,1)S(1)}, u32[]{:S(2)}, u32[]{:S(2)}) collective-permute-start(bf16[128,2048]{1,0:T(8,128)(2,1)} %collective-permute-done.61), channel_id=1, source_target_pairs={{0,1},{1,0},{2,3},{3,2},{4,5},{5,4},{6,7},{7,6},{8,9},{9,8},{10,11... | collective-permute-start | bytes 1572872 | tf_op jit(solution)/shard_map/ppermute | solution.py:38
  367.7 51.3 %collective-permute-start.92 = (bf16[4,4,2,3,16,704]{5,4,3,2,1,0:T(8,128)(2,1)}, bf16[4,4,2,3,16,704]{5,4,3,2,1,0:T(8,128)(2,1)}, u32[]{:S(2)}, u32[]{:S(2)}) collective-permute-start(bf16[4,4,2,3,16,704]{5,4,3,2,1,0:T(8,128)(2,1)} %get-tuple-element.135), channel_id=1, source_target_pairs={{0,16},{1,49},{2,18},{3,51},{4,20},{5,53},{6,22},{7,55},{8,24},{9,... | collective-permute-start | bytes 6488072 | tf_op jit(solution)/shard_map/ppermute | solution.py:38
  404.7 78.5 %collective-permute-start.91 = (bf16[4,4,2,3,16,704]{5,4,3,2,1,0:T(8,128)(2,1)}, bf16[4,4,2,3,16,704]{5,4,3,2,1,0:T(8,128)(2,1)}, u32[]{:S(2)}, u32[]{:S(2)}) collective-permute-start(bf16[4,4,2,3,16,704]{5,4,3,2,1,0:T(8,128)(2,1)} %get-tuple-element.133), channel_id=1, source_target_pairs={{0,48},{1,17},{2,50},{3,19},{4,52},{5,21},{6,54},{7,23},{8,56},{9,... | collective-permute-start | bytes 6488072 | tf_op jit(solution)/shard_map/ppermute | solution.py:38
  423.0 60.2 %collective-permute-start.93 = (bf16[4,4,2,3,16,704]{5,4,3,2,1,0:T(8,128)(2,1)}, bf16[4,4,2,3,16,704]{5,4,3,2,1,0:T(8,128)(2,1)}, u32[]{:S(2)}, u32[]{:S(2)}) collective-permute-start(bf16[4,4,2,3,16,704]{5,4,3,2,1,0:T(8,128)(2,1)} %add_convert_fusion.1), channel_id=1, source_target_pairs={{0,16},{1,49},{2,18},{3,51},{4,20},{5,53},{6,22},{7,55},{8,24},{9,... | collective-permute-start | bytes 6488072 | tf_op jit(solution)/shard_map/ppermute | solution.py:38
  434.1 92.2 %collective-permute-start.76 = (bf16[4,4,2,16,576]{4,3,2,1,0:T(8,128)(2,1)S(1)}, bf16[4,4,2,16,576]{4,3,2,1,0:T(8,128)(2,1)}, u32[]{:S(2)}, u32[]{:S(2)}) collective-permute-start(bf16[4,4,2,16,576]{4,3,2,1,0:T(8,128)(2,1)S(1)} %get-tuple-element.122), channel_id=1, source_target_pairs={{0,48},{1,17},{2,50},{3,19},{4,52},{5,21},{6,54},{7,23},{8,56},{9,... | collective-permute-start | bytes 1769480 | tf_op jit(solution)/shard_map/ppermute | solution.py:38
  435.1 44.7 %collective-permute-start.77 = (bf16[4,4,2,16,576]{4,3,2,1,0:T(8,128)(2,1)}, bf16[4,4,2,16,576]{4,3,2,1,0:T(8,128)(2,1)S(1)}, u32[]{:S(2)}, u32[]{:S(2)}) collective-permute-start(bf16[4,4,2,16,576]{4,3,2,1,0:T(8,128)(2,1)} %get-tuple-element.124), channel_id=1, source_target_pairs={{0,16},{1,49},{2,18},{3,51},{4,20},{5,53},{6,22},{7,55},{8,24},{9,... | collective-permute-start | bytes 1769480 | tf_op jit(solution)/shard_map/ppermute | solution.py:38
  480.9 45.5 %collective-permute-start.78 = (bf16[4,4,2,16,576]{4,3,2,1,0:T(8,128)(2,1)}, bf16[4,4,2,16,576]{4,3,2,1,0:T(8,128)(2,1)S(1)}, u32[]{:S(2)}, u32[]{:S(2)}) collective-permute-start(bf16[4,4,2,16,576]{4,3,2,1,0:T(8,128)(2,1)} %add_convert_fusion.3), channel_id=1, source_target_pairs={{0,16},{1,49},{2,18},{3,51},{4,20},{5,53},{6,22},{7,55},{8,24},{9,... | collective-permute-start | bytes 1769480 | tf_op jit(solution)/shard_map/ppermute | solution.py:38
  489.3 39.0 %collective-permute-start.95 = (bf16[4,2,3,16,704]{4,3,2,1,0:T(8,128)(2,1)}, bf16[4,2,3,16,704]{4,3,2,1,0:T(8,128)(2,1)}, u32[]{:S(2)}, u32[]{:S(2)}) collective-permute-start(bf16[4,2,3,16,704]{4,3,2,1,0:T(8,128)(2,1)} %get-tuple-element.159), channel_id=1, source_target_pairs={{0,8},{1,73},{2,10},{3,75},{4,12},{5,77},{6,14},{7,79},{8,64},{9,1... | collective-permute-start | bytes 1622024 | tf_op jit(solution)/shard_map/ppermute | solution.py:38
  525.7 70.6 %collective-permute-start.69 = (bf16[128,2048]{1,0:T(8,128)(2,1)}, bf16[128,2048]{1,0:T(8,128)(2,1)S(1)}, u32[]{:S(2)}, u32[]{:S(2)}) collective-permute-start(bf16[128,2048]{1,0:T(8,128)(2,1)} %get-tuple-element.151), channel_id=1, source_target_pairs={{0,1},{1,0},{2,3},{3,2},{4,5},{5,4},{6,7},{7,6},{8,9},{9,8},{10,11... | collective-permute-start | bytes 1572872 | tf_op jit(solution)/shard_map/ppermute | solution.py:38
  534.8 72.2 %collective-permute-start.71 = (bf16[128,2048]{1,0:T(8,128)(2,1)S(1)}, bf16[128,2048]{1,0:T(8,128)(2,1)S(1)}, u32[]{:S(2)}, u32[]{:S(2)}) collective-permute-start(bf16[128,2048]{1,0:T(8,128)(2,1)S(1)} %get-tuple-element.155), channel_id=1, source_target_pairs={{0,4},{1,5},{2,6},{3,7},{4,0},{5,1},{6,2},{7,3},{8,12},{9,13},{10,... | collective-permute-start | bytes 1572872 | tf_op jit(solution)/shard_map/ppermute | solution.py:38
  535.9 32.7 %collective-permute-start.79 = (bf16[4,2,16,576]{3,2,1,0:T(8,128)(2,1)S(1)}, bf16[4,2,16,576]{3,2,1,0:T(8,128)(2,1)S(1)}, u32[]{:S(2)}, u32[]{:S(2)}) collective-permute-start(bf16[4,2,16,576]{3,2,1,0:T(8,128)(2,1)S(1)} %get-tuple-element.167), channel_id=1, source_target_pairs={{0,72},{1,9},{2,74},{3,11},{4,76},{5,13},{6,78},{7,15},{8,0},{9,65... | collective-permute-start | bytes 442376 | tf_op jit(solution)/shard_map/ppermute | solution.py:38
  545.3 23.3 %collective-permute-start.81 = (bf16[4,2,16,576]{3,2,1,0:T(8,128)(2,1)S(1)}, bf16[4,2,16,576]{3,2,1,0:T(8,128)(2,1)S(1)}, u32[]{:S(2)}, u32[]{:S(2)}) collective-permute-start(bf16[4,2,16,576]{3,2,1,0:T(8,128)(2,1)S(1)} %fusion.22), channel_id=1, source_target_pairs={{0,8},{1,73},{2,10},{3,75},{4,12},{5,77},{6,14},{7,79},{8,64},{9,1... | collective-permute-start | bytes 442376 | tf_op jit(solution)/shard_map/ppermute | solution.py:38
  604.1 45.8 %collective-permute-start.103 = (bf16[2,2,4,3,16,704]{5,4,3,2,1,0:T(8,128)(2,1)S(1)}, bf16[2,2,4,3,16,704]{5,4,3,2,1,0:T(8,128)(2,1)S(1)}, u32[]{:S(2)}, u32[]{:S(2)}) collective-permute-start(bf16[2,2,4,3,16,704]{5,4,3,2,1,0:T(8,128)(2,1)S(1)} %pad_maximum_fusion.refs_0_), channel_id=1, source_target_pairs={{0,48},{1,17},{2,50},{3,19},{4,52},{5,21},{6,54},{7,23},{8,56},{9,... | collective-permute-start | bytes 3244040 | tf_op jit(solution)/shard_map/ppermute | solution.py:38
  607.0 42.8 %collective-permute-start.104 = (bf16[2,2,4,3,16,704]{5,4,3,2,1,0:T(8,128)(2,1)S(1)}, bf16[2,2,4,3,16,704]{5,4,3,2,1,0:T(8,128)(2,1)S(1)}, u32[]{:S(2)}, u32[]{:S(2)}) collective-permute-start(bf16[2,2,4,3,16,704]{5,4,3,2,1,0:T(8,128)(2,1)S(1)} %collective-permute-done.102.refs_1_), channel_id=1, source_target_pairs={{0,16},{1,49},{2,18},{3,51},{4,20},{5,53},{6,22},{7,55},{8,24},{9,... | collective-permute-start | bytes 3244040 | tf_op jit(solution)/shard_map/ppermute | solution.py:38
  607.1 32.3 %collective-permute-start.88 = (bf16[2,2,4,16,576]{4,3,2,1,0:T(8,128)(2,1)S(1)}, bf16[2,2,4,16,576]{4,3,2,1,0:T(8,128)(2,1)S(1)}, u32[]{:S(2)}, u32[]{:S(2)}) collective-permute-start(bf16[2,2,4,16,576]{4,3,2,1,0:T(8,128)(2,1)S(1)} %pad_maximum_fusion.6.refs_0_), channel_id=1, source_target_pairs={{0,16},{1,49},{2,18},{3,51},{4,20},{5,53},{6,22},{7,55},{8,24},{9,... | collective-permute-start | bytes 884744 | tf_op jit(solution)/shard_map/ppermute | solution.py:38
  613.4 28.6 %collective-permute-start.89 = (bf16[2,2,4,16,576]{4,3,2,1,0:T(8,128)(2,1)S(1)}, bf16[2,2,4,16,576]{4,3,2,1,0:T(8,128)(2,1)S(1)}, u32[]{:S(2)}, u32[]{:S(2)}) collective-permute-start(bf16[2,2,4,16,576]{4,3,2,1,0:T(8,128)(2,1)S(1)} %pad_maximum_fusion.6.refs_0_), channel_id=1, source_target_pairs={{0,48},{1,17},{2,50},{3,19},{4,52},{5,21},{6,54},{7,23},{8,56},{9,... | collective-permute-start | bytes 884744 | tf_op jit(solution)/shard_map/ppermute | solution.py:38
  (141 other events, 1753.2 us)
Sparse Core Ops, SparseCore 0:
  83.4 36.4 all-gather.5

commit v3 on v2

--- a/solution.py
+++ b/solution.py
@@ -55,7 +55,9 @@
 
 def across(value, axis):
     def target(yh, x, yl, z, c):
-        if axis == "z":
+        if axis == "x":
+            x = (x + 2) % 4
+        elif axis == "z":
             z = (z + 2) % 4
         else:
             yh = 1 - yh
@@ -72,10 +74,10 @@
     return send(value, lambda yh, x, yl, z, c: (yh, x, 1 - yl, z, c))
 
 
-def ring_gather(value, axis):
+def ring_gather(value, axis, forward=False):
     first = step(value, axis, 1)
     second = step(value, axis, -1)
-    third = step(first, axis, 1)
+    third = step(first, axis, 1) if forward else across(value, axis)
     return value, first, second, third
 
 
@@ -87,10 +89,16 @@
 
 
 def ring_scatter(own, before, after, far, axis):
-    got_far = step(far, axis, 1)
-    got_after = step(before, axis, -1)
-    got_before = step(add(after, got_far).astype(BF), axis, 1)
-    return add(own, got_after, got_before)
+    got = across(far, axis), step(before, axis, -1), step(after, axis, 1)
+    return add(own, *got)
+
+
+def sum_all(value):
+    value = value + swap(value)
+    for axis in ("z", "y", "x"):
+        value = value + across(value, axis)
+        value = value + step(value, axis, 1)
+    return value
 
 
 def exchange_z(own, before, after, far):
@@ -127,11 +135,7 @@
     return pltpu.CompilerParams(vmem_limit_bytes=mib * MIB)
 
 
-def cost(flops, moved):
-    return pl.CostEstimate(flops=flops, bytes_accessed=moved, transcendentals=0)
-
-
-def call(body, tables, grid, in_specs, out_specs, out_shape, scratch, mib, flops, moved, args, aliases=None):
+def call(body, tables, grid, in_specs, out_specs, out_shape, scratch, mib, args, aliases=None):
     return pl.pallas_call(
         body,
         grid_spec=pltpu.PrefetchScalarGridSpec(
@@ -139,7 +143,7 @@
         ),
         out_shape=out_shape,
         compiler_params=params(mib),
-        cost_estimate=cost(flops, moved),
+        cost_estimate=pl.CostEstimate(flops=1000, bytes_accessed=1000, transcendentals=0),
         input_output_aliases=aliases or {},
     )(*tables, *args)
 
@@ -176,7 +180,7 @@
     return call(
         pack_attn_kernel, (spots, core), (1,),
         [pl.BlockSpec((32, w.shape[1]), rows) for w in (q, k, v)],
-        [pl.BlockSpec(shape, whole)] * 2, [sds(shape)] * 2, [], 16, 1000, 400000, (q, k, v),
+        [pl.BlockSpec(shape, whole)] * 2, [sds(shape)] * 2, [], 16, (q, k, v),
     )
 
 
@@ -204,7 +208,7 @@
         pack_mlp_kernel, (spots, core), (1,),
         [pl.BlockSpec((32, FF), rows), pl.BlockSpec((32, FF), rows), pl.BlockSpec((FF, 128), lambda i, *_: (0, 0))],
         [pl.BlockSpec(shape, whole)] * 2, [sds(shape)] * 2, [pltpu.VMEM((128, FF), F32)],
-        24, 1000, 4000000, (gate, up, down),
+        24, (gate, up, down),
     )
 
 
@@ -226,7 +230,7 @@
             pl.BlockSpec((2, 1, 128, QKV), lambda i, slot, *_: (0, slot[i], 0, 0)),
             pl.BlockSpec((2, 128, QUERY), lambda i, *_: (0, 0, i)),
         ],
-        [sds((2, 8, 128, QKV)), sds((2, 128, D))], [], 16, 1000, 5000000, tuple(pieces),
+        [sds((2, 8, 128, QKV)), sds((2, 128, D))], [], 16, tuple(pieces),
     )
     return qkv.reshape(D, QKV), out.reshape(QUERY, D)
 
@@ -245,7 +249,7 @@
         place_mlp_kernel, (slot, xs, halves), (8,),
         [pl.BlockSpec((1, 3, 32, WIDE), lambda i, *_: (i, 0, 0, 0))] * 8,
         pl.BlockSpec((3, 2, 1, 128, WIDE), lambda i, slot, *_: (0, 0, slot[i], 0, 0)),
-        sds((3, 2, 8, 128, WIDE)), [], 16, 1000, 18000000, tuple(pieces),
+        sds((3, 2, 8, 128, WIDE)), [], 16, tuple(pieces),
     )
     return out.reshape(3, D, WIDE)
 
@@ -296,11 +300,11 @@
         [q_spec, pl.BlockSpec(k.shape, whole), pl.BlockSpec(v.shape, whole), pl.BlockSpec(w.shape, whole)],
         [q_spec, pl.BlockSpec((TOK, D), lambda i, *_: (i, 0))],
         [sds(q.shape), sds((rows, D))], [pltpu.VMEM((4 * TOK, HEAD), F32)],
-        16, 6 * rows * 2048 * 256, 3 * MIB, (q, k, v, w),
-    )
-
-
-def attend_back_kernel(query_place, key_slot, q_ref, g_ref, k_ref, v_ref, kt_ref, dq_ref, dk_ref, dv_ref, total):
+        16, (q, k, v, w),
+    )
+
+
+def attend_back_kernel(query_place, key_slot, core, count, q_ref, g_ref, k_ref, v_ref, kt_ref, dq_ref, keep_ref, give_ref, total, dk_ref, dv_ref):
     step_at = pl.program_id(0)
     place = query_place[step_at]
     queries = head_rows(q_ref[...])
@@ -338,36 +342,50 @@
 
     dq_ref[...] = head_columns((total[...] * SCORE).T).astype(BF)
 
-
-def attend_back(query_place, key_slot, q, g, k, v):
+    @pl.when(step_at == pl.num_programs(0) - 1)
+    def _():
+        first = core[0] == 0
+        for j in range(16):
+            key = dk_ref[j * TOK : (j + 1) * TOK, :] * SCORE
+            value = dv_ref[j * TOK : (j + 1) * TOK, :]
+            row = lax.broadcasted_iota(jnp.int32, value.shape, 0)
+            value = jnp.where(row < count[j], value, 0.0)
+            keep_ref[j * TOK : (j + 1) * TOK, :] = jnp.where(first, key, value).astype(BF)
+            other = j ^ 1
+            give_ref[other * TOK : (other + 1) * TOK, :] = jnp.where(first, value, key).astype(BF)
+
+
+def attend_back(query_place, key_slot, core, count, q, g, k, v):
     rows = q.shape[0]
     whole = lambda i, *_: (0, 0)
     rows_spec = pl.BlockSpec((TOK, QUERY), lambda i, *_: (i, 0))
+    kv_spec = pl.BlockSpec(k.shape, whole)
     return call(
-        attend_back_kernel, (query_place, key_slot), (rows // TOK,),
-        [rows_spec, rows_spec, pl.BlockSpec(k.shape, whole), pl.BlockSpec(v.shape, whole), pl.BlockSpec((HEAD, k.shape[0]), whole)],
-        [rows_spec, pl.BlockSpec(k.shape, whole), pl.BlockSpec(v.shape, whole)],
-        [sds(q.shape), sds(k.shape, F32), sds(v.shape, F32)], [pltpu.VMEM((HEAD, 4 * TOK), F32)],
-        16, 10 * 2048 * 2048 * 256, 4 * MIB, (q, g, k, v, k.T),
-    )
-
-
-SPLIT = 4
+        attend_back_kernel, (query_place, key_slot, core, count), (rows // TOK,),
+        [rows_spec, rows_spec, kv_spec, kv_spec, pl.BlockSpec((HEAD, k.shape[0]), whole)],
+        [rows_spec, kv_spec, kv_spec], [sds(q.shape), sds(k.shape), sds(v.shape)],
+        [pltpu.VMEM((HEAD, 4 * TOK), F32), pltpu.VMEM(k.shape, F32), pltpu.VMEM(k.shape, F32)],
+        16, (q, g, k, v, k.T),
+    )
+
+
+SPLIT = 2
 DEEP = D // SPLIT
-
-
-def mlp_kernel(chunk, a_ref, b_ref, ga_ref, gb_ref, w_ref, *refs):
-    refs = refs[-14:]
-    z_ref, da_ref, dc_ref, grad_mine, grad_peer, out_mine, out_peer = refs[:7]
-    weights, gate, up, back, gate_grad, up_grad, hidden = refs[7:]
+ROWS = 4 * TOK
+
+
+def mlp_kernel(chunk, *refs):
+    rows_refs, grads_refs, w_ref = refs[:4], refs[4:8], refs[8]
+    z_ref, da_ref, dc_ref, grad_ref = refs[-8:-4]
+    weights, gate, up, back = refs[-4:]
     k = pl.program_id(0)
 
     @pl.when(k < SPLIT)
     def _():
-        rows = jnp.concatenate([a_ref[...], b_ref[...]], axis=0)
-        grads = jnp.concatenate([ga_ref[...], gb_ref[...]], axis=0)
+        rows = jnp.concatenate([ref[...] for ref in rows_refs], axis=0)
+        grads = jnp.concatenate([ref[...] for ref in grads_refs], axis=0)
         terms = (dot(rows, w_ref[0]), dot(rows, w_ref[1]), dot(grads, w_ref[2]))
-        weights[k] = w_ref[...]
+        weights[k] = w_ref[:2]
 
         @pl.when(k == 0)
         def _():
@@ -384,103 +402,121 @@
         a, c, dz = gate[...], up[...], back[...]
         sig = 1.0 / (1.0 + jnp.exp(-a))
         silu = a * sig
-        hidden[...] = (silu * c).astype(BF)
-        gate_grad[...] = (dz * c * sig * (1.0 + a * (1.0 - sig))).astype(BF)
-        up_grad[...] = (dz * silu).astype(BF)
-        z_ref[...] = hidden[...]
-        da_ref[...] = gate_grad[...]
-        dc_ref[...] = up_grad[...]
+        z_ref[...] = (silu * c).astype(BF)
+        da_ref[...] = (dz * c * sig * (1.0 + a * (1.0 - sig))).astype(BF)
+        dc_ref[...] = (dz * silu).astype(BF)
 
     @pl.when(k >= SPLIT)
     def _():
         j = k - SPLIT
-        grad = dot_last(gate_grad[...], weights[j, 0]) + dot_last(up_grad[...], weights[j, 1])
-        out = dot_last(hidden[...], weights[j, 2])
-        grad_mine[...] = grad[:TOK].astype(BF)
-        grad_peer[...] = grad[TOK:].astype(BF)
-        out_mine[...] = out[:TOK].astype(BF)
-        out_peer[...] = out[TOK:].astype(BF)
-
-
-def mlp_group(group, chunk, own, peer, grads, weights, kept):
+        grad = dot_last(da_ref[...], weights[j, 0]) + dot_last(dc_ref[...], weights[j, 1])
+        for r in range(4):
+            grad_ref[r] = grad[TOK * r : TOK * (r + 1)].astype(BF)
+
+
+def mlp_half(part, chunk, rows, grads, weights, kept):
     deep = lambda k: jnp.minimum(k, SPLIT - 1)
-    token_spec = pl.BlockSpec((TOK, DEEP), lambda k, chunk: (0, deep(k)))
-    out_spec = pl.BlockSpec((TOK, DEEP), lambda k, chunk: (0, jnp.maximum(k - SPLIT, 0)))
-    kept_spec = pl.BlockSpec((2 * TOK, WIDE), lambda k, chunk: (group, 0))
-    args = (own, peer, grads, grads, weights)
-    specs = [
-        token_spec,
-        token_spec,
-        pl.BlockSpec((TOK, DEEP), lambda k, chunk: (chunk[2 * group], deep(k))),
-        pl.BlockSpec((TOK, DEEP), lambda k, chunk: (chunk[2 * group + 1], deep(k))),
-        pl.BlockSpec((3, DEEP, WIDE), lambda k, chunk: (0, deep(k), 0)),
-    ]
+    kept_spec = pl.BlockSpec((ROWS, WIDE), lambda k, chunk: (part, 0))
+
+    def grads_spec(r):
+        return pl.BlockSpec((TOK, DEEP), lambda k, chunk: (chunk[4 * part + r], deep(k)))
+
+    args = tuple(rows) + (grads,) * 4 + (weights,)
+    specs = [pl.BlockSpec((TOK, DEEP), lambda k, chunk: (0, deep(k)))] * 4
+    specs += [grads_spec(r) for r in range(4)]
+    specs += [pl.BlockSpec((3, DEEP, WIDE), lambda k, chunk: (0, deep(k), 0))]
     aliases = {}
     if kept is not None:
         args = args + tuple(kept)
         specs = specs + [pl.BlockSpec(memory_space=pl.ANY)] * 3
-        aliases = {6: 0, 7: 1, 8: 2}
-    wide = pltpu.VMEM((2 * TOK, WIDE), F32)
-    narrow = pltpu.VMEM((2 * TOK, WIDE), BF)
+        aliases = {10: 0, 11: 1, 12: 2}
+    wide = pltpu.VMEM((ROWS, WIDE), F32)
     out = call(
-        mlp_kernel, (chunk,), (2 * SPLIT,), specs, [kept_spec] * 3 + [out_spec] * 4,
-        [sds((8 * TOK, WIDE))] * 3 + [sds((TOK, D))] * 4,
-        [pltpu.VMEM((SPLIT, 3, DEEP, WIDE), BF), wide, wide, wide, narrow, narrow, narrow],
-        40, 12 * 2 * TOK * D * WIDE, 14 * MIB, args, aliases,
-    )
-    return out[:3], out[3:]
+        mlp_kernel, (chunk,), (2 * SPLIT,), specs,
+        [kept_spec] * 3 + [pl.BlockSpec((4, TOK, DEEP), lambda k, chunk: (0, 0, jnp.maximum(k - SPLIT, 0)))],
+        [sds((8 * TOK, WIDE))] * 3 + [sds((4, TOK, D))],
+        [pltpu.VMEM((SPLIT, 2, DEEP, WIDE), BF), wide, wide, wide],
+        48, args, aliases,
+    )
+    return out[:3], out[3]
+
+
+def grads_specs(tail):
+    zeros = (0,) * (1 + len(tail))
+    x_first = pl.BlockSpec((2, 1, 2) + tail, lambda h, p, *_: (h, jnp.minimum(p, 1)) + zeros)
+    y_own = pl.BlockSpec((4, 1, 2) + tail, lambda h, p, *_: (0, jnp.where(h == 0, jnp.maximum(p - 2, 0), 1)) + zeros)
+    y_other = pl.BlockSpec((4, 1, 2) + tail, lambda h, p, *_: (0, jnp.where(h == 1, jnp.maximum(p - 2, 0), 0)) + zeros)
+    return [x_first] * 4 + [y_own] * 2 + [y_other] * 2, [sds((4, 2, 2) + tail)] * 8
+
+
+def write_grads(outs, xs, yhs, core, write):
+    half, p = pl.program_id(0), pl.program_id(1)
+
+    def go(pos, r, ref):
+        inside = yhs[2 * half + pos] * 64 + xs[r] * 16
+        for rc in range(2):
+            write(ref.at[rc], inside, jnp.abs(core[0] - rc), rc)
+
+    @pl.when(p < 2)
+    def _():
+        for r in range(4):
+            for pos in range(2):
+                go(pos, r, outs[r].at[pos, 0])
+
+    for each in range(2):
+
+        @pl.when((p >= 2) & (half == each))
+        def _():
+            for r in range(4):
+                for pos in range(2):
+                    go(pos, r, outs[4 + 2 * each + pos].at[r, 0])
 
 
 def mlp_grads_kernel(column, xs, yhs, core, nat, *refs):
-    tokens, (g_ref, da_ref, dc_ref, z_ref), outs, (turned, grads) = refs[:8], refs[8:12], refs[12:16], refs[16:]
-    half = pl.program_id(0)
+    tokens, (g_ref, da_ref, dc_ref, z_ref), outs, (turned, grads) = refs[:8], refs[8:12], refs[12:20], refs[20:]
     rows = jnp.concatenate([ref[...] for ref in tokens], axis=0).T
     grads[0] = dot(rows, da_ref[...])
     grads[1] = dot(rows, dc_ref[...])
     for r in range(8):
         turned[:, TOK * r : TOK * (r + 1)] = g_ref[pl.ds(pl.multiple_of(nat[r] * TOK, TOK), TOK), :].T
     grads[2] = dot(turned[...], z_ref[...])
-    for r in range(4):
-        for pos in range(2):
-            for rc in range(2):
-                start = jnp.abs(core[0] - rc) * 128 + yhs[2 * half + pos] * 64 + xs[r] * 16
-                for m in range(3):
-                    outs[r][pos, 0, rc, m] = grads[m, at_rows(start, 16), :].astype(BF)
+
+    def write(ref, inside, which, rc):
+        for m in range(3):
+            ref[m] = grads[m, at_rows(which * 128 + inside, 16), :].astype(BF)
+
+    write_grads(outs, xs, yhs, core, write)
 
 
 def mlp_grads(column, xs, yhs, core, nat, tokens, g, da, dc, z):
     col = lambda h, p, column, *_: (0, column[4 * h + p])
-    whole = lambda h, p, *_: (0, 0)
-    hidden = pl.BlockSpec((8 * TOK, WIDE), whole)
-    out = pl.BlockSpec((2, 1, 2, 3, 16, WIDE), lambda h, p, *_: (h, p, 0, 0, 0, 0))
+    hidden = pl.BlockSpec((8 * TOK, WIDE), lambda h, p, *_: (0, 0))
+    specs, shapes = grads_specs((3, 16, WIDE))
     return call(
         mlp_grads_kernel, (column, xs, yhs, core, nat), (2, 4),
         [pl.BlockSpec((TOK, 256), col)] * 8 + [pl.BlockSpec((8 * TOK, 256), col), hidden, hidden, hidden],
-        [out] * 4, [sds((4, 4, 2, 3, 16, WIDE))] * 4,
-        [pltpu.VMEM((256, 8 * TOK), BF), pltpu.VMEM((3, 256, WIDE), F32)],
-        32, 6 * 8 * TOK * D * WIDE, 22 * MIB, tuple(tokens) + (g, da, dc, z),
+        specs, shapes, [pltpu.VMEM((256, 8 * TOK), BF), pltpu.VMEM((3, 256, WIDE), F32)],
+        40, tuple(tokens) + (g, da, dc, z),
     )
 
 
 def attn_grads_kernel(column, xs, yhs, core, halves, h_ref, g_ref, o_ref, dqkv_ref, w_ref, *refs):
-    outs, gain_ref, (first, second) = refs[:4], refs[4], refs[5:]
-    half = pl.program_id(0)
+    outs, gain_ref, (first, second) = refs[:8], refs[8], refs[9:]
     first[...] = dot(h_ref[...].T, dqkv_ref[...])
     second[...] = dot(o_ref[...].T, g_ref[...])
     gain = jnp.sum(first[...] * w_ref[...].astype(F32), axis=1, keepdims=True)
     gain_ref[0] = jnp.broadcast_to(gain, (256, 128)).T[:8]
-    for r in range(4):
-        for pos in range(2):
-            inside = yhs[2 * half + pos] * 64 + xs[r] * 16
-            for rc in range(2):
-                start = jnp.abs(core[0] - rc) * 128 + inside
-                outs[r][pos, 0, rc, :, :QUERY] = second[at_rows(inside, 16), QUERY * rc : QUERY * (rc + 1)].astype(BF)
-                outs[r][pos, 0, rc, :, QUERY:] = first[at_rows(start, 16), :].astype(BF)
+
+    def write(ref, inside, which, rc):
+        ref[:, :QUERY] = second[at_rows(inside, 16), QUERY * rc : QUERY * (rc + 1)].astype(BF)
+        ref[:, QUERY:] = first[at_rows(which * 128 + inside, 16), :].astype(BF)
+
+    write_grads(outs, xs, yhs, core, write)
 
 
 def attn_grads(column, xs, yhs, core, halves, h, g, o, dqkv, w):
     col = lambda i, p, column, *_: (0, column[4 * i + p])
-    out = pl.BlockSpec((2, 1, 2, 16, PACK), lambda i, p, *_: (i, p, 0, 0, 0))
+    specs, shapes = grads_specs((16, PACK))
     *outs, gain = call(
         attn_grads_kernel, (column, xs, yhs, core, halves), (2, 4),
         [
@@ -490,10 +526,10 @@
             pl.BlockSpec((8 * TOK, QKV), lambda i, p, *_: (0, 0)),
             pl.BlockSpec((256, QKV), lambda i, p, column, *_: (column[4 * i + p], 0)),
         ],
-        [out] * 4 + [pl.BlockSpec((1, 8, 256), lambda i, p, column, *_: (column[4 * i + p], 0, 0))],
-        [sds((4, 4, 2, 16, PACK))] * 4 + [sds((8, 8, 256), F32)],
+        specs + [pl.BlockSpec((1, 8, 256), lambda i, p, column, *_: (column[4 * i + p], 0, 0))],
+        shapes + [sds((8, 8, 256), F32)],
         [pltpu.VMEM((256, QKV), F32), pltpu.VMEM((128, 2 * QUERY), F32)],
-        24, 2 * 8 * TOK * D * PACK, 12 * MIB, (h, g, o, dqkv, w),
+        24, (h, g, o, dqkv, w),
     )
     return outs, gain[:, 0, :].reshape(D)
 
@@ -519,7 +555,7 @@
         [pl.BlockSpec((2, 2, 1, 3, 16, WIDE), lambda p, *_: (0, 0, p, 0, 0, 0))] * 4,
         [side, side, pl.BlockSpec((2 * WIDE, 128), lambda p, spots, *_: (spots[1 + p], 0))],
         [sds((128, FF), F32), sds((128, FF), F32), sds((FF, 128), F32)], [pltpu.VMEM((128, 2 * WIDE), F32)],
-        24, 1000, 14 * MIB, tuple(parts),
+        24, tuple(parts),
     )
 
 
@@ -555,7 +591,7 @@
         finish_attn_kernel, (spots, xs, yhs, core), (1,),
         [pl.BlockSpec((2, 2, 4, 16, PACK), lambda i, *_: (0, 0, 0, 0, 0))] * 4,
         [pl.BlockSpec(shape, whole) for shape in shapes], [sds(shape, F32) for shape in shapes], [],
-        16, 1000, 4 * MIB, tuple(parts),
+        16, tuple(parts),
     )
 
 
@@ -637,8 +673,8 @@
         parts = jnp.concatenate(exchange_z(own, before, forward, far))
         return parts
 
-    def spread(part):
-        pieces = ring_gather(part, "x")
+    def spread(part, forward):
+        pieces = ring_gather(part, "x", forward)
         return list(pieces) + [step(piece, "y", 1) for piece in pieces]
 
     out_rows = lax.dynamic_slice_in_dim(output_weight, x * 32, 32, axis=0)
@@ -648,7 +684,7 @@
     )
     attn_part = exchange(*pack_attn(spots, core, query_weight, key_weight, value_weight))
     attn_part = jnp.concatenate([out_part, attn_part], axis=-1)
-    attn_pieces = spread(attn_part)
+    attn_pieces = spread(attn_part, False)
     w_qkv, w_out = place_attn(slot, xs, halves, attn_pieces)
 
     normed_parts = gather_tokens((rows_in * scale_attn * gain_one).astype(BF))
@@ -656,7 +692,7 @@
 
     mlp_mine, mlp_other = pack_mlp(spots, core, gate_weight, up_weight, down_weight)
     mlp_part = exchange(mlp_mine, after(mlp_other, attn_part))
-    w_mlp = place_mlp(slot, xs, halves, spread(after(mlp_part, attn_pieces[3])))
+    w_mlp = place_mlp(slot, xs, halves, spread(mlp_part, True))
 
     grad_rows = lax.all_gather(
         after(cotangent[0], normed_parts[6]), "blk", axis=0, tiled=True,
@@ -692,22 +728,28 @@
 
 
     kept, results = None, []
-    for g in range(4):
-        kept, result = mlp_group(g, chunk, mlp_parts[2 * g], mlp_parts[2 * g + 1], grad_rows, w_mlp, kept)
-        results.append(result)
+    for part in range(2):
+        kept, result = mlp_half(part, chunk, mlp_parts[4 * part : 4 * part + 4], grad_rows, w_mlp, kept)
+        results += [result[r] for r in range(4)]
     hidden, gate_grad_rows, up_grad_rows = kept
-    grad_mine, grad_peer, out_mine, out_peer = zip(*results)
-    normed_grad = scatter_tokens(grad_mine, grad_peer)
+    mlp_sums = mlp_grads(
+        column, xs, yhs, core, chunk, mlp_parts, grad_rows, gate_grad_rows, up_grad_rows, hidden
+    )
+    normed_grad = after(scatter_tokens(results[::2], results[1::2]), mlp_sums[0])
     residual_grad = cotangent[0].astype(F32) + norm_back(residual, scale_mlp, gain_two, normed_grad)
     mlp_gain_part = jnp.sum(normed_grad * residual * scale_mlp, axis=0)
     branch_parts = gather_tokens(residual_grad.astype(BF))
     branch_grad = jnp.concatenate(branch_parts)
-    layer_out = (residual + scatter_tokens(out_mine, out_peer)).astype(BF)[None]
+    branch = dot_last(after(hidden, mlp_sums[0]), w_mlp[2]).astype(BF).reshape(4, 2, TOK, D)
+    layer_out = (residual + scatter_tokens(branch[:, 0], branch[:, 1])).astype(BF)[None]
 
 
     def reduce_planes(outs):
-        got = ring_scatter(*outs, "x").astype(BF)
-        return ring_scatter(got[0], got[2], got[3], got[1], "y").astype(BF)
+        low = ring_scatter(*outs[:4], "x").astype(BF)
+        low = ring_scatter(low[0], low[2], low[3], low[1], "y").astype(BF)
+        high = ring_scatter(outs[4], outs[6], outs[7], outs[5], "y").astype(BF)
+        high = ring_scatter(high[0], high[1], high[2], high[3], "x").astype(BF)
+        return jnp.concatenate([low, high])
 
     def resplit_back(part):
         got = exchange_z(part[0], part[1], part[2], part[3])
@@ -715,25 +757,18 @@
         other = swap(jnp.stack([got[p][1] for p in (0, 2, 1, 3)]))
         return jnp.stack([mine, other])
 
-    def gather_batch(part):
-        return ring_gather(jnp.stack([part, across(part, "y")]), "x")
-
-    mlp_sums = mlp_grads(
-        column, xs, yhs, core, chunk, mlp_parts, grad_rows, gate_grad_rows, up_grad_rows, hidden
-    )
-    mlp_sums = gather_batch(resplit_back(reduce_planes(mlp_sums)))
+    def gather_batch(part, forward):
+        return ring_gather(jnp.stack([part, across(part, "y")]), "x", forward)
+
+    mlp_sums = gather_batch(resplit_back(reduce_planes(mlp_sums)), True)
     gate_grad, up_grad, down_grad = finish_mlp(spots, xs, yhs, core, mlp_sums)
 
 
     attn_grad = dot_last(branch_grad, w_out).astype(BF)
-    query_grad_rows, key_terms, value_terms = attend_back(
-        query_place, key_slot, queries, attn_grad, keys, values
-    )
-    key_terms = (key_terms * SCORE).astype(BF)
-    value_terms = jnp.where(usable, value_terms, 0.0).astype(BF)
-    kv_keep = jnp.where(first_core, key_terms, value_terms)
-    kv_give = flip(swap(jnp.where(first_core, value_terms, key_terms)))
-    kv_terms = add(kv_keep, kv_give)
+    query_grad_rows, kv_keep, kv_give = attend_back(
+        query_place, key_slot, core, key_count, queries, attn_grad, keys, values
+    )
+    kv_terms = add(kv_keep, swap(kv_give))
     half_rows = 8 * TOK
     kv_grad_rows = add(kv_terms[:half_rows], to_half(kv_terms[half_rows:].astype(BF))).astype(BF)
     qkv_grad_rows = jnp.concatenate([query_grad_rows, kv_grad_rows], axis=1)
@@ -741,16 +776,14 @@
     attn_sums, attn_gain_part = attn_grads(
         column, xs, yhs, core, halves, normed_attn, branch_grad, attn_rows, qkv_grad_rows, w_qkv
     )
-    gain_grads = jnp.stack([attn_gain_part / gain_one, mlp_gain_part])
-    for axis in ("blk", "batch"):
-        gain_grads = jnp.sum(lax.all_gather(gain_grads, axis), axis=0)
+    gain_grads = sum_all(jnp.stack([attn_gain_part / gain_one, mlp_gain_part]))
     attn_sums = reduce_planes(attn_sums)
     out_sums = send(
         attn_sums[..., :QUERY], lambda yh, x, yl, z, c: (yh, x, z // 2, 2 * (z % 2) + c, yl)
     )
     qkv_sums = resplit_back(attn_sums[..., QUERY:])
     attn_sums = jnp.concatenate([out_sums.reshape(2, 4, 16, QUERY), qkv_sums], axis=-1)
-    query_grad, key_grad, value_grad, output_grad = finish_attn(spots, xs, yhs, core, gather_batch(attn_sums))
+    query_grad, key_grad, value_grad, output_grad = finish_attn(spots, xs, yhs, core, gather_batch(attn_sums, False))
 
     attn_partial = dot_last(qkv_grad_rows, w_qkv).astype(BF).reshape(4, 2, TOK, D)
     normed_attn_grad = scatter_tokens(attn_partial[:, 0], attn_partial[:, 1])

time: 673 us -> 712 us (1.058)
  waiting for transfers between devices: 197 us -> 256 us
  blocking collectives: 54.4 us -> 0 us
  starting transfers between devices: 147 us -> 200 us
  local copies, waits for them, and re-layouts: 62.6 us -> 52.5 us
  other arithmetic: 41 us -> 31.4 us
    ppermute x105 -> x124, waiting for transfers between devices: 197 us -> 256 us  [send(): return lax.ppermute(value, BOTH, pairs)]
    all_gather x2 -> x0, blocking collectives: 54.4 us -> none  [on_device(): gain_grads = jnp.sum(lax.all_gather(gain_grads, axis), axis=0)]
    ppermute x105 -> x124, starting transfers between devices: 147 us -> 200 us  [send(): return lax.ppermute(value, BOTH, pairs)]
    unnamed x182 -> x192, local copies, waits for them, and re-layouts: 43.7 us -> 33 us
    convert_element_type x8, other arithmetic: 11.4 us -> 3.35 us  [the longest x2 2.11 us: reduce_planes(): high = ring_scatter(outs[4], outs[6], outs[7], outs[5], 'y').astype(BF)]
    pallas_call x17 -> x15, Pallas kernels: 134 us -> 133 us  [call(): pl.pallas_call(body, grid_spec=pltpu.PrefetchScalarGridSpec(num_scalar_pr...]
  transfers between devices with their start and end apart: 106 -> 125, of which waited for: 40 -> 49; matrix products, arithmetic and copies ran while one was open for 12% -> 10% of each run, Pallas kernels for 20% -> 16%
where the time goes in v3:
time: 712 us; the launch traced here: 701 us
  waiting for transfers between devices  256 us (36%)
  starting transfers between devices  200 us (28%)
  Pallas kernels  133 us (19%)
  local copies, waits for them, and re-layouts  52.5 us (7%)
  other arithmetic  31.4 us (4%)
  between operations  16.4 us (2%)
  matrix products  11.3 us (2%)
    ppermute x124, waiting for transfers between devices, send(): return lax.ppermute(value, BOTH, pairs)  256 us
    ppermute x124, starting transfers between devices, send(): return lax.ppermute(value, BOTH, pairs)  200 us
    pallas_call x15, Pallas kernels, call(): pl.pallas_call(body, grid_spec=pltpu.PrefetchScalarGridSpec(num_scalar_pr...  133 us
    unnamed x192, local copies, waits for them, and re-layouts  33 us
  transfers between devices with their start and end apart: 125, of which 49 were waited for; matrix products, arithmetic and copies ran while one was open for 10% of the time, Pallas kernels for 16%

profile of v3, /device:TPU:24, one launch (start us, length us, event | category | flops | bytes accessed | tf_op | source)
XLA Modules:
  0.0 700.5 jit_solution(7121305569687021379)
XLA Ops:
  22.7 4.1 collective-permute-start.7
  32.8 5.4 collective-permute-done.9
  43.6 4.4 collective-permute-done.11
  52.4 6.6 collective-permute-done.12.refs_1_
  62.1 6.7 collective-permute-done.14.refs_3_
  114.8 4.1 collective-permute-start.34
  129.0 5.3 shard_map.216
  140.4 7.8 %shard_map.215 = (bf16[256,256]{1,0:T(8,128)(2,1)S(1)}, bf16[256,2048]{1,0:T(8,128)(2,1)S(1)}) custom-call(s32[2]{0:T(128)S(1)} %get-tuple-element.216.query_place, s32[16]{0:T(128)S(1)} %select_reduce_fusion.1.key_slot, bf16[256,256]{1,0:T(8,128)(2,1)S(1)} %copy.62.q_ref, bf16[2048,64]{1,0:T(8,128)(2,1)S(1)} %copy.60.k_ref, ...), custom_call_target="tpu_custom_call" | custom-call | flops 1000 | bytes 1000 | tf_op jit(solution)/shard_map/pallas_call | solution.py:139
  148.4 7.3 %shard_map.214 = (bf16[256,256]{1,0:T(8,128)(2,1)S(1)}, bf16[256,2048]{1,0:T(8,128)(2,1)S(1)}) custom-call(s32[2]{0:T(128)S(1)} %get-tuple-element.213.query_place, s32[16]{0:T(128)S(1)} %select_reduce_fusion.1.key_slot, bf16[256,256]{1,0:T(8,128)(2,1)S(1)} %copy.59.q_ref, bf16[2048,64]{1,0:T(8,128)(2,1)S(1)} %copy.60.k_ref, ...), custom_call_target="tpu_custom_call" | custom-call | flops 1000 | bytes 1000 | tf_op jit(solution)/shard_map/pallas_call | solution.py:139
  166.3 4.6 collective-permute-start.39
  172.2 12.5 %collective-permute-start.40 = (bf16[8,3,32,704]{3,2,1,0:T(8,128)(2,1)}, bf16[8,3,32,704]{3,2,1,0:T(8,128)(2,1)S(1)}, u32[]{:S(2)}, u32[]{:S(2)}) collective-permute-start(bf16[8,3,32,704]{3,2,1,0:T(8,128)(2,1)} %collective-permute-done.36.refs_1_), channel_id=1, source_target_pairs={{0,8},{1,73},{2,10},{3,75},{4,12},{5,77},{6,14},{7,79},{8,64},{9,1... | collective-permute-start | bytes 3244040 | tf_op jit(solution)/shard_map/ppermute | solution.py:38
  186.1 10.8 %collective-permute-start.28 = (bf16[128,2048]{1,0:T(8,128)(2,1)S(1)}, bf16[128,2048]{1,0:T(8,128)(2,1)S(1)}, u32[]{:S(2)}, u32[]{:S(2)}) collective-permute-start(bf16[128,2048]{1,0:T(8,128)(2,1)S(1)} %multiply_convert_fusion.refs_0_), channel_id=1, source_target_pairs={{0,6},{1,3},{2,0},{3,5},{4,2},{5,7},{6,4},{7,1},{8,14},{9,11},{10,... | collective-permute-start | bytes 1572872 | tf_op jit(solution)/shard_map/ppermute | solution.py:38
  196.9 6.5 collective-permute-start.42
  209.6 7.5 %collective-permute-done.30.refs_2_.refs_6_ = bf16[128,2048]{1,0:T(8,128)(2,1)} collective-permute-done((bf16[128,2048]{1,0:T(8,128)(2,1)S(1)}, bf16[128,2048]{1,0:T(8,128)(2,1)}, u32[]{:S(2)}, u32[]{:S(2)}) %collective-permute-start.30) | collective-permute-done | bytes 524320 | tf_op jit(solution)/shard_map/ppermute | solution.py:38
  219.4 4.4 collective-permute-done.44.refs_2_
  236.0 6.2 shard_map.219
  248.5 15.9 %shard_map.220 = (bf16[1024,704]{1,0:T(8,128)(2,1)S(1)}, bf16[1024,704]{1,0:T(8,128)(2,1)S(1)}, bf16[1024,704]{1,0:T(8,128)(2,1)}, bf16[4,128,2048]{2,1,0:T(8,128)(2,1)}) custom-call(s32[8]{0:T(128)S(1)} %copy-done.35, bf16[128,2048]{1,0:T(8,128)(2,1)S(1)} %multiply_convert_fusion.refs_0_, bf16[128,2048]{1,0:T(8,128)(2,1)} %collective-permute-done.43.refs_1_, ...), custom_call_target="tpu_custom_call" | custom-call | flops 1000 | bytes 1000 | tf_op jit(solution)/shard_map/pallas_call | solution.py:139
  264.4 15.9 %shard_map.221 = (bf16[1024,704]{1,0:T(8,128)(2,1)S(1)}, bf16[1024,704]{1,0:T(8,128)(2,1)S(1)}, bf16[1024,704]{1,0:T(8,128)(2,1)}, bf16[4,128,2048]{2,1,0:T(8,128)(2,1)}) custom-call(s32[8]{0:T(128)S(1)} %copy-done.35, bf16[128,2048]{1,0:T(8,128)(2,1)S(1)} %collective-permute-done.28.refs_0_.refs_4_, ...), custom_call_target="tpu_custom_call", output_to_operand_aliasing={{0}: (10, {}), {1}: (11, {}), {2}: (12, {})} | custom-call | flops 1000 | bytes 1000 | tf_op jit(solution)/shard_map/pallas_call | solution.py:139
  285.6 19.6 %shard_map.222 = (bf16[4,2,2,3,16,704]{5,4,3,2,1,0:T(8,128)(2,1)S(1)}, bf16[4,2,2,3,16,704]{5,4,3,2,1,0:T(8,128)(2,1)S(1)}, bf16[4,2,2,3,16,704]{5,4,3,2,1,0:T(8...) custom-call(s32[8]{0:T(128)S(1)} %copy-done.37, ...), custom_call_target="tpu_custom_call" | custom-call | flops 1000 | bytes 1000 | tf_op jit(solution)/shard_map/pallas_call | solution.py:139
  315.1 8.2 %collective-permute-start.112 = (bf16[4,2,2,3,16,704]{5,4,3,2,1,0:T(8,128)(2,1)}, bf16[4,2,2,3,16,704]{5,4,3,2,1,0:T(8,128)(2,1)}, u32[]{:S(2)}, u32[]{:S(2)}) collective-permute-start(bf16[4,2,2,3,16,704]{5,4,3,2,1,0:T(8,128)(2,1)} %get-tuple-element.113), channel_id=1, source_target_pairs={{0,8},{1,73},{2,10},{3,75},{4,12},{5,77},{6,14},{7,79},{8,64},{9,1... | collective-permute-start | bytes 3244040 | tf_op jit(solution)/shard_map/ppermute | solution.py:38
  331.1 13.1 %collective-permute-done.59 = bf16[128,2048]{1,0:T(8,128)(2,1)} collective-permute-done((bf16[128,2048]{1,0:T(8,128)(2,1)}, bf16[128,2048]{1,0:T(8,128)(2,1)}, u32[]{:S(2)}, u32[]{:S(2)}) %collective-permute-start.59) | collective-permute-done | bytes 524320 | tf_op jit(solution)/shard_map/ppermute | solution.py:38
  344.3 5.9 collective-permute-start.50
  352.6 15.8 %collective-permute-done.50 = bf16[128,2048]{1,0:T(8,128)(2,1)S(1)} collective-permute-done((bf16[128,2048]{1,0:T(8,128)(2,1)}, bf16[128,2048]{1,0:T(8,128)(2,1)S(1)}, u32[]{:S(2)}, u32[]{:S(2)}) %collective-permute-start.50) | collective-permute-done | bytes 524320 | tf_op jit(solution)/shard_map/ppermute | solution.py:38
  376.3 10.9 %collective-permute-done.111 = bf16[4,2,2,3,16,704]{5,4,3,2,1,0:T(8,128)(2,1)S(1)} collective-permute-done((bf16[4,2,2,3,16,704]{5,4,3,2,1,0:T(8,128)(2,1)}, bf16[4,2,2,3,16,704]{5,4,3,2,1,0:T(8,128)(2,1)S(1)}, u32[]{:S(2)}, u32[]{:S(2)}) %collective-permute-start.111) | collective-permute-done | bytes 1081376 | tf_op jit(solution)/shard_map/ppermute | solution.py:38
  392.5 25.1 %collective-permute-done.106 = bf16[4,2,2,3,16,704]{5,4,3,2,1,0:T(8,128)(2,1)S(1)} collective-permute-done((bf16[4,2,2,3,16,704]{5,4,3,2,1,0:T(8,128)(2,1)S(1)}, bf16[4,2,2,3,16,704]{5,4,3,2,1,0:T(8,128)(2,1)S(1)}, u32[]{:S(2)}, u32[]{:S(2)}) %collective-permute-start.106) | collective-permute-done | bytes 1081376 | tf_op jit(solution)/shard_map/ppermute | solution.py:38
  421.0 7.7 %collective-permute-start.109 = (bf16[2,2,3,16,704]{4,3,2,1,0:T(8,128)(2,1)S(1)}, bf16[2,2,3,16,704]{4,3,2,1,0:T(8,128)(2,1)S(1)}, u32[]{:S(2)}, u32[]{:S(2)}) collective-permute-start(bf16[2,2,3,16,704]{4,3,2,1,0:T(8,128)(2,1)S(1)} %get-tuple-element.149), channel_id=1, source_target_pairs={{0,8},{1,73},{2,10},{3,75},{4,12},{5,77},{6,14},{7,79},{8,64},{9,1... | collective-permute-start | bytes 811016 | tf_op jit(solution)/shard_map/ppermute | solution.py:38
  437.3 5.6 collective-permute-start.63
  443.1 4.4 collective-permute-done.61
  450.0 4.9 collective-permute-start.118
  456.2 12.0 %collective-permute-done.63 = bf16[128,2048]{1,0:T(8,128)(2,1)S(1)} collective-permute-done((bf16[128,2048]{1,0:T(8,128)(2,1)S(1)}, bf16[128,2048]{1,0:T(8,128)(2,1)S(1)}, u32[]{:S(2)}, u32[]{:S(2)}) %collective-permute-start.63) | collective-permute-done | bytes 524320 | tf_op jit(solution)/shard_map/ppermute | solution.py:38
  468.2 4.4 collective-permute-start.64
  476.3 30.5 %shard_map.223 = (bf16[1024,256]{1,0:T(8,128)(2,1)S(1)}, bf16[2048,64]{1,0:T(8,128)(2,1)S(1)}, bf16[2048,64]{1,0:T(8,128)(2,1)S(1)}) custom-call(s32[8]{0:T(128)S(1)} %bitcast.250, s32[16]{0:T(128)S(1)} %copy-done.33, s32[1]{0:T(128)} %bitcast.22.core, s32[16]{0:T(128)S(1)} %copy-done.45, bf16[1024,256]{1,0:T(8,128)(2,1)S(1)} %copy.71.q_ref, ...), custom_call_target="tpu_custom_call" | custom-call | flops 1000 | bytes 1000 | tf_op jit(solution)/shard_map/pallas_call | solution.py:139
  509.8 8.0 %collective-permute-done.68 = bf16[1024,64]{1,0:T(8,128)(2,1)S(1)} collective-permute-done((bf16[1024,64]{1,0:T(8,128)(2,1)S(1)}, bf16[1024,64]{1,0:T(8,128)(2,1)S(1)}, u32[]{:S(2)}, u32[]{:S(2)}) %collective-permute-start.68) | collective-permute-done | bytes 131104 | tf_op jit(solution)/shard_map/ppermute | solution.py:38
  518.1 8.5 %shard_map.224 = (bf16[4,2,2,16,576]{4,3,2,1,0:T(8,128)(2,1)S(1)}, bf16[4,2,2,16,576]{4,3,2,1,0:T(8,128)(2,1)S(1)}, bf16[4,2,2,16,576]{4,3,2,1,0:T(8,128)(2,1)S(...) custom-call(s32[8]{0:T(128)S(1)} %copy-done.38, ...), custom_call_target="tpu_custom_call" | custom-call | flops 1000 | bytes 1000 | tf_op jit(solution)/shard_map/pallas_call | solution.py:139
  528.5 4.8 collective-permute-done.77
  535.0 9.2 %collective-permute-done.120 = bf16[2,4,3,16,704]{4,3,2,1,0:T(8,128)(2,1)S(1)} collective-permute-done((bf16[2,4,3,16,704]{4,3,2,1,0:T(8,128)(2,1)S(1)}, bf16[2,4,3,16,704]{4,3,2,1,0:T(8,128)(2,1)S(1)}, u32[]{:S(2)}, u32[]{:S(2)}) %collective-permute-start.120) | collective-permute-done | bytes 540704 | tf_op jit(solution)/shard_map/ppermute | solution.py:38
  553.4 9.6 %collective-permute-done.80 = f32[2,2048]{1,0:T(2,128)S(1)} collective-permute-done((f32[2,2048]{1,0:T(2,128)S(1)}, f32[2,2048]{1,0:T(2,128)S(1)}, u32[]{:S(2)}, u32[]{:S(2)}) %collective-permute-start.80) | collective-permute-done | bytes 16416 | tf_op jit(solution)/shard_map/ppermute | solution.py:38
  570.2 4.2 collective-permute-done.85
  577.1 6.0 collective-permute-done.84
  599.7 4.9 collective-permute-done.98
  618.0 5.4 collective-permute-done.95
  630.6 4.8 collective-permute-done.100
  635.6 4.8 collective-permute-done.82
  644.4 7.5 %collective-permute-done.101.refs_1_ = bf16[2,2,4,16,576]{4,3,2,1,0:T(8,128)(2,1)S(1)} collective-permute-done((bf16[2,2,4,16,576]{4,3,2,1,0:T(8,128)(2,1)S(1)}, bf16[2,2,4,16,576]{4,3,2,1,0:T(8,128)(2,1)S(1)}, u32[]{:S(2)}, u32[]{:S(2)}) %collective-permute-start.101) | collective-permute-done | bytes 294944 | tf_op jit(solution)/shard_map/ppermute | solution.py:38
  651.9 7.3 %collective-permute-start.73 = (bf16[128,2048]{1,0:T(8,128)(2,1)S(1)}, bf16[128,2048]{1,0:T(8,128)(2,1)S(1)}, u32[]{:S(2)}, u32[]{:S(2)}) collective-permute-start(bf16[128,2048]{1,0:T(8,128)(2,1)S(1)} %get-tuple-element.134), channel_id=1, source_target_pairs={{0,6},{1,3},{2,0},{3,5},{4,2},{5,7},{6,4},{7,1},{8,14},{9,11},{10,... | collective-permute-start | bytes 1572872 | tf_op jit(solution)/shard_map/ppermute | solution.py:38
  664.8 12.2 %collective-permute-done.73 = bf16[128,2048]{1,0:T(8,128)(2,1)S(1)} collective-permute-done((bf16[128,2048]{1,0:T(8,128)(2,1)S(1)}, bf16[128,2048]{1,0:T(8,128)(2,1)S(1)}, u32[]{:S(2)}, u32[]{:S(2)}) %collective-permute-start.73) | collective-permute-done | bytes 524320 | tf_op jit(solution)/shard_map/ppermute | solution.py:38
  679.1 8.2 %collective-permute-done.122.refs_2_ = bf16[2,2,4,3,16,704]{5,4,3,2,1,0:T(8,128)(2,1)S(1)} collective-permute-done((bf16[2,2,4,3,16,704]{5,4,3,2,1,0:T(8,128)(2,1)S(1)}, bf16[2,2,4,3,16,704]{5,4,3,2,1,0:T(8,128)(2,1)S(1)}, u32[]{:S(2)}, u32[]{:S(2)}) %collective-permute-start.122) | collective-permute-done | bytes 1081376 | tf_op jit(solution)/shard_map/ppermute | solution.py:38
  688.5 4.8 shard_map.226
  (540 shorter events, 269.5 us)
Async XLA Ops:
  7.2 240.6 %all-gather.2.cloned.1.call-start = ((), (), s32[]{:S(2)}) async-start(), calls=%async_computation | async-start | bytes 4718592 | tf_op jit(solution)/shard_map/all_gather | solution.py:697
  12.2 58.3 %collective-permute-start = (bf16[128,2048]{1,0:T(8,128)(2,1)}, bf16[128,2048]{1,0:T(8,128)(2,1)}, u32[]{:S(2)}, u32[]{:S(2)}) collective-permute-start(bf16[128,2048]{1,0:T(8,128)(2,1)} %get-tuple-element.127), channel_id=1, source_target_pairs={{0,1},{1,0},{2,3},{3,2},{4,5},{5,4},{6,7},{7,6},{8,9},{9,8},{10,11... | collective-permute-start | bytes 1572872 | tf_op jit(solution)/shard_map/ppermute | solution.py:38
  12.2 48.6 %collective-permute-start.1 = (bf16[128,2048]{1,0:T(8,128)(2,1)}, bf16[128,2048]{1,0:T(8,128)(2,1)}, u32[]{:S(2)}, u32[]{:S(2)}) collective-permute-start(bf16[128,2048]{1,0:T(8,128)(2,1)} %get-tuple-element.127), channel_id=1, source_target_pairs={{0,2},{1,7},{2,4},{3,1},{4,6},{5,3},{6,0},{7,5},{8,10},{9,15},{10,... | collective-permute-start | bytes 1572872 | tf_op jit(solution)/shard_map/ppermute | solution.py:38
  14.1 47.7 %collective-permute-start.5 = (bf16[128,2048]{1,0:T(8,128)(2,1)}, bf16[128,2048]{1,0:T(8,128)(2,1)}, u32[]{:S(2)}, u32[]{:S(2)}) collective-permute-start(bf16[128,2048]{1,0:T(8,128)(2,1)} %get-tuple-element.127), channel_id=1, source_target_pairs={{0,4},{1,5},{2,6},{3,7},{4,0},{5,1},{6,2},{7,3},{8,12},{9,13},{10,... | collective-permute-start | bytes 1572872 | tf_op jit(solution)/shard_map/ppermute | solution.py:38
  22.7 25.3 %collective-permute-start.7 = (bf16[8,32,256]{2,1,0:T(8,128)(2,1)}, bf16[8,32,256]{2,1,0:T(8,128)(2,1)}, u32[]{:S(2)}, u32[]{:S(2)}) collective-permute-start(bf16[8,32,256]{2,1,0:T(8,128)(2,1)} %bitcast.237), channel_id=1, source_target_pairs={{0,0},{1,8},{2,1},{3,9},{4,2},{5,10},{6,3},{7,11},{8,4},{9,12},{10... | collective-permute-start | bytes 393224 | tf_op jit(solution)/shard_map/ppermute | solution.py:38
  61.8 22.4 %collective-permute-start.2 = (bf16[128,2048]{1,0:T(8,128)(2,1)}, bf16[128,2048]{1,0:T(8,128)(2,1)}, u32[]{:S(2)}, u32[]{:S(2)}) collective-permute-start(bf16[128,2048]{1,0:T(8,128)(2,1)} %collective-permute-done.1), channel_id=1, source_target_pairs={{0,1},{1,0},{2,3},{3,2},{4,5},{5,4},{6,7},{7,6},{8,9},{9,8},{10,11... | collective-permute-start | bytes 1572872 | tf_op jit(solution)/shard_map/ppermute | solution.py:38
  114.8 41.1 %collective-permute-start.26 = (bf16[128,2048]{1,0:T(8,128)(2,1)}, bf16[128,2048]{1,0:T(8,128)(2,1)}, u32[]{:S(2)}, u32[]{:S(2)}) collective-permute-start(bf16[128,2048]{1,0:T(8,128)(2,1)} %slice.361), channel_id=1, source_target_pairs={{0,1},{1,0},{2,3},{3,2},{4,5},{5,4},{6,7},{7,6},{8,9},{9,8},{10,11... | collective-permute-start | bytes 1572872 | tf_op jit(solution)/shard_map/ppermute | solution.py:38
  136.9 29.4 %collective-permute-start.36 = (bf16[8,3,32,704]{3,2,1,0:T(8,128)(2,1)}, bf16[8,3,32,704]{3,2,1,0:T(8,128)(2,1)}, u32[]{:S(2)}, u32[]{:S(2)}) collective-permute-start(bf16[8,3,32,704]{3,2,1,0:T(8,128)(2,1)} %constant_dynamic-update-slice_fusion.13.refs_0_), channel_id=1, source_target_pairs={{0,16},{1,49},{2,18},{3,51},{4,20},{5,53},{6,22},{7,55},{8,24},{9,... | collective-permute-start | bytes 3244040 | tf_op jit(solution)/shard_map/ppermute | solution.py:38
  136.9 34.0 %collective-permute-start.37 = (bf16[8,3,32,704]{3,2,1,0:T(8,128)(2,1)}, bf16[8,3,32,704]{3,2,1,0:T(8,128)(2,1)}, u32[]{:S(2)}, u32[]{:S(2)}) collective-permute-start(bf16[8,3,32,704]{3,2,1,0:T(8,128)(2,1)} %constant_dynamic-update-slice_fusion.13.refs_0_), channel_id=1, source_target_pairs={{0,48},{1,17},{2,50},{3,19},{4,52},{5,21},{6,54},{7,23},{8,56},{9,... | collective-permute-start | bytes 3244040 | tf_op jit(solution)/shard_map/ppermute | solution.py:38
  160.0 24.6 %collective-permute-start.25 = (bf16[128,2048]{1,0:T(8,128)(2,1)S(1)}, bf16[128,2048]{1,0:T(8,128)(2,1)S(1)}, u32[]{:S(2)}, u32[]{:S(2)}) collective-permute-start(bf16[128,2048]{1,0:T(8,128)(2,1)S(1)} %add_convert_fusion.3), channel_id=1, source_target_pairs={{0,6},{1,3},{2,0},{3,5},{4,2},{5,7},{6,4},{7,1},{8,14},{9,11},{10,... | collective-permute-start | bytes 1572872 | tf_op jit(solution)/shard_map/ppermute | solution.py:38
  162.3 22.4 %collective-permute-start.23 = (bf16[128,2048]{1,0:T(8,128)(2,1)S(1)}, bf16[128,2048]{1,0:T(8,128)(2,1)S(1)}, u32[]{:S(2)}, u32[]{:S(2)}) collective-permute-start(bf16[128,2048]{1,0:T(8,128)(2,1)S(1)} %add_convert_fusion.4), channel_id=1, source_target_pairs={{0,4},{1,5},{2,6},{3,7},{4,0},{5,1},{6,2},{7,3},{8,12},{9,13},{10,... | collective-permute-start | bytes 1572872 | tf_op jit(solution)/shard_map/ppermute | solution.py:38
  166.3 37.1 %collective-permute-start.39 = (bf16[8,3,32,704]{3,2,1,0:T(8,128)(2,1)}, bf16[8,3,32,704]{3,2,1,0:T(8,128)(2,1)S(1)}, u32[]{:S(2)}, u32[]{:S(2)}) collective-permute-start(bf16[8,3,32,704]{3,2,1,0:T(8,128)(2,1)} %constant_dynamic-update-slice_fusion.13.refs_0_), channel_id=1, source_target_pairs={{0,8},{1,73},{2,10},{3,75},{4,12},{5,77},{6,14},{7,79},{8,64},{9,1... | collective-permute-start | bytes 3244040 | tf_op jit(solution)/shard_map/ppermute | solution.py:38
  170.9 26.0 %collective-permute-start.38 = (bf16[8,3,32,704]{3,2,1,0:T(8,128)(2,1)}, bf16[8,3,32,704]{3,2,1,0:T(8,128)(2,1)}, u32[]{:S(2)}, u32[]{:S(2)}) collective-permute-start(bf16[8,3,32,704]{3,2,1,0:T(8,128)(2,1)} %collective-permute-done.36.refs_1_), channel_id=1, source_target_pairs={{0,16},{1,49},{2,18},{3,51},{4,20},{5,53},{6,22},{7,55},{8,24},{9,... | collective-permute-start | bytes 3244040 | tf_op jit(solution)/shard_map/ppermute | solution.py:38
  172.2 55.3 %collective-permute-start.40 = (bf16[8,3,32,704]{3,2,1,0:T(8,128)(2,1)}, bf16[8,3,32,704]{3,2,1,0:T(8,128)(2,1)S(1)}, u32[]{:S(2)}, u32[]{:S(2)}) collective-permute-start(bf16[8,3,32,704]{3,2,1,0:T(8,128)(2,1)} %collective-permute-done.36.refs_1_), channel_id=1, source_target_pairs={{0,8},{1,73},{2,10},{3,75},{4,12},{5,77},{6,14},{7,79},{8,64},{9,1... | collective-permute-start | bytes 3244040 | tf_op jit(solution)/shard_map/ppermute | solution.py:38
  184.7 43.9 %collective-permute-start.41 = (bf16[8,3,32,704]{3,2,1,0:T(8,128)(2,1)}, bf16[8,3,32,704]{3,2,1,0:T(8,128)(2,1)S(1)}, u32[]{:S(2)}, u32[]{:S(2)}) collective-permute-start(bf16[8,3,32,704]{3,2,1,0:T(8,128)(2,1)} %collective-permute-done.37.refs_2_), channel_id=1, source_target_pairs={{0,8},{1,73},{2,10},{3,75},{4,12},{5,77},{6,14},{7,79},{8,64},{9,1... | collective-permute-start | bytes 3244040 | tf_op jit(solution)/shard_map/ppermute | solution.py:38
  186.1 21.7 %collective-permute-start.28 = (bf16[128,2048]{1,0:T(8,128)(2,1)S(1)}, bf16[128,2048]{1,0:T(8,128)(2,1)S(1)}, u32[]{:S(2)}, u32[]{:S(2)}) collective-permute-start(bf16[128,2048]{1,0:T(8,128)(2,1)S(1)} %multiply_convert_fusion.refs_0_), channel_id=1, source_target_pairs={{0,6},{1,3},{2,0},{3,5},{4,2},{5,7},{6,4},{7,1},{8,14},{9,11},{10,... | collective-permute-start | bytes 1572872 | tf_op jit(solution)/shard_map/ppermute | solution.py:38
  196.9 33.9 %collective-permute-start.42 = (bf16[8,3,32,704]{3,2,1,0:T(8,128)(2,1)}, bf16[8,3,32,704]{3,2,1,0:T(8,128)(2,1)}, u32[]{:S(2)}, u32[]{:S(2)}) collective-permute-start(bf16[8,3,32,704]{3,2,1,0:T(8,128)(2,1)} %collective-permute-done.38.refs_3_), channel_id=1, source_target_pairs={{0,8},{1,73},{2,10},{3,75},{4,12},{5,77},{6,14},{7,79},{8,64},{9,1... | collective-permute-start | bytes 3244040 | tf_op jit(solution)/shard_map/ppermute | solution.py:38
  217.1 30.7 %collective-permute-start.43 = (bf16[128,2048]{1,0:T(8,128)(2,1)S(1)}, bf16[128,2048]{1,0:T(8,128)(2,1)}, u32[]{:S(2)}, u32[]{:S(2)}) collective-permute-start(bf16[128,2048]{1,0:T(8,128)(2,1)S(1)} %multiply_convert_fusion.refs_0_), channel_id=1, source_target_pairs={{0,1},{1,0},{2,3},{3,2},{4,5},{5,4},{6,7},{7,6},{8,9},{9,8},{10,11... | collective-permute-start | bytes 1572872 | tf_op jit(solution)/shard_map/ppermute | solution.py:38
  223.8 24.0 %collective-permute-start.45 = (bf16[128,2048]{1,0:T(8,128)(2,1)}, bf16[128,2048]{1,0:T(8,128)(2,1)}, u32[]{:S(2)}, u32[]{:S(2)}) collective-permute-start(bf16[128,2048]{1,0:T(8,128)(2,1)} %collective-permute-done.44.refs_2_), channel_id=1, source_target_pairs={{0,1},{1,0},{2,3},{3,2},{4,5},{5,4},{6,7},{7,6},{8,9},{9,8},{10,11... | collective-permute-start | bytes 1572872 | tf_op jit(solution)/shard_map/ppermute | solution.py:38
  228.5 35.9 %collective-permute-start.29 = (bf16[128,2048]{1,0:T(8,128)(2,1)S(1)}, bf16[128,2048]{1,0:T(8,128)(2,1)}, u32[]{:S(2)}, u32[]{:S(2)}) collective-permute-start(bf16[128,2048]{1,0:T(8,128)(2,1)S(1)} %collective-permute-done.28.refs_0_.refs_4_), channel_id=1, source_target_pairs={{0,1},{1,0},{2,3},{3,2},{4,5},{5,4},{6,7},{7,6},{8,9},{9,8},{10,11... | collective-permute-start | bytes 1572872 | tf_op jit(solution)/shard_map/ppermute | solution.py:38
  229.6 34.8 %collective-permute-start.31 = (bf16[128,2048]{1,0:T(8,128)(2,1)}, bf16[128,2048]{1,0:T(8,128)(2,1)}, u32[]{:S(2)}, u32[]{:S(2)}) collective-permute-start(bf16[128,2048]{1,0:T(8,128)(2,1)} %collective-permute-done.30.refs_2_.refs_6_), channel_id=1, source_target_pairs={{0,1},{1,0},{2,3},{3,2},{4,5},{5,4},{6,7},{7,6},{8,9},{9,8},{10,11... | collective-permute-start | bytes 1572872 | tf_op jit(solution)/shard_map/ppermute | solution.py:38
  283.6 27.8 %collective-permute-start.54 = (bf16[128,2048]{1,0:T(8,128)(2,1)}, bf16[128,2048]{1,0:T(8,128)(2,1)}, u32[]{:S(2)}, u32[]{:S(2)}) collective-permute-start(bf16[128,2048]{1,0:T(8,128)(2,1)} %get-tuple-element.146), channel_id=1, source_target_pairs={{0,1},{1,0},{2,3},{3,2},{4,5},{5,4},{6,7},{7,6},{8,9},{9,8},{10,11... | collective-permute-start | bytes 1572872 | tf_op jit(solution)/shard_map/ppermute | solution.py:38
  283.6 27.9 %collective-permute-start.58 = (bf16[128,2048]{1,0:T(8,128)(2,1)}, bf16[128,2048]{1,0:T(8,128)(2,1)}, u32[]{:S(2)}, u32[]{:S(2)}) collective-permute-start(bf16[128,2048]{1,0:T(8,128)(2,1)} %get-tuple-element.147), channel_id=1, source_target_pairs={{0,1},{1,0},{2,3},{3,2},{4,5},{5,4},{6,7},{7,6},{8,9},{9,8},{10,11... | collective-permute-start | bytes 1572872 | tf_op jit(solution)/shard_map/ppermute | solution.py:38
  285.1 24.8 %collective-permute-start.56 = (bf16[128,2048]{1,0:T(8,128)(2,1)}, bf16[128,2048]{1,0:T(8,128)(2,1)S(1)}, u32[]{:S(2)}, u32[]{:S(2)}) collective-permute-start(bf16[128,2048]{1,0:T(8,128)(2,1)} %get-tuple-element.143), channel_id=1, source_target_pairs={{0,1},{1,0},{2,3},{3,2},{4,5},{5,4},{6,7},{7,6},{8,9},{9,8},{10,11... | collective-permute-start | bytes 1572872 | tf_op jit(solution)/shard_map/ppermute | solution.py:38
  315.1 56.6 %collective-permute-start.112 = (bf16[4,2,2,3,16,704]{5,4,3,2,1,0:T(8,128)(2,1)}, bf16[4,2,2,3,16,704]{5,4,3,2,1,0:T(8,128)(2,1)}, u32[]{:S(2)}, u32[]{:S(2)}) collective-permute-start(bf16[4,2,2,3,16,704]{5,4,3,2,1,0:T(8,128)(2,1)} %get-tuple-element.113), channel_id=1, source_target_pairs={{0,8},{1,73},{2,10},{3,75},{4,12},{5,77},{6,14},{7,79},{8,64},{9,1... | collective-permute-start | bytes 3244040 | tf_op jit(solution)/shard_map/ppermute | solution.py:38
  328.3 21.9 %collective-permute-start.52 = (bf16[128,2048]{1,0:T(8,128)(2,1)}, bf16[128,2048]{1,0:T(8,128)(2,1)}, u32[]{:S(2)}, u32[]{:S(2)}) collective-permute-start(bf16[128,2048]{1,0:T(8,128)(2,1)} %get-tuple-element.140), channel_id=1, source_target_pairs={{0,2},{1,7},{2,4},{3,1},{4,6},{5,3},{6,0},{7,5},{8,10},{9,15},{10,... | collective-permute-start | bytes 1572872 | tf_op jit(solution)/shard_map/ppermute | solution.py:38
  344.3 42.9 %collective-permute-start.111 = (bf16[4,2,2,3,16,704]{5,4,3,2,1,0:T(8,128)(2,1)}, bf16[4,2,2,3,16,704]{5,4,3,2,1,0:T(8,128)(2,1)S(1)}, u32[]{:S(2)}, u32[]{:S(2)}) collective-permute-start(bf16[4,2,2,3,16,704]{5,4,3,2,1,0:T(8,128)(2,1)} %copy-done.53), channel_id=1, source_target_pairs={{0,72},{1,9},{2,74},{3,11},{4,76},{5,13},{6,78},{7,15},{8,0},{9,65... | collective-permute-start | bytes 3244040 | tf_op jit(solution)/shard_map/ppermute | solution.py:38
  344.3 42.9 %collective-permute-start.110 = (bf16[4,2,2,3,16,704]{5,4,3,2,1,0:T(8,128)(2,1)}, bf16[4,2,2,3,16,704]{5,4,3,2,1,0:T(8,128)(2,1)S(1)}, u32[]{:S(2)}, u32[]{:S(2)}) collective-permute-start(bf16[4,2,2,3,16,704]{5,4,3,2,1,0:T(8,128)(2,1)} %copy-done.52), channel_id=1, source_target_pairs={{0,64},{1,65},{2,66},{3,67},{4,68},{5,69},{6,70},{7,71},{8,72},{9,... | collective-permute-start | bytes 3244040 | tf_op jit(solution)/shard_map/ppermute | solution.py:38
  344.3 24.1 %collective-permute-start.50 = (bf16[128,2048]{1,0:T(8,128)(2,1)}, bf16[128,2048]{1,0:T(8,128)(2,1)S(1)}, u32[]{:S(2)}, u32[]{:S(2)}) collective-permute-start(bf16[128,2048]{1,0:T(8,128)(2,1)} %get-tuple-element.141), channel_id=1, source_target_pairs={{0,6},{1,3},{2,0},{3,5},{4,2},{5,7},{6,4},{7,1},{8,14},{9,11},{10,... | collective-permute-start | bytes 1572872 | tf_op jit(solution)/shard_map/ppermute | solution.py:38
  368.4 49.2 %collective-permute-start.106 = (bf16[4,2,2,3,16,704]{5,4,3,2,1,0:T(8,128)(2,1)S(1)}, bf16[4,2,2,3,16,704]{5,4,3,2,1,0:T(8,128)(2,1)S(1)}, u32[]{:S(2)}, u32[]{:S(2)}) collective-permute-start(bf16[4,2,2,3,16,704]{5,4,3,2,1,0:T(8,128)(2,1)S(1)} %copy-done.51), channel_id=1, source_target_pairs={{0,16},{1,49},{2,18},{3,51},{4,20},{5,53},{6,22},{7,55},{8,24},{9,... | collective-permute-start | bytes 3244040 | tf_op jit(solution)/shard_map/ppermute | solution.py:38
  371.0 46.6 %collective-permute-start.105 = (bf16[4,2,2,3,16,704]{5,4,3,2,1,0:T(8,128)(2,1)S(1)}, bf16[4,2,2,3,16,704]{5,4,3,2,1,0:T(8,128)(2,1)S(1)}, u32[]{:S(2)}, u32[]{:S(2)}) collective-permute-start(bf16[4,2,2,3,16,704]{5,4,3,2,1,0:T(8,128)(2,1)S(1)} %copy-done.49), channel_id=1, source_target_pairs={{0,48},{1,17},{2,50},{3,19},{4,52},{5,21},{6,54},{7,23},{8,56},{9,... | collective-permute-start | bytes 3244040 | tf_op jit(solution)/shard_map/ppermute | solution.py:38
  371.7 48.5 %collective-permute-start.104 = (bf16[4,2,2,3,16,704]{5,4,3,2,1,0:T(8,128)(2,1)S(1)}, bf16[4,2,2,3,16,704]{5,4,3,2,1,0:T(8,128)(2,1)S(1)}, u32[]{:S(2)}, u32[]{:S(2)}) collective-permute-start(bf16[4,2,2,3,16,704]{5,4,3,2,1,0:T(8,128)(2,1)S(1)} %copy-done.47), channel_id=1, source_target_pairs={{0,32},{1,33},{2,34},{3,35},{4,36},{5,37},{6,38},{7,39},{8,40},{9,... | collective-permute-start | bytes 3244040 | tf_op jit(solution)/shard_map/ppermute | solution.py:38
  389.2 43.8 %collective-permute-start.115 = (bf16[2,2,3,16,704]{4,3,2,1,0:T(8,128)(2,1)S(1)}, bf16[2,2,3,16,704]{4,3,2,1,0:T(8,128)(2,1)S(1)}, u32[]{:S(2)}, u32[]{:S(2)}) collective-permute-start(bf16[2,2,3,16,704]{4,3,2,1,0:T(8,128)(2,1)S(1)} %get-tuple-element.152), channel_id=1, source_target_pairs={{0,16},{1,49},{2,18},{3,51},{4,20},{5,53},{6,22},{7,55},{8,24},{9,... | collective-permute-start | bytes 811016 | tf_op jit(solution)/shard_map/ppermute | solution.py:38
  391.4 42.0 %collective-permute-start.114 = (bf16[2,2,3,16,704]{4,3,2,1,0:T(8,128)(2,1)S(1)}, bf16[2,2,3,16,704]{4,3,2,1,0:T(8,128)(2,1)S(1)}, u32[]{:S(2)}, u32[]{:S(2)}) collective-permute-start(bf16[2,2,3,16,704]{4,3,2,1,0:T(8,128)(2,1)S(1)} %get-tuple-element.153), channel_id=1, source_target_pairs={{0,48},{1,17},{2,50},{3,19},{4,52},{5,21},{6,54},{7,23},{8,56},{9,... | collective-permute-start | bytes 811016 | tf_op jit(solution)/shard_map/ppermute | solution.py:38
  433.4 21.6 %collective-permute-start.60 = (bf16[128,2048]{1,0:T(8,128)(2,1)S(1)}, bf16[128,2048]{1,0:T(8,128)(2,1)S(1)}, u32[]{:S(2)}, u32[]{:S(2)}) collective-permute-start(bf16[128,2048]{1,0:T(8,128)(2,1)S(1)} %get-tuple-element.122), channel_id=1, source_target_pairs={{0,1},{1,0},{2,3},{3,2},{4,5},{5,4},{6,7},{7,6},{8,9},{9,8},{10,11... | collective-permute-start | bytes 1572872 | tf_op jit(solution)/shard_map/ppermute | solution.py:38
  437.3 30.9 %collective-permute-start.63 = (bf16[128,2048]{1,0:T(8,128)(2,1)S(1)}, bf16[128,2048]{1,0:T(8,128)(2,1)S(1)}, u32[]{:S(2)}, u32[]{:S(2)}) collective-permute-start(bf16[128,2048]{1,0:T(8,128)(2,1)S(1)} %get-tuple-element.122), channel_id=1, source_target_pairs={{0,6},{1,3},{2,0},{3,5},{4,2},{5,7},{6,4},{7,1},{8,14},{9,11},{10,... | collective-permute-start | bytes 1572872 | tf_op jit(solution)/shard_map/ppermute | solution.py:38
  442.9 29.8 %collective-permute-start.65 = (bf16[128,2048]{1,0:T(8,128)(2,1)S(1)}, bf16[128,2048]{1,0:T(8,128)(2,1)S(1)}, u32[]{:S(2)}, u32[]{:S(2)}) collective-permute-start(bf16[128,2048]{1,0:T(8,128)(2,1)S(1)} %get-tuple-element.122), channel_id=1, source_target_pairs={{0,4},{1,5},{2,6},{3,7},{4,0},{5,1},{6,2},{7,3},{8,12},{9,13},{10,... | collective-permute-start | bytes 1572872 | tf_op jit(solution)/shard_map/ppermute | solution.py:38
  447.6 25.2 %collective-permute-start.62 = (bf16[128,2048]{1,0:T(8,128)(2,1)S(1)}, bf16[128,2048]{1,0:T(8,128)(2,1)S(1)}, u32[]{:S(2)}, u32[]{:S(2)}) collective-permute-start(bf16[128,2048]{1,0:T(8,128)(2,1)S(1)} %collective-permute-done.61), channel_id=1, source_target_pairs={{0,1},{1,0},{2,3},{3,2},{4,5},{5,4},{6,7},{7,6},{8,9},{9,8},{10,11... | collective-permute-start | bytes 1572872 | tf_op jit(solution)/shard_map/ppermute | solution.py:38
  450.0 57.2 %collective-permute-start.118 = (bf16[2,3,16,704]{3,2,1,0:T(8,128)(2,1)S(1)}, bf16[2,3,16,704]{3,2,1,0:T(8,128)(2,1)S(1)}, u32[]{:S(2)}, u32[]{:S(2)}) collective-permute-start(bf16[2,3,16,704]{3,2,1,0:T(8,128)(2,1)S(1)} %get-tuple-element.180), channel_id=1, source_target_pairs={{0,4},{1,5},{2,6},{3,7},{4,0},{5,1},{6,2},{7,3},{8,12},{9,13},{10,... | collective-permute-start | bytes 405512 | tf_op jit(solution)/shard_map/ppermute | solution.py:38
  455.0 52.3 %collective-permute-start.116 = (bf16[2,3,16,704]{3,2,1,0:T(8,128)(2,1)S(1)}, bf16[2,3,16,704]{3,2,1,0:T(8,128)(2,1)S(1)}, u32[]{:S(2)}, u32[]{:S(2)}) collective-permute-start(bf16[2,3,16,704]{3,2,1,0:T(8,128)(2,1)S(1)} %get-tuple-element.179), channel_id=1, source_target_pairs={{0,2},{1,7},{2,4},{3,1},{4,6},{5,3},{6,0},{7,5},{8,10},{9,15},{10,... | collective-permute-start | bytes 405512 | tf_op jit(solution)/shard_map/ppermute | solution.py:38
  472.7 36.6 %collective-permute-start.117 = (bf16[2,3,16,704]{3,2,1,0:T(8,128)(2,1)S(1)}, bf16[2,3,16,704]{3,2,1,0:T(8,128)(2,1)S(1)}, u32[]{:S(2)}, u32[]{:S(2)}) collective-permute-start(bf16[2,3,16,704]{3,2,1,0:T(8,128)(2,1)S(1)} %slice_bitcast_fusion.29), channel_id=1, source_target_pairs={{0,6},{1,3},{2,0},{3,5},{4,2},{5,7},{6,4},{7,1},{8,14},{9,11},{10,... | collective-permute-start | bytes 405512 | tf_op jit(solution)/shard_map/ppermute | solution.py:38
  544.3 116.0 %collective-permute-start.121 = (bf16[2,2,4,3,16,704]{5,4,3,2,1,0:T(8,128)(2,1)S(1)}, bf16[2,2,4,3,16,704]{5,4,3,2,1,0:T(8,128)(2,1)S(1)}, u32[]{:S(2)}, u32[]{:S(2)}) collective-permute-start(bf16[2,2,4,3,16,704]{5,4,3,2,1,0:T(8,128)(2,1)S(1)} %pad_maximum_fusion.refs_0_), channel_id=1, source_target_pairs={{0,16},{1,49},{2,18},{3,51},{4,20},{5,53},{6,22},{7,55},{8,24},{9,... | collective-permute-start | bytes 3244040 | tf_op jit(solution)/shard_map/ppermute | solution.py:38
  563.0 77.4 %collective-permute-start.70 = (bf16[128,2048]{1,0:T(8,128)(2,1)S(1)}, bf16[128,2048]{1,0:T(8,128)(2,1)S(1)}, u32[]{:S(2)}, u32[]{:S(2)}) collective-permute-start(bf16[128,2048]{1,0:T(8,128)(2,1)S(1)} %get-tuple-element.131), channel_id=1, source_target_pairs={{0,1},{1,0},{2,3},{3,2},{4,5},{5,4},{6,7},{7,6},{8,9},{9,8},{10,11... | collective-permute-start | bytes 1572872 | tf_op jit(solution)/shard_map/ppermute | solution.py:38
  595.4 45.1 %collective-permute-start.74 = (bf16[128,2048]{1,0:T(8,128)(2,1)S(1)}, bf16[128,2048]{1,0:T(8,128)(2,1)S(1)}, u32[]{:S(2)}, u32[]{:S(2)}) collective-permute-start(bf16[128,2048]{1,0:T(8,128)(2,1)S(1)} %get-tuple-element.129), channel_id=1, source_target_pairs={{0,1},{1,0},{2,3},{3,2},{4,5},{5,4},{6,7},{7,6},{8,9},{9,8},{10,11... | collective-permute-start | bytes 1572872 | tf_op jit(solution)/shard_map/ppermute | solution.py:38
  596.0 47.7 %collective-permute-start.72 = (bf16[128,2048]{1,0:T(8,128)(2,1)S(1)}, bf16[128,2048]{1,0:T(8,128)(2,1)S(1)}, u32[]{:S(2)}, u32[]{:S(2)}) collective-permute-start(bf16[128,2048]{1,0:T(8,128)(2,1)S(1)} %get-tuple-element.130), channel_id=1, source_target_pairs={{0,1},{1,0},{2,3},{3,2},{4,5},{5,4},{6,7},{7,6},{8,9},{9,8},{10,11... | collective-permute-start | bytes 1572872 | tf_op jit(solution)/shard_map/ppermute | solution.py:38
  651.9 25.0 %collective-permute-start.73 = (bf16[128,2048]{1,0:T(8,128)(2,1)S(1)}, bf16[128,2048]{1,0:T(8,128)(2,1)S(1)}, u32[]{:S(2)}, u32[]{:S(2)}) collective-permute-start(bf16[128,2048]{1,0:T(8,128)(2,1)S(1)} %get-tuple-element.134), channel_id=1, source_target_pairs={{0,6},{1,3},{2,0},{3,5},{4,2},{5,7},{6,4},{7,1},{8,14},{9,11},{10,... | collective-permute-start | bytes 1572872 | tf_op jit(solution)/shard_map/ppermute | solution.py:38
  659.9 27.5 %collective-permute-start.122 = (bf16[2,2,4,3,16,704]{5,4,3,2,1,0:T(8,128)(2,1)S(1)}, bf16[2,2,4,3,16,704]{5,4,3,2,1,0:T(8,128)(2,1)S(1)}, u32[]{:S(2)}, u32[]{:S(2)}) collective-permute-start(bf16[2,2,4,3,16,704]{5,4,3,2,1,0:T(8,128)(2,1)S(1)} %pad_maximum_fusion.refs_0_), channel_id=1, source_target_pairs={{0,48},{1,17},{2,50},{3,19},{4,52},{5,21},{6,54},{7,23},{8,56},{9,... | collective-permute-start | bytes 3244040 | tf_op jit(solution)/shard_map/ppermute | solution.py:38
  660.3 28.2 %collective-permute-start.123 = (bf16[2,2,4,3,16,704]{5,4,3,2,1,0:T(8,128)(2,1)S(1)}, bf16[2,2,4,3,16,704]{5,4,3,2,1,0:T(8,128)(2,1)S(1)}, u32[]{:S(2)}, u32[]{:S(2)}) collective-permute-start(bf16[2,2,4,3,16,704]{5,4,3,2,1,0:T(8,128)(2,1)S(1)} %collective-permute-done.121.refs_1_), channel_id=1, source_target_pairs={{0,16},{1,49},{2,18},{3,51},{4,20},{5,53},{6,22},{7,55},{8,24},{9,... | collective-permute-start | bytes 3244040 | tf_op jit(solution)/shard_map/ppermute | solution.py:38
  (166 other events, 2129.9 us)
Sparse Core Ops, SparseCore 0:
  62.2 33.0 all-gather.1
